TPU v7x, 32 devices: a whole 2x2x4 slice. The times are simulated.
32 devices in a mesh: groups: 1, samp: 4 (over x, core), var: 8 (over z, y).
Axes of the slice: x: 2, y: 2, z: 4, core: 2. Of those that a mesh axis runs over, the one named last changes fastest.
Arguments:
- expression: bfloat16 [4096, 5120], P(('groups', 'samp'), 'var'), may hold values from -6 to 6
- genotypes: bfloat16 [4096, 1536], P(('groups', 'samp'), 'var'), may hold values from 0 to 2
- covariates: bfloat16 [4096, 64], P(('groups', 'samp')), may hold values from -6 to 6
- distance_bins: int32 [24, 5120], P('groups', ('var', 'samp')), may hold values from 0 to 15
- gene_folds: int32 [5120], P(('groups', 'var', 'samp')), may hold values from 0 to 4
- fold_weights: float32 [5, 16], replicated, may hold values from 0.25 to 4
Outputs:
- weighted_stats: float32 [5120, 1536], P(('groups', 'var', 'samp'))
Inputs may be any that keep to these rules, and one draw needn't show every extreme that they name: `distance_bins`: bins index rows of fold_weights' second dimension. `gene_folds`: folds index rows of fold_weights.
All inputs are finite; a program needn't handle non-finite values.
Results may differ from a plain program's by a relative error of at most 0.0047.
Values may be sent and summed in bfloat16 or wider, within the bound.
No kernel may reach another device: no remote copies, remote signals or barrier semaphores. Data moves between devices by JAX's collectives and lax.ppermute only.
A program may use at most 64 MiB of HBM per device.

v0:
```python
import functools
import math

import jax
import jax.numpy as jnp
from jax import lax
from jax.experimental import pallas as pl
from jax.experimental.pallas import tpu as pltpu
from jax.sharding import PartitionSpec as P

LANES = 128
EPS = 1e-06
COST = {'products': 10**8, 'add': 1, 'solve': 10**8, 'stat': 1, 'place': 1, 'finish': 1, 'gate': 10**11}
VMEM_LIMIT = 10 * 1024 * 1024

NT = (((1,), (1,)), ((), ()))
NN = (((1,), (0,)), ((), ()))
HIGHEST = lax.Precision.HIGHEST


def ring_order(mesh):
    members = list(mesh.devices[0, 0])
    places = [getattr(device, "coords", None) for device in members]
    if len(members) < 2 or any(place is None for place in places):
        return list(range(len(members)))
    axis = [i for i in range(len(places[0])) if places[0][i] != places[1][i]][0]
    columns = {}
    for index, place in enumerate(places):
        columns.setdefault(place[axis], []).append(index)
    order = []
    for step, key in enumerate(sorted(columns)):
        order += columns[key] if step % 2 == 0 else columns[key][::-1]
    return order


def call(kernel, out_shape, name, flops, operands, scratch=(), scalars=1, tokens=0):
    vmem = pl.BlockSpec(memory_space=pltpu.VMEM)
    smem = pl.BlockSpec(memory_space=pltpu.SMEM)
    rest = len(operands) - scalars - tokens
    return pl.pallas_call(
        kernel,
        out_shape=out_shape,
        in_specs=[smem] * scalars + [vmem] * rest + [pl.BlockSpec(memory_space=pl.ANY)] * tokens,
        out_specs=jax.tree.map(lambda _: vmem, out_shape),
        scratch_shapes=list(scratch),
        compiler_params=pltpu.CompilerParams(vmem_limit_bytes=VMEM_LIMIT),
        cost_estimate=pl.CostEstimate(flops=flops, bytes_accessed=0, transcendentals=0),
        name=name,
    )(*operands)


def gate_kernel(*refs):
    pass


def gate(blocks, tokens):
    vmem = pl.BlockSpec(memory_space=pltpu.VMEM)
    return pl.pallas_call(
        gate_kernel,
        out_shape=[jax.ShapeDtypeStruct(b.shape, b.dtype) for b in blocks],
        in_specs=[vmem] * len(blocks) + [pl.BlockSpec(memory_space=pl.ANY)] * len(tokens),
        out_specs=[vmem] * len(blocks),
        input_output_aliases={i: i for i in range(len(blocks))},
        compiler_params=pltpu.CompilerParams(vmem_limit_bytes=VMEM_LIMIT),
        cost_estimate=pl.CostEstimate(flops=COST["gate"], bytes_accessed=0, transcendentals=0),
        name="gate",
    )(*blocks, *tokens)


def first_kernel(parts, covs, ids_ref, e_ref, gt_ref, dt_ref, left_ref, send_ref, other_ref, mine_ref, wide):
    width = e_ref.shape[1]
    genes = width // parts
    sid = ids_ref[0]
    wide[...] = e_ref[...].T
    owners = [sid ^ 1 ^ d for d in range(2, parts, 2)] + [sid ^ 1]
    owners += [sid ^ d for d in range(2, parts, 2)] + [sid]
    for i, owner in enumerate(owners):
        start = pl.multiple_of(owner * genes, 16)
        left_ref[i * genes : (i + 1) * genes] = wide[pl.ds(start, genes), :]
    rows = dt_ref.shape[1]
    left_ref[width : width + covs] = dt_ref[...]
    first = lax.broadcasted_iota(jnp.int32, (16, rows), 0) == 0
    left_ref[width + covs :] = first.astype(jnp.float32).astype(jnp.bfloat16)
    design = left_ref[width:]
    right = jnp.concatenate([design, jnp.zeros((LANES - design.shape[0], rows), jnp.bfloat16)], axis=0)
    right = jnp.concatenate([right, gt_ref[...]], axis=0)
    split(parts, covs, genes, left_ref, right, send_ref, other_ref, mine_ref, True)


def next_kernel(parts, covs, blocks, left_ref, *rest):
    right = jnp.concatenate([ref[...] for ref in rest[:blocks]], axis=0)
    send_ref, other_ref, mine_ref = rest[-3:]
    genes = mine_ref.shape[0]
    split(parts, covs, genes, left_ref, right, send_ref, other_ref, mine_ref, False)


def split(parts, covs, genes, left_ref, right, send_ref, other_ref, mine_ref, squares):
    width = genes * parts
    span = genes * (parts // 2 - 1)
    deep = covs + 8

    prod = lax.dot_general(left_ref[...], right, NT, preferred_element_type=jnp.float32)
    outs = prod[:width]
    if squares:
        a = left_ref[:width].astype(jnp.float32)
        lane = lax.broadcasted_iota(jnp.int32, outs.shape, 1)
        outs = jnp.where(lane == covs + 1, jnp.sum(a * a, axis=1, keepdims=True), outs)
    send_ref[:span] = outs[:span]
    send_ref[span + deep :] = outs[span : span + genes]
    other_ref[:span] = outs[span + genes : 2 * span + genes]
    mine_ref[...] = outs[2 * span + genes :]
    square = right.astype(jnp.float32)
    square = square * square
    high = square.astype(jnp.bfloat16)
    low = (square - high.astype(jnp.float32)).astype(jnp.bfloat16)
    ones = jnp.ones((16, right.shape[1]), jnp.bfloat16)
    total = lax.dot_general(ones, high, NT, preferred_element_type=jnp.float32)
    total += lax.dot_general(ones, low, NT, preferred_element_type=jnp.float32)
    fits = prod[width : width + deep]
    row = lax.broadcasted_iota(jnp.int32, fits.shape, 0)
    fits = jnp.where(row == covs + 1, total[:1], fits)
    send_ref[span : span + deep] = fits
    other_ref[span:] = fits


def product_shapes(parts, covs, genes, columns):
    span = genes * (parts // 2 - 1)
    rows = (span + covs + 8 + genes, span + covs + 8, genes)
    return [jax.ShapeDtypeStruct((r, columns), jnp.float32) for r in rows]


def first_products(ids, e, gt, dt, parts):
    rows, width = e.shape
    covs = dt.shape[0]
    columns = LANES + gt.shape[0]
    left = jax.ShapeDtypeStruct((width + covs + 16, rows), jnp.bfloat16)
    return call(
        functools.partial(first_kernel, parts, covs),
        [left] + product_shapes(parts, covs, width // parts, columns),
        "first_products",
        COST["products"],
        (ids, e, gt, dt),
        scratch=[pltpu.VMEM((width, rows), jnp.bfloat16)],
    )


def next_products(left, blocks, parts, covs, tokens):
    rows = left.shape[1]
    width = left.shape[0] - covs - 16
    columns = sum(b.shape[0] for b in blocks)
    return call(
        functools.partial(next_kernel, parts, covs, len(blocks)),
        product_shapes(parts, covs, width // parts, columns),
        "next_products",
        COST["products"],
        (left, *blocks, *tokens),
        scalars=0,
        tokens=len(tokens),
    )


def packed_rows(tall, columns):
    return tall * (columns // LANES) + -(-tall // 16) * 8 if columns % LANES == LANES // 2 and columns > LANES else 0


def pack(block):
    tall, columns = block.shape
    fold = -(-tall // 16) * 8
    whole = columns // LANES
    rest = block[:, whole * LANES :]
    rest = jnp.concatenate([rest, jnp.zeros((2 * fold - tall, LANES // 2), rest.dtype)], axis=0)
    tiles = [block[:, i * LANES : (i + 1) * LANES] for i in range(whole)]
    return jnp.concatenate([*tiles, jnp.concatenate([rest[:fold], rest[fold:]], axis=1)], axis=0)


def unpack(block, tall):
    fold = -(-tall // 16) * 8
    whole = block.shape[0] // tall
    rest = block[whole * tall :]
    rest = jnp.concatenate([rest[:, : LANES // 2], rest[: tall - fold, LANES // 2 :]], axis=0)
    tiles = [block[i * tall : (i + 1) * tall] for i in range(whole)]
    return jnp.concatenate([*tiles, rest], axis=1)


def add_kernel(genes, deep, tokens, other_ref, came_ref, *rest):
    out_refs = rest[tokens:]
    cuts = len(out_refs) * genes // (other_ref.shape[0] - deep)
    span = other_ref.shape[0] - deep
    for i in range(span // genes):
        start = i * genes
        total = other_ref[start : start + genes] + came_ref[start : start + genes]
        fits = other_ref[span:] + came_ref[span : span + deep]
        total = jnp.concatenate([total, fits], axis=0)
        if out_refs[i * cuts].shape[0] > genes + deep:
            total = pack(total)
        row = 0
        for out_ref in out_refs[i * cuts : (i + 1) * cuts]:
            out_ref[...] = total[row : row + out_ref.shape[0]]
            row += out_ref.shape[0]


def add_cores(other, came, genes, deep, cuts, tokens):
    chips = (other.shape[0] - deep) // genes
    tall = genes + deep
    dense = packed_rows(tall, other.shape[1])
    if dense:
        heights, columns, cuts = [dense], LANES, 1
    else:
        heights, columns = [tall] if cuts == 1 else [tall // 16 * 8, tall - tall // 16 * 8], other.shape[1]
    shapes = [jax.ShapeDtypeStruct((h, columns), jnp.float32) for h in heights]
    out = call(
        functools.partial(add_kernel, genes, deep, len(tokens)),
        shapes * chips,
        "add_cores",
        COST["add"],
        (other, came, *tokens),
        scalars=0,
        tokens=len(tokens),
    )
    return [out[i * cuts : (i + 1) * cuts] for i in range(chips)]


def chunk_sums(genes, deep, mine_ref, came_ref, refs):
    tall = genes + deep
    blocks, rows = [], []
    for ref in refs:
        rows.append(unpack(ref[...], tall) if ref.shape[0] > tall else ref[...])
        if sum(r.shape[0] for r in rows) == tall:
            blocks.append(jnp.concatenate(rows, axis=0) if len(rows) > 1 else rows[0])
            rows = []
    corr = mine_ref[...] + came_ref[came_ref.shape[0] - genes :]
    fits = blocks[0][genes:]
    for block in blocks[1:]:
        corr = corr + block[:genes]
        fits = fits + block[genes:]
    return corr, fits


def solve_kernel(covs, dof, weight_ref, mine_ref, came_ref, *rest):
    refs, (bins_ref, folds_ref, solved_ref, scale_ref) = rest[:-4], rest[-4:]
    genes = mine_ref.shape[0]
    rank, deep = covs + 1, covs + 8
    corr, fits = chunk_sums(genes, deep, mine_ref, came_ref, refs)
    cross, gram = corr[:, :LANES], fits[:, :LANES]
    row = lax.broadcasted_iota(jnp.int32, gram.shape, 0)
    lane = lax.broadcasted_iota(jnp.int32, gram.shape, 1)
    inside = jnp.logical_and(row < rank, lane < rank)
    a = jnp.where(inside, gram, jnp.where(row == lane, 1.0, 0.0))
    for k in range(0, rank, 2):
        down0 = jnp.broadcast_to(a[:, k : k + 1], a.shape)
        down1 = jnp.broadcast_to(a[:, k + 1 : k + 2], a.shape)
        p00, p01, p11 = down0[k : k + 1], down1[k : k + 1], down1[k + 1 : k + 2]
        inv = 1.0 / (p00 * p11 - p01 * p01)
        q00, q01, q11 = p11 * inv, -p01 * inv, p00 * inv
        row0, row1 = a[k : k + 1], a[k + 1 : k + 2]
        first = q00 * row0 + q01 * row1
        second = q01 * row0 + q11 * row1
        swept = a - down0 * first - down1 * second
        swept = jnp.where(lane == k, down0 * q00 + down1 * q01, swept)
        swept = jnp.where(lane == k + 1, down0 * q01 + down1 * q11, swept)
        first = jnp.where(lane[:1] == k, -q00, jnp.where(lane[:1] == k + 1, -q01, first))
        second = jnp.where(lane[:1] == k, -q01, jnp.where(lane[:1] == k + 1, -q11, second))
        a = jnp.where(row == k, first, jnp.where(row == k + 1, second, swept))
    inverse = jnp.where(inside, -a, 0.0)
    lane = lax.broadcasted_iota(jnp.int32, cross.shape, 1)
    squares = jnp.sum(jnp.where(lane == rank, cross, 0.0), axis=1, keepdims=True)
    cross = jnp.where(lane < rank, cross, 0.0)
    beta = lax.dot_general(cross, inverse, NT, precision=HIGHEST, preferred_element_type=jnp.float32)
    norm = squares - jnp.sum(beta * cross[:, :deep], axis=1, keepdims=True)
    norm = jnp.maximum(norm, 1e-06 * squares) + EPS
    solved_ref[:genes] = beta
    solved_ref[genes:] = inverse[:, :deep]

    bins, folds = bins_ref[...], folds_ref[...]
    tile = jnp.zeros(bins.shape, jnp.float32)
    for b in range(weight_ref.shape[1]):
        of_bin = jnp.zeros(folds.shape, jnp.float32)
        for f in range(weight_ref.shape[0]):
            of_bin = jnp.where(folds == f, weight_ref[f, b], of_bin)
        tile = jnp.where(bins == b, of_bin, tile)
    tile = tile.T * (dof / norm)
    width = scale_ref.shape[1] // tile.shape[1]
    for t in range(0, tile.shape[1], 2):
        pair = [jnp.broadcast_to(tile[:, i : i + 1], (genes, width)) for i in (t, t + 1)]
        scale_ref[:, t * width : (t + 2) * width] = jnp.concatenate(pair, axis=1)


def solve(weights, mine, came, swapped, bins, folds, covs, dof, variants):
    genes = mine.shape[0]
    outs = [
        jax.ShapeDtypeStruct((genes + covs + 8, covs + 8), jnp.float32),
        jax.ShapeDtypeStruct((genes, variants), jnp.float32),
    ]
    return call(
        functools.partial(solve_kernel, covs, dof),
        outs,
        "solve",
        COST["solve"],
        (weights, mine, came, *swapped, bins, folds),
    )


def fitted_stat(covs, skip, solved_ref, mine_ref, came_ref, refs):
    genes = mine_ref.shape[0]
    corr, fits = chunk_sums(genes, covs + 8, mine_ref, came_ref, refs)
    corr, fits = corr[:, skip:], fits[:, skip:]
    row = lax.broadcasted_iota(jnp.int32, fits.shape, 0)
    squares = fits[covs + 1 : covs + 2]
    fits = jnp.where(row <= covs, fits, 0.0)
    both = lax.dot_general(solved_ref[...], fits, NN, precision=HIGHEST, preferred_element_type=jnp.float32)
    norm = squares - jnp.sum(both[genes:] * fits, axis=0, keepdims=True)
    norm = jnp.maximum(norm, 1e-06 * squares) + EPS
    corr = corr - both[:genes]
    return corr * corr * (1.0 / norm)


def stat_kernel(covs, skip, solved_ref, mine_ref, came_ref, *rest):
    rest[-1][...] = fitted_stat(covs, skip, solved_ref, mine_ref, came_ref, rest[:-1])


def chunk_stat(solved, mine, came, swapped, covs, skip):
    return call(
        functools.partial(stat_kernel, covs, skip),
        jax.ShapeDtypeStruct((mine.shape[0], mine.shape[1] - skip), jnp.float32),
        "chunk_stat",
        COST["stat"],
        (solved, mine, came, *swapped),
        scalars=0,
    )


def slot_of(index, here, ring, order):
    position = {block: i for i, block in enumerate(order)}
    mine = jnp.int32(0)
    for block in range(ring):
        mine = jnp.where(here == block, position[block], mine)
    return lax.rem(position[index] - mine + ring, ring)


def place_kernel(ring, order, ids_ref, scale_ref, *rest):
    stats, (out_ref, held) = rest[:-2], rest[-2:]
    variants = held.shape[2]
    held[ring // 2] = jnp.zeros_like(held[0])
    for k, stat in enumerate(stats):
        if k == 0:
            held[0] = stat[...]
        else:
            held[ring - k] = stat[:, :variants]
            held[k] = stat[:, variants:]
    group = LANES // math.gcd(variants, LANES)
    for j in range(0, ring, group):
        pieces = [held[slot_of(j + b, ids_ref[1], ring, order)] for b in range(group)]
        span = slice(j * variants, (j + group) * variants)
        out_ref[:, span] = jnp.concatenate(pieces, axis=1) * scale_ref[:, span]


def place(ids, scale, stats, ring, order):
    genes, total = scale.shape
    return call(
        functools.partial(place_kernel, ring, order),
        jax.ShapeDtypeStruct(scale.shape, jnp.float32),
        "place",
        COST["place"],
        (ids, scale, *stats),
        scratch=[pltpu.VMEM((ring, genes, total // ring), jnp.float32)],
    )


def finish_kernel(covs, ring, order, ids_ref, solved_ref, scale_ref, placed_ref, mine_ref, came_ref, *rest):
    out_ref = rest[-1]
    variants = mine_ref.shape[1]
    group = LANES // math.gcd(variants, LANES)
    width = group * variants
    stat = fitted_stat(covs, 0, solved_ref, mine_ref, came_ref, rest[:-1])
    out_ref[...] = placed_ref[...]
    index = jnp.int32(0)
    for block in range(ring):
        index = jnp.where(slot_of(block, ids_ref[1], ring, order) == ring // 2, block, index)
    span = pl.ds(pl.multiple_of(index // group * width, LANES), width)
    stat = jnp.concatenate([stat] * group, axis=1)
    lane = lax.broadcasted_iota(jnp.int32, stat.shape, 1)
    first = lax.rem(index, group) * variants
    inside = jnp.logical_and(lane >= first, lane < first + variants)
    out_ref[:, span] = jnp.where(inside, stat * scale_ref[:, span], placed_ref[:, span])


def finish(ids, solved, scale, placed, last, covs, ring, order):
    return call(
        functools.partial(finish_kernel, covs, ring, order),
        jax.ShapeDtypeStruct(scale.shape, jnp.float32),
        "finish",
        COST["finish"],
        (ids, solved, scale, placed, *last),
    )


def shards(order, expression, genotypes, covariates, distance_bins, gene_folds, fold_weights):
    parts, ring = lax.axis_size("samp"), lax.axis_size("var")
    rows, width = expression.shape
    covs = covariates.shape[1]
    genes = width // parts
    deep = covs + 8
    dof = float(rows * parts - covs - 2)
    gt = genotypes.T
    variants = gt.shape[0]
    middle = ring // 2
    ids = jnp.stack([lax.axis_index("samp"), lax.axis_index("var")]).astype(jnp.int32)

    def exchange(x, d):
        return lax.ppermute(x, "samp", [(s, s ^ d) for s in range(parts)])

    forward = [(order[i], order[(i + 1) % ring]) for i in range(ring)]
    backward = [(b, a) for a, b in forward]

    def right(x):
        return lax.ppermute(x, "var", forward)

    def left(x):
        return lax.ppermute(x, "var", backward)

    stats = []
    lhs = solved = scale = None

    done = {}

    def starts(k):
        return [("came", 0) if k == 1 else ("got", 0) if k == 2 else ("sent", k - 1)]

    def turns(k):
        return ([("got", k - 2)] if 1 < k < middle else []) + ([("solved", 0)] if k == middle - 1 else [])

    def ends(k):
        return [("got", k - 2)] if k == middle else []

    def after(*names):
        return [done[name] for name in names if name in done]

    block = (gt, gt)
    for k in range(middle + 1):
        if k > 0:
            block = gate(block, after(*turns(k)))
        if k < middle - 1:
            ahead = (right(block[0]), left(block[-1]))
        elif k == middle - 1:
            ahead = (right(block[0][: variants // 2]), left(block[-1][variants // 2 :]))
        if k == 0:
            lhs, send, other, mine = first_products(ids, expression, gt, covariates.T, parts)
        else:
            tokens = after(*starts(k))
            send, other, mine = next_products(lhs, block, parts, covs, tokens)
        came = exchange(send, 1)
        sent = add_cores(other, came, genes, deep, 1, after(*ends(k)))
        got = [[exchange(x, 2 * (i + 1)) for x in cut] for i, cut in enumerate(sent)]
        swapped = [*sent[0], *sum(got, [])]
        done["came", k], done["sent", k] = came, sent[0][0]
        done["got", k], done["rest", k] = got[-1][0], got[-1][-1]
        if k == 0:
            solved, scale = solve(
                fold_weights, mine, came, swapped, distance_bins, gene_folds[None], covs, dof, ring * variants
            )
            done["solved", 0] = solved
        if k < middle:
            stats.append(chunk_stat(solved, mine, came, swapped, covs, LANES if k == 0 else 0))
            done["stat", k] = stats[k]
            block = ahead
    placed = place(ids, scale, stats, ring, tuple(order))
    return finish(ids, solved, scale, placed, (mine, came, *swapped), covs, ring, tuple(order))


def solution(mesh):
    return jax.shard_map(
        functools.partial(shards, ring_order(mesh)),
        mesh=mesh,
        in_specs=(
            P(("groups", "samp"), "var"),
            P(("groups", "samp"), "var"),
            P(("groups", "samp"), None),
            P("groups", ("var", "samp")),
            P(("groups", "var", "samp")),
            P(),
        ),
        out_specs=P(("groups", "var", "samp"), None),
        check_vma=False,
    )
```

profile of v0, /device:TPU:0, one launch (start us, length us, event | category | flops | bytes accessed | tf_op | source)
XLA Modules:
  0.0 61.3 jit_solution(4318892064228508406)
XLA Ops:
  0.0 3.0 %collective-permute-start.2 = (bf16[192,1024]{1,0:T(8,128)(2,1)}, bf16[192,1024]{1,0:T(8,128)(2,1)S(1)}, u32[]{:S(2)}, u32[]{:S(2)}) collective-permute-start(bf16[192,1024]{1,0:T(8,128)(2,1)} %bitcast.5), channel_id=1, source_target_pairs={{0,2},{2,4},{4,6},{6,7},{7,5},{5,3},{3,1},{1,0},{8,10},{10,12},{12... | collective-permute-start | bytes 1179656 | tf_op jit(solution)/shard_map/ppermute | solution.py:416
  3.0 0.0 collective-permute-start.3
  3.0 0.1 pad_add_fusion.ids_ref
  3.1 1.3 %copy-done.4 = bf16[1024,640]{1,0:T(8,128)(2,1)S(1)} copy-done((bf16[1024,640]{1,0:T(8,128)(2,1)S(1)}, bf16[1024,640]{1,0:T(8,128)(2,1)}, u32[]{:S(2)}) %copy-start.4) | copy-done | bytes 1310744
  4.4 1.0 %copy-done.7 = bf16[1024,192]{0,1:T(8,128)(2,1)S(1)} copy-done((bf16[1024,192]{0,1:T(8,128)(2,1)S(1)}, bf16[1024,192]{0,1:T(8,128)(2,1)}, u32[]{:S(2)}) %copy-start.7) | copy-done | bytes 393240
  5.4 0.9 %copy-done.8 = bf16[1024,64]{0,1:T(8,128)(2,1)S(1)} copy-done((bf16[1024,64]{0,1:T(8,128)(2,1)S(1)}, bf16[1024,64]{0,1:T(8,128)(2,1)}, u32[]{:S(2)}) %copy-start.8) | copy-done | bytes 131096
  6.3 2.4 %first_products.1 = (bf16[720,1024]{1,0:T(8,128)(2,1)S(1)}, f32[392,320]{1,0:T(8,128)S(1)}, f32[232,320]{1,0:T(8,128)S(1)}, f32[160,320]{1,0:T(8,128)S(1)}) custom-call(s32[2]{0:T(128)S(1)} %pad_add_fusion.ids_ref, bf16[1024,640]{1,0:T(8,128)(2,1)S(1)} %copy-done.4, bf16[192,1024]{1,0:T(8,128)(2,1)S(1)} %bitcast.7, bf16[64,1024]{1,0:T(8,128)(2,1)S(1)} %bitcast.8), custom_call_target="tpu_custom_call" | custom-call | flops 100000000 | tf_op jit(solution)/shard_map/first_products/pallas_call | solution.py:40
  8.7 0.0 collective-permute-start
  8.7 3.6 %collective-permute-done.2.refs_0_ = bf16[192,1024]{1,0:T(8,128)(2,1)S(1)} collective-permute-done((bf16[192,1024]{1,0:T(8,128)(2,1)}, bf16[192,1024]{1,0:T(8,128)(2,1)S(1)}, u32[]{:S(2)}, u32[]{:S(2)}) %collective-permute-start.2) | collective-permute-done | bytes 393248 | tf_op jit(solution)/shard_map/ppermute | solution.py:416
  12.3 1.5 %collective-permute-done.3.refs_1_ = bf16[192,1024]{1,0:T(8,128)(2,1)S(1)} collective-permute-done((bf16[192,1024]{1,0:T(8,128)(2,1)}, bf16[192,1024]{1,0:T(8,128)(2,1)S(1)}, u32[]{:S(2)}, u32[]{:S(2)}) %collective-permute-start.3) | collective-permute-done | bytes 393248 | tf_op jit(solution)/shard_map/ppermute | solution.py:419
  13.8 1.6 %collective-permute-start.6 = (bf16[192,1024]{1,0:T(8,128)(2,1)S(1)}, bf16[192,1024]{1,0:T(8,128)(2,1)S(1)}, u32[]{:S(2)}, u32[]{:S(2)}) collective-permute-start(bf16[192,1024]{1,0:T(8,128)(2,1)S(1)} %get-tuple-element.37.rest_0_), channel_id=1, source_target_pairs={{0,2},{2,4},{4,6},{6,7},{7,5},{5,3},{3,1},{1,0},{8,10},{10,12},{12... | collective-permute-start | bytes 1179656 | tf_op jit(solution)/shard_map/ppermute | solution.py:416
  15.4 0.4 collective-permute-start.7
  15.8 0.0 collective-permute-done.came_ref.rest_2_
  15.8 0.1 add_cores.5.rest_0_
  15.9 1.6 %collective-permute-start.1 = (f32[584,128]{1,0:T(8,128)S(1)}, f32[584,128]{1,0:T(8,128)S(1)}, u32[]{:S(2)}, u32[]{:S(2)}) collective-permute-start(f32[584,128]{1,0:T(8,128)S(1)} %add_cores.5.rest_0_), channel_id=1, source_target_pairs={{0,16},{8,24},{16,0},{24,8},{1,17},{9,25},{17,1},{25,9},{2,18},{10... | collective-permute-start | bytes 897032 | tf_op jit(solution)/shard_map/ppermute | solution.py:410
  17.5 1.3 %next_products.4 = (f32[392,384]{1,0:T(8,128)S(1)}, f32[232,384]{1,0:T(8,128)S(1)}, f32[160,384]{1,0:T(8,128)S(1)}) custom-call(bf16[720,1024]{1,0:T(8,128)(2,1)S(1)} %get-tuple-element.36.left_ref, bf16[192,1024]{1,0:T(8,128)(2,1)S(1)} %get-tuple-element.37.rest_0_, bf16[192,1024]{1,0:T(8,128)(2,1)S(1)} %get-tuple-element.38.rest_1_, ...), custom_call_target="tpu_custom_call" | custom-call | flops 100000000 | tf_op jit(solution)/shard_map/next_products/pallas_call | solution.py:40
  18.8 0.0 collective-permute-start.4
  18.8 4.7 %collective-permute-done.6.refs_0_ = bf16[192,1024]{1,0:T(8,128)(2,1)S(1)} collective-permute-done((bf16[192,1024]{1,0:T(8,128)(2,1)S(1)}, bf16[192,1024]{1,0:T(8,128)(2,1)S(1)}, u32[]{:S(2)}, u32[]{:S(2)}) %collective-permute-start.6) | collective-permute-done | bytes 393248 | tf_op jit(solution)/shard_map/ppermute | solution.py:416
  23.5 1.3 %collective-permute-done.7.refs_1_ = bf16[192,1024]{1,0:T(8,128)(2,1)S(1)} collective-permute-done((bf16[192,1024]{1,0:T(8,128)(2,1)S(1)}, bf16[192,1024]{1,0:T(8,128)(2,1)S(1)}, u32[]{:S(2)}, u32[]{:S(2)}) %collective-permute-start.7) | collective-permute-done | bytes 393248 | tf_op jit(solution)/shard_map/ppermute | solution.py:419
  24.8 0.0 collective-permute-done.1.rest_1_.refs_2_.rest_2_
  24.8 1.6 %collective-permute-start.10 = (bf16[192,1024]{1,0:T(8,128)(2,1)S(1)}, bf16[192,1024]{1,0:T(8,128)(2,1)S(1)}, u32[]{:S(2)}, u32[]{:S(2)}) collective-permute-start(bf16[192,1024]{1,0:T(8,128)(2,1)S(1)} %get-tuple-element.42.rest_0_), channel_id=1, source_target_pairs={{0,2},{2,4},{4,6},{6,7},{7,5},{5,3},{3,1},{1,0},{8,10},{10,12},{12... | collective-permute-start | bytes 1179656 | tf_op jit(solution)/shard_map/ppermute | solution.py:416
  26.4 0.4 collective-permute-start.11
  26.8 0.0 collective-permute-done.4.came_ref
  26.8 0.1 add_cores.6.rest_0_
  26.9 0.0 copy-start.2
  26.9 0.0 copy-start.9
  26.9 0.0 copy-start.12
  26.9 0.0 copy-start.13
  26.9 1.6 %collective-permute-start.5 = (f32[232,384]{1,0:T(8,128)S(1)}, f32[232,384]{1,0:T(8,128)S(1)}, u32[]{:S(2)}, u32[]{:S(2)}) collective-permute-start(f32[232,384]{1,0:T(8,128)S(1)} %add_cores.6.rest_0_), channel_id=1, source_target_pairs={{0,16},{8,24},{16,0},{24,8},{1,17},{9,25},{17,1},{25,9},{2,18},{10... | collective-permute-start | bytes 1069064 | tf_op jit(solution)/shard_map/ppermute | solution.py:410
  28.5 1.3 %next_products.5 = (f32[392,384]{1,0:T(8,128)S(1)}, f32[232,384]{1,0:T(8,128)S(1)}, f32[160,384]{1,0:T(8,128)S(1)}) custom-call(bf16[720,1024]{1,0:T(8,128)(2,1)S(1)} %get-tuple-element.36.left_ref, bf16[192,1024]{1,0:T(8,128)(2,1)S(1)} %get-tuple-element.42.rest_0_, bf16[192,1024]{1,0:T(8,128)(2,1)S(1)} %get-tuple-element.43.rest_1_, ...), custom_call_target="tpu_custom_call" | custom-call | flops 100000000 | tf_op jit(solution)/shard_map/next_products/pallas_call | solution.py:40
  29.8 0.0 collective-permute-start.8
  29.8 0.0 copy-done.5
  29.8 0.0 copy-done.9
  29.8 0.0 copy-done.12
  29.8 0.0 copy-done.13
  29.8 5.1 %solve.1 = (f32[232,72]{1,0:T(8,128)S(1)}, f32[160,1536]{1,0:T(8,128)S(1)}) custom-call(f32[5,16]{1,0:T(8,128)S(1)} %copy-done.12, f32[160,320]{1,0:T(8,128)S(1)} %get-tuple-element.31.mine_ref, f32[392,320]{1,0:T(8,128)S(1)} %collective-permute-done.came_ref.rest_2_, f32[584,128]{1,0:T(8,128)S(1)} %add_cores.5.rest_0_, ...), custom_call_target="tpu_custom_call" | custom-call | flops 100000000 | tf_op jit(solution)/shard_map/solve/pallas_call | solution.py:40
  34.9 0.0 collective-permute-done.10.refs_0_
  34.9 0.0 collective-permute-done.11.refs_1_
  35.0 0.0 collective-permute-done.5.rest_1_.refs_2_
  35.0 1.6 %collective-permute-start.14 = (bf16[96,1024]{1,0:T(8,128)(2,1)S(1)}, bf16[96,1024]{1,0:T(8,128)(2,1)S(1)}, u32[]{:S(2)}, u32[]{:S(2)}) collective-permute-start(bf16[96,1024]{1,0:T(8,128)(2,1)S(1)} %slice.6), channel_id=1, source_target_pairs={{0,2},{2,4},{4,6},{6,7},{7,5},{5,3},{3,1},{1,0},{8,10},{10,12},{12... | collective-permute-start | bytes 589832 | tf_op jit(solution)/shard_map/ppermute | solution.py:416
  36.6 0.5 collective-permute-start.15
  37.1 0.0 collective-permute-done.8.came_ref
  37.2 1.1 %collective-permute-start.9 = (f32[232,384]{1,0:T(8,128)S(1)}, f32[232,384]{1,0:T(8,128)S(1)}, u32[]{:S(2)}, u32[]{:S(2)}) collective-permute-start(f32[232,384]{1,0:T(8,128)S(1)} %add_cores.7.rest_0_.rest_2_), channel_id=1, source_target_pairs={{0,16},{8,24},{16,0},{24,8},{1,17},{9,25},{17,1},{25,9},{2,18},{10... | collective-permute-start | bytes 1069064 | tf_op jit(solution)/shard_map/ppermute | solution.py:410
  38.3 1.3 %next_products.6 = (f32[392,384]{1,0:T(8,128)S(1)}, f32[232,384]{1,0:T(8,128)S(1)}, f32[160,384]{1,0:T(8,128)S(1)}) custom-call(bf16[720,1024]{1,0:T(8,128)(2,1)S(1)} %get-tuple-element.36.left_ref, bf16[192,1024]{1,0:T(8,128)(2,1)S(1)} %get-tuple-element.47.rest_0_, bf16[192,1024]{1,0:T(8,128)(2,1)S(1)} %get-tuple-element.48.rest_1_, ...), custom_call_target="tpu_custom_call" | custom-call | flops 100000000 | tf_op jit(solution)/shard_map/next_products/pallas_call | solution.py:40
  39.6 0.0 collective-permute-start.12
  39.6 2.7 %collective-permute-done.14.refs_0_ = bf16[96,1024]{1,0:T(8,128)(2,1)S(1)} collective-permute-done((bf16[96,1024]{1,0:T(8,128)(2,1)S(1)}, bf16[96,1024]{1,0:T(8,128)(2,1)S(1)}, u32[]{:S(2)}, u32[]{:S(2)}) %collective-permute-start.14) | collective-permute-done | bytes 196640 | tf_op jit(solution)/shard_map/ppermute | solution.py:416
  42.3 1.4 %collective-permute-done.15.refs_1_ = bf16[96,1024]{1,0:T(8,128)(2,1)S(1)} collective-permute-done((bf16[96,1024]{1,0:T(8,128)(2,1)S(1)}, bf16[96,1024]{1,0:T(8,128)(2,1)S(1)}, u32[]{:S(2)}, u32[]{:S(2)}) %collective-permute-start.15) | collective-permute-done | bytes 196640 | tf_op jit(solution)/shard_map/ppermute | solution.py:419
  43.7 0.0 collective-permute-done.12.came_ref
  43.8 0.8 %next_products.7 = (f32[392,192]{1,0:T(8,128)S(1)}, f32[232,192]{1,0:T(8,128)S(1)}, f32[160,192]{1,0:T(8,128)S(1)}) custom-call(bf16[720,1024]{1,0:T(8,128)(2,1)S(1)} %get-tuple-element.36.left_ref, bf16[96,1024]{1,0:T(8,128)(2,1)S(1)} %get-tuple-element.52.rest_0_, bf16[96,1024]{1,0:T(8,128)(2,1)S(1)} %get-tuple-element.53.rest_1_, ...), custom_call_target="tpu_custom_call" | custom-call | flops 100000000 | tf_op jit(solution)/shard_map/next_products/pallas_call | solution.py:40
  44.5 0.0 copy-start.1
  44.5 0.1 collective-permute-start.16
  44.6 0.6 collective-permute-start.13
  45.2 2.2 %collective-permute-done.9.rest_1_.rest_0_ = f32[232,384]{1,0:T(8,128)S(1)} collective-permute-done((f32[232,384]{1,0:T(8,128)S(1)}, f32[232,384]{1,0:T(8,128)S(1)}, u32[]{:S(2)}, u32[]{:S(2)}) %collective-permute-start.9) | collective-permute-done | bytes 356384 | tf_op jit(solution)/shard_map/ppermute | solution.py:410
  47.4 0.0 collective-permute-done.16.came_ref
  47.4 0.1 add_cores.9.rest_0_
  47.5 0.6 collective-permute-start.17
  48.1 0.4 chunk_stat.4.rest_0_
  48.6 0.6 chunk_stat.5.rest_1_
  49.2 0.6 chunk_stat.6.rest_2_
  49.8 6.1 %collective-permute-done.13.rest_1_ = f32[232,384]{1,0:T(8,128)S(1)} collective-permute-done((f32[232,384]{1,0:T(8,128)S(1)}, f32[232,384]{1,0:T(8,128)S(1)}, u32[]{:S(2)}, u32[]{:S(2)}) %collective-permute-start.13) | collective-permute-done | bytes 356384 | tf_op jit(solution)/shard_map/ppermute | solution.py:410
  55.8 0.6 chunk_stat.7.rest_3_
  56.4 1.0 %place.1.placed_ref = f32[160,1536]{1,0:T(8,128)S(1)} custom-call(s32[2]{0:T(128)S(1)} %copy-done.11, f32[160,1536]{1,0:T(8,128)S(1)} %get-tuple-element.35.scale_ref, f32[160,192]{1,0:T(8,128)S(1)} %chunk_stat.4.rest_0_, f32[160,384]{1,0:T(8,128)S(1)} %chunk_stat.5.rest_1_, f32[160,384]{1,0:T(8,128)S(1)} %chunk_stat.6.rest_2_, f32[160,384]{1,0:T(8,128)S(1)} %chunk_stat.7.rest_3_), custom_call_target="tpu_custom_call" | custom-call | flops 1 | tf_op jit(solution)/shard_map/place/pallas_call | solution.py:40
  57.4 1.8 %collective-permute-done.17.rest_1_ = f32[352,128]{1,0:T(8,128)S(1)} collective-permute-done((f32[352,128]{1,0:T(8,128)S(1)}, f32[352,128]{1,0:T(8,128)S(1)}, u32[]{:S(2)}, u32[]{:S(2)}) %collective-permute-start.17) | collective-permute-done | bytes 180256 | tf_op jit(solution)/shard_map/ppermute | solution.py:410
  59.2 2.1 %finish.1 = f32[160,1536]{1,0:T(8,128)} custom-call(s32[2]{0:T(128)S(1)} %copy-done.11, f32[232,72]{1,0:T(8,128)S(1)} %get-tuple-element.34.solved_ref.refs_3_, f32[160,1536]{1,0:T(8,128)S(1)} %get-tuple-element.35.scale_ref, f32[160,1536]{1,0:T(8,128)S(1)} %place.1.placed_ref, f32[160,192]{1,0:T(8,128)S(1)} %get-tuple-element.54.mine_ref, ...), custom_call_target="tpu_custom_call" | custom-call | flops 1 | tf_op jit(solution)/shard_map/finish/pallas_call | solution.py:40
  (24 shorter events, 0.1 us)
Async XLA Ops:
  0.0 12.3 %collective-permute-start.2 = (bf16[192,1024]{1,0:T(8,128)(2,1)}, bf16[192,1024]{1,0:T(8,128)(2,1)S(1)}, u32[]{:S(2)}, u32[]{:S(2)}) collective-permute-start(bf16[192,1024]{1,0:T(8,128)(2,1)} %bitcast.5), channel_id=1, source_target_pairs={{0,2},{2,4},{4,6},{6,7},{7,5},{5,3},{3,1},{1,0},{8,10},{10,12},{12... | collective-permute-start | bytes 1179656 | tf_op jit(solution)/shard_map/ppermute | solution.py:416
  3.0 10.8 %collective-permute-start.3 = (bf16[192,1024]{1,0:T(8,128)(2,1)}, bf16[192,1024]{1,0:T(8,128)(2,1)S(1)}, u32[]{:S(2)}, u32[]{:S(2)}) collective-permute-start(bf16[192,1024]{1,0:T(8,128)(2,1)} %bitcast.6), channel_id=1, source_target_pairs={{2,0},{4,2},{6,4},{7,6},{5,7},{3,5},{1,3},{0,1},{10,8},{12,10},{14... | collective-permute-start | bytes 1179656 | tf_op jit(solution)/shard_map/ppermute | solution.py:419
  3.1 10.7 %copy-start.10 = (s32[2]{0:T(128)}, s32[2]{0:T(128)S(1)}, u32[]{:S(2)}) copy-start(s32[2]{0:T(128)S(1)} %pad_add_fusion.ids_ref) | copy-start | bytes 28
  3.1 1.3 %copy-start.4 = (bf16[1024,640]{1,0:T(8,128)(2,1)S(1)}, bf16[1024,640]{1,0:T(8,128)(2,1)}, u32[]{:S(2)}) copy-start(bf16[1024,640]{1,0:T(8,128)(2,1)} %e_ref.1) | copy-start | bytes 3932164
  4.4 1.0 %copy-start.7 = (bf16[1024,192]{0,1:T(8,128)(2,1)S(1)}, bf16[1024,192]{0,1:T(8,128)(2,1)}, u32[]{:S(2)}) copy-start(bf16[1024,192]{0,1:T(8,128)(2,1)} %param.7) | copy-start | bytes 1179652
  5.4 0.9 %copy-start.8 = (bf16[1024,64]{0,1:T(8,128)(2,1)S(1)}, bf16[1024,64]{0,1:T(8,128)(2,1)}, u32[]{:S(2)}) copy-start(bf16[1024,64]{0,1:T(8,128)(2,1)} %param.8) | copy-start | bytes 393220
  8.7 21.1 %copy-start.5 = (f32[160,320]{1,0:T(8,128)}, f32[160,320]{1,0:T(8,128)S(1)}, u32[]{:S(2)}) copy-start(f32[160,320]{1,0:T(8,128)S(1)} %get-tuple-element.31.mine_ref) | copy-start | bytes 614404
  8.7 7.2 %collective-permute-start = (f32[392,320]{1,0:T(8,128)S(1)}, f32[392,320]{1,0:T(8,128)S(1)}, u32[]{:S(2)}, u32[]{:S(2)}) collective-permute-start(f32[392,320]{1,0:T(8,128)S(1)} %get-tuple-element.32), channel_id=1, source_target_pairs={{0,8},{8,0},{16,24},{24,16},{1,9},{9,1},{17,25},{25,17},{2,10},{10... | collective-permute-start | bytes 1505288 | tf_op jit(solution)/shard_map/ppermute | solution.py:410
  13.8 9.7 %collective-permute-start.6 = (bf16[192,1024]{1,0:T(8,128)(2,1)S(1)}, bf16[192,1024]{1,0:T(8,128)(2,1)S(1)}, u32[]{:S(2)}, u32[]{:S(2)}) collective-permute-start(bf16[192,1024]{1,0:T(8,128)(2,1)S(1)} %get-tuple-element.37.rest_0_), channel_id=1, source_target_pairs={{0,2},{2,4},{4,6},{6,7},{7,5},{5,3},{3,1},{1,0},{8,10},{10,12},{12... | collective-permute-start | bytes 1179656 | tf_op jit(solution)/shard_map/ppermute | solution.py:416
  15.4 9.4 %collective-permute-start.7 = (bf16[192,1024]{1,0:T(8,128)(2,1)S(1)}, bf16[192,1024]{1,0:T(8,128)(2,1)S(1)}, u32[]{:S(2)}, u32[]{:S(2)}) collective-permute-start(bf16[192,1024]{1,0:T(8,128)(2,1)S(1)} %get-tuple-element.38.rest_1_), channel_id=1, source_target_pairs={{2,0},{4,2},{6,4},{7,6},{5,7},{3,5},{1,3},{0,1},{10,8},{12,10},{14... | collective-permute-start | bytes 1179656 | tf_op jit(solution)/shard_map/ppermute | solution.py:419
  15.9 8.8 %collective-permute-start.1 = (f32[584,128]{1,0:T(8,128)S(1)}, f32[584,128]{1,0:T(8,128)S(1)}, u32[]{:S(2)}, u32[]{:S(2)}) collective-permute-start(f32[584,128]{1,0:T(8,128)S(1)} %add_cores.5.rest_0_), channel_id=1, source_target_pairs={{0,16},{8,24},{16,0},{24,8},{1,17},{9,25},{17,1},{25,9},{2,18},{10... | collective-permute-start | bytes 897032 | tf_op jit(solution)/shard_map/ppermute | solution.py:410
  18.8 8.0 %collective-permute-start.4 = (f32[392,384]{1,0:T(8,128)S(1)}, f32[392,384]{1,0:T(8,128)S(1)}, u32[]{:S(2)}, u32[]{:S(2)}) collective-permute-start(f32[392,384]{1,0:T(8,128)S(1)} %get-tuple-element.40), channel_id=1, source_target_pairs={{0,8},{8,0},{16,24},{24,16},{1,9},{9,1},{17,25},{25,17},{2,10},{10... | collective-permute-start | bytes 1806344 | tf_op jit(solution)/shard_map/ppermute | solution.py:410
  24.8 10.2 %collective-permute-start.10 = (bf16[192,1024]{1,0:T(8,128)(2,1)S(1)}, bf16[192,1024]{1,0:T(8,128)(2,1)S(1)}, u32[]{:S(2)}, u32[]{:S(2)}) collective-permute-start(bf16[192,1024]{1,0:T(8,128)(2,1)S(1)} %get-tuple-element.42.rest_0_), channel_id=1, source_target_pairs={{0,2},{2,4},{4,6},{6,7},{7,5},{5,3},{3,1},{1,0},{8,10},{10,12},{12... | collective-permute-start | bytes 1179656 | tf_op jit(solution)/shard_map/ppermute | solution.py:416
  26.4 8.6 %collective-permute-start.11 = (bf16[192,1024]{1,0:T(8,128)(2,1)S(1)}, bf16[192,1024]{1,0:T(8,128)(2,1)S(1)}, u32[]{:S(2)}, u32[]{:S(2)}) collective-permute-start(bf16[192,1024]{1,0:T(8,128)(2,1)S(1)} %get-tuple-element.43.rest_1_), channel_id=1, source_target_pairs={{2,0},{4,2},{6,4},{7,6},{5,7},{3,5},{1,3},{0,1},{10,8},{12,10},{14... | collective-permute-start | bytes 1179656 | tf_op jit(solution)/shard_map/ppermute | solution.py:419
  26.8 2.9 %copy-start = (f32[392,384]{1,0:T(8,128)}, f32[392,384]{1,0:T(8,128)S(1)}, u32[]{:S(2)}) copy-start(f32[392,384]{1,0:T(8,128)S(1)} %collective-permute-done.4.came_ref) | copy-start | bytes 1806340
  26.9 8.1 %copy-start.2 = (f32[232,384]{1,0:T(8,128)}, f32[232,384]{1,0:T(8,128)S(1)}, u32[]{:S(2)}) copy-start(f32[232,384]{1,0:T(8,128)S(1)} %add_cores.6.rest_0_) | copy-start | bytes 1069060
  26.9 2.9 %copy-start.9 = (s32[24,160]{1,0:T(8,128)S(1)}, s32[24,160]{1,0:T(8,128)}, u32[]{:S(2)}) copy-start(s32[24,160]{1,0:T(8,128)} %rest_2_.1) | copy-start | bytes 46084
  26.9 2.9 %copy-start.12 = (f32[5,16]{1,0:T(8,128)S(1)}, f32[5,16]{1,0:T(8,128)}, u32[]{:S(2)}) copy-start(f32[5,16]{1,0:T(8,128)} %weight_ref.1) | copy-start | bytes 964
  26.9 2.9 %copy-start.13 = (s32[160]{0:T(256)S(1)}, s32[160]{0:T(256)}, u32[]{:S(2)}) copy-start(s32[160]{0:T(256)} %param.10) | copy-start | bytes 1924
  26.9 8.0 %collective-permute-start.5 = (f32[232,384]{1,0:T(8,128)S(1)}, f32[232,384]{1,0:T(8,128)S(1)}, u32[]{:S(2)}, u32[]{:S(2)}) collective-permute-start(f32[232,384]{1,0:T(8,128)S(1)} %add_cores.6.rest_0_), channel_id=1, source_target_pairs={{0,16},{8,24},{16,0},{24,8},{1,17},{9,25},{17,1},{25,9},{2,18},{10... | collective-permute-start | bytes 1069064 | tf_op jit(solution)/shard_map/ppermute | solution.py:410
  29.8 7.4 %collective-permute-start.8 = (f32[392,384]{1,0:T(8,128)S(1)}, f32[392,384]{1,0:T(8,128)S(1)}, u32[]{:S(2)}, u32[]{:S(2)}) collective-permute-start(f32[392,384]{1,0:T(8,128)S(1)} %get-tuple-element.45), channel_id=1, source_target_pairs={{0,8},{8,0},{16,24},{24,16},{1,9},{9,1},{17,25},{25,17},{2,10},{10... | collective-permute-start | bytes 1806344 | tf_op jit(solution)/shard_map/ppermute | solution.py:410
  35.0 7.3 %collective-permute-start.14 = (bf16[96,1024]{1,0:T(8,128)(2,1)S(1)}, bf16[96,1024]{1,0:T(8,128)(2,1)S(1)}, u32[]{:S(2)}, u32[]{:S(2)}) collective-permute-start(bf16[96,1024]{1,0:T(8,128)(2,1)S(1)} %slice.6), channel_id=1, source_target_pairs={{0,2},{2,4},{4,6},{6,7},{7,5},{5,3},{3,1},{1,0},{8,10},{10,12},{12... | collective-permute-start | bytes 589832 | tf_op jit(solution)/shard_map/ppermute | solution.py:416
  36.6 7.1 %collective-permute-start.15 = (bf16[96,1024]{1,0:T(8,128)(2,1)S(1)}, bf16[96,1024]{1,0:T(8,128)(2,1)S(1)}, u32[]{:S(2)}, u32[]{:S(2)}) collective-permute-start(bf16[96,1024]{1,0:T(8,128)(2,1)S(1)} %slice.7), channel_id=1, source_target_pairs={{2,0},{4,2},{6,4},{7,6},{5,7},{3,5},{1,3},{0,1},{10,8},{12,10},{14... | collective-permute-start | bytes 589832 | tf_op jit(solution)/shard_map/ppermute | solution.py:419
  37.2 10.2 %collective-permute-start.9 = (f32[232,384]{1,0:T(8,128)S(1)}, f32[232,384]{1,0:T(8,128)S(1)}, u32[]{:S(2)}, u32[]{:S(2)}) collective-permute-start(f32[232,384]{1,0:T(8,128)S(1)} %add_cores.7.rest_0_.rest_2_), channel_id=1, source_target_pairs={{0,16},{8,24},{16,0},{24,8},{1,17},{9,25},{17,1},{25,9},{2,18},{10... | collective-permute-start | bytes 1069064 | tf_op jit(solution)/shard_map/ppermute | solution.py:410
  39.6 4.1 %collective-permute-start.12 = (f32[392,384]{1,0:T(8,128)S(1)}, f32[392,384]{1,0:T(8,128)S(1)}, u32[]{:S(2)}, u32[]{:S(2)}) collective-permute-start(f32[392,384]{1,0:T(8,128)S(1)} %get-tuple-element.50), channel_id=1, source_target_pairs={{0,8},{8,0},{16,24},{24,16},{1,9},{9,1},{17,25},{25,17},{2,10},{10... | collective-permute-start | bytes 1806344 | tf_op jit(solution)/shard_map/ppermute | solution.py:410
  43.7 4.4 %copy-start.6 = (f32[160,320]{1,0:T(8,128)S(1)}, f32[160,320]{1,0:T(8,128)}, u32[]{:S(2)}) copy-start(f32[160,320]{1,0:T(8,128)} %copy-done.5) | copy-start | bytes 614404
  44.5 4.0 %copy-start.1 = (f32[392,384]{1,0:T(8,128)S(1)}, f32[392,384]{1,0:T(8,128)}, u32[]{:S(2)}) copy-start(f32[392,384]{1,0:T(8,128)} %copy-done) | copy-start | bytes 1806340
  44.5 4.0 %copy-start.3 = (f32[232,384]{1,0:T(8,128)S(1)}, f32[232,384]{1,0:T(8,128)}, u32[]{:S(2)}) copy-start(f32[232,384]{1,0:T(8,128)} %copy-done.2) | copy-start | bytes 1069060
  44.5 2.9 %collective-permute-start.16 = (f32[392,192]{1,0:T(8,128)S(1)}, f32[392,192]{1,0:T(8,128)S(1)}, u32[]{:S(2)}, u32[]{:S(2)}) collective-permute-start(f32[392,192]{1,0:T(8,128)S(1)} %get-tuple-element.55), channel_id=1, source_target_pairs={{0,8},{8,0},{16,24},{24,16},{1,9},{9,1},{17,25},{25,17},{2,10},{10... | collective-permute-start | bytes 903176 | tf_op jit(solution)/shard_map/ppermute | solution.py:410
  44.6 11.2 %collective-permute-start.13 = (f32[232,384]{1,0:T(8,128)S(1)}, f32[232,384]{1,0:T(8,128)S(1)}, u32[]{:S(2)}, u32[]{:S(2)}) collective-permute-start(f32[232,384]{1,0:T(8,128)S(1)} %add_cores.8.rest_0_.rest_2_), channel_id=1, source_target_pairs={{0,16},{8,24},{16,0},{24,8},{1,17},{9,25},{17,1},{25,9},{2,18},{10... | collective-permute-start | bytes 1069064 | tf_op jit(solution)/shard_map/ppermute | solution.py:410
  47.5 11.7 %collective-permute-start.17 = (f32[352,128]{1,0:T(8,128)S(1)}, f32[352,128]{1,0:T(8,128)S(1)}, u32[]{:S(2)}, u32[]{:S(2)}) collective-permute-start(f32[352,128]{1,0:T(8,128)S(1)} %add_cores.9.rest_0_), channel_id=1, source_target_pairs={{0,16},{8,24},{16,0},{24,8},{1,17},{9,25},{17,1},{25,9},{2,18},{10... | collective-permute-start | bytes 540680 | tf_op jit(solution)/shard_map/ppermute | solution.py:410
  49.2 7.2 %copy-start.11 = (s32[2]{0:T(128)S(1)}, s32[2]{0:T(128)}, u32[]{:S(2)}) copy-start(s32[2]{0:T(128)} %copy-done.10) | copy-start | bytes 28
where the time goes:
time: 61.5 us; the launch traced here: 61.3 us
  waiting for transfers between devices  25.3 us (41%)
  Pallas kernels  17.6 us (29%)
  starting transfers between devices  14.8 us (24%)
  local copies, waits for them, and re-layouts  3.3 us (5%)
    pallas_call x17, Pallas kernels, call(): pl.pallas_call(kernel, out_shape=out_shape, in_specs=[smem] * scalars + [...  17.6 us
    ppermute x4, waiting for transfers between devices, right(): return lax.ppermute(x, 'var', forward)  11 us
    ppermute x10, waiting for transfers between devices, exchange(): return lax.ppermute(x, 'samp', [(s, s ^ d) for s in range(parts)])  10.1 us
    ppermute x4, starting transfers between devices, right(): return lax.ppermute(x, 'var', forward)  7.81 us
    ppermute x10, starting transfers between devices, exchange(): return lax.ppermute(x, 'samp', [(s, s ^ d) for s in range(parts)])  5.55 us
    ppermute x4, waiting for transfers between devices, left(): return lax.ppermute(x, 'var', backward)  4.18 us
    unnamed x28, local copies, waits for them, and re-layouts  3.27 us
    ppermute x4, starting transfers between devices, left(): return lax.ppermute(x, 'var', backward)  1.4 us
  transfers between devices with their start and end apart: 18, of which 9 were waited for; matrix products, arithmetic and copies ran while one was open for 0% of the time, Pallas kernels for 25%

commit v1 on v0

--- a/solution.py
+++ b/solution.py
@@ -10,7 +10,7 @@
 
 LANES = 128
 EPS = 1e-06
-COST = {'products': 10**8, 'add': 1, 'solve': 10**8, 'stat': 1, 'place': 1, 'finish': 1, 'gate': 10**11}
+COST = {'products': 10**8, 'add': 1, 'solve': 10**8, 'stat': 1, 'place': 1, 'finish': 1, 'gate': 10**10}
 VMEM_LIMIT = 10 * 1024 * 1024
 
 NT = (((1,), (1,)), ((), ()))
@@ -236,8 +236,8 @@
     return corr, fits
 
 
-def solve_kernel(covs, dof, weight_ref, mine_ref, came_ref, *rest):
-    refs, (bins_ref, folds_ref, solved_ref, scale_ref) = rest[:-4], rest[-4:]
+def solve_kernel(covs, dof, mine_ref, came_ref, *rest):
+    refs, (solved_ref, norm_ref) = rest[:-2], rest[-2:]
     genes = mine_ref.shape[0]
     rank, deep = covs + 1, covs + 8
     corr, fits = chunk_sums(genes, deep, mine_ref, came_ref, refs)
@@ -271,6 +271,26 @@
     solved_ref[:genes] = beta
     solved_ref[genes:] = inverse[:, :deep]
 
+    norm_ref[...] = jnp.broadcast_to(dof / norm, norm_ref.shape)
+
+
+def solve(mine, came, swapped, covs, dof):
+    genes = mine.shape[0]
+    outs = [
+        jax.ShapeDtypeStruct((genes + covs + 8, covs + 8), jnp.float32),
+        jax.ShapeDtypeStruct((genes, LANES), jnp.float32),
+    ]
+    return call(
+        functools.partial(solve_kernel, covs, dof),
+        outs,
+        "solve",
+        COST["solve"],
+        (mine, came, *swapped),
+        scalars=0,
+    )
+
+
+def widen_kernel(weight_ref, norm_ref, bins_ref, folds_ref, scale_ref):
     bins, folds = bins_ref[...], folds_ref[...]
     tile = jnp.zeros(bins.shape, jnp.float32)
     for b in range(weight_ref.shape[1]):
@@ -278,25 +298,20 @@
         for f in range(weight_ref.shape[0]):
             of_bin = jnp.where(folds == f, weight_ref[f, b], of_bin)
         tile = jnp.where(bins == b, of_bin, tile)
-    tile = tile.T * (dof / norm)
-    width = scale_ref.shape[1] // tile.shape[1]
+    tile = tile.T * norm_ref[:, :1]
+    genes, width = tile.shape[0], scale_ref.shape[1] // tile.shape[1]
     for t in range(0, tile.shape[1], 2):
         pair = [jnp.broadcast_to(tile[:, i : i + 1], (genes, width)) for i in (t, t + 1)]
         scale_ref[:, t * width : (t + 2) * width] = jnp.concatenate(pair, axis=1)
 
 
-def solve(weights, mine, came, swapped, bins, folds, covs, dof, variants):
-    genes = mine.shape[0]
-    outs = [
-        jax.ShapeDtypeStruct((genes + covs + 8, covs + 8), jnp.float32),
-        jax.ShapeDtypeStruct((genes, variants), jnp.float32),
-    ]
-    return call(
-        functools.partial(solve_kernel, covs, dof),
-        outs,
-        "solve",
-        COST["solve"],
-        (weights, mine, came, *swapped, bins, folds),
+def widen(weights, norm, bins, folds, variants):
+    return call(
+        widen_kernel,
+        jax.ShapeDtypeStruct((norm.shape[0], variants), jnp.float32),
+        "widen",
+        COST["place"],
+        (weights, norm, bins, folds),
     )
 
 
@@ -455,9 +470,8 @@
         done["came", k], done["sent", k] = came, sent[0][0]
         done["got", k], done["rest", k] = got[-1][0], got[-1][-1]
         if k == 0:
-            solved, scale = solve(
-                fold_weights, mine, came, swapped, distance_bins, gene_folds[None], covs, dof, ring * variants
-            )
+            solved, norm = solve(mine, came, swapped, covs, dof)
+            scale = widen(fold_weights, norm, distance_bins, gene_folds[None], ring * variants)
             done["solved", 0] = solved
         if k < middle:
             stats.append(chunk_stat(solved, mine, came, swapped, covs, LANES if k == 0 else 0))

time: 61.5 us -> 60 us (0.976)
  waiting for transfers between devices: 25.3 us -> 22.9 us
  starting transfers between devices: 14.8 us -> 15.8 us
    ppermute x10, waiting for transfers between devices: 10.1 us -> 8.05 us  [exchange(): return lax.ppermute(x, 'samp', [(s, s ^ d) for s in range(parts)])]
    ppermute x4, waiting for transfers between devices: 11 us -> 9.52 us  [right(): return lax.ppermute(x, 'var', forward)]
    ppermute x4, waiting for transfers between devices: 4.18 us -> 5.33 us  [left(): return lax.ppermute(x, 'var', backward)]
    ppermute x10, starting transfers between devices: 5.55 us -> 6.61 us  [exchange(): return lax.ppermute(x, 'samp', [(s, s ^ d) for s in range(parts)])]
    pallas_call x17 -> x18, Pallas kernels: 17.6 us -> 17.6 us  [call(): pl.pallas_call(kernel, out_shape=out_shape, in_specs=[smem] * scalars + [...]
    unnamed x28 -> x12, local copies, waits for them, and re-layouts: 3.27 us -> 3.23 us
  transfers between devices with their start and end apart: 18 -> 18, of which waited for: 9 -> 10; matrix products, arithmetic and copies ran while one was open for 0% -> 0% of each run, Pallas kernels for 25% -> 26%
where the time goes in v1:
time: 60 us; the launch traced here: 59.8 us
  waiting for transfers between devices  22.9 us (38%)
  Pallas kernels  17.6 us (29%)
  starting transfers between devices  15.8 us (26%)
  local copies, waits for them, and re-layouts  3.26 us (5%)
    pallas_call x18, Pallas kernels, call(): pl.pallas_call(kernel, out_shape=out_shape, in_specs=[smem] * scalars + [...  17.6 us
    ppermute x4, waiting for transfers between devices, right(): return lax.ppermute(x, 'var', forward)  9.52 us
    ppermute x10, waiting for transfers between devices, exchange(): return lax.ppermute(x, 'samp', [(s, s ^ d) for s in range(parts)])  8.05 us
    ppermute x4, starting transfers between devices, right(): return lax.ppermute(x, 'var', forward)  7.75 us
    ppermute x10, starting transfers between devices, exchange(): return lax.ppermute(x, 'samp', [(s, s ^ d) for s in range(parts)])  6.61 us
    ppermute x4, waiting for transfers between devices, left(): return lax.ppermute(x, 'var', backward)  5.33 us
    unnamed x12, local copies, waits for them, and re-layouts  3.23 us
    ppermute x4, starting transfers between devices, left(): return lax.ppermute(x, 'var', backward)  1.46 us
  transfers between devices with their start and end apart: 18, of which 10 were waited for; matrix products, arithmetic and copies ran while one was open for 0% of the time, Pallas kernels for 26%

profile of v1, /device:TPU:0, one launch (start us, length us, event | category | flops | bytes accessed | tf_op | source)
XLA Modules:
  0.0 59.8 jit_solution(12390554516749576774)
XLA Ops:
  0.0 3.0 %collective-permute-start.2 = (bf16[192,1024]{1,0:T(8,128)(2,1)}, bf16[192,1024]{1,0:T(8,128)(2,1)S(1)}, u32[]{:S(2)}, u32[]{:S(2)}) collective-permute-start(bf16[192,1024]{1,0:T(8,128)(2,1)} %bitcast.5), channel_id=1, source_target_pairs={{0,2},{2,4},{4,6},{6,7},{7,5},{5,3},{3,1},{1,0},{8,10},{10,12},{12... | collective-permute-start | bytes 1179656 | tf_op jit(solution)/shard_map/ppermute | solution.py:431
  3.0 0.0 collective-permute-start.3
  3.0 0.1 pad_add_fusion.ids_ref
  3.1 0.0 copy-start
  3.1 1.3 %copy-done = bf16[1024,640]{1,0:T(8,128)(2,1)S(1)} copy-done((bf16[1024,640]{1,0:T(8,128)(2,1)S(1)}, bf16[1024,640]{1,0:T(8,128)(2,1)}, u32[]{:S(2)}) %copy-start) | copy-done | bytes 1310744
  4.4 0.0 copy-start.1
  4.4 1.0 %copy-done.1 = bf16[1024,192]{0,1:T(8,128)(2,1)S(1)} copy-done((bf16[1024,192]{0,1:T(8,128)(2,1)S(1)}, bf16[1024,192]{0,1:T(8,128)(2,1)}, u32[]{:S(2)}) %copy-start.1) | copy-done | bytes 393240
  5.4 0.0 copy-start.2
  5.4 0.9 %copy-done.2 = bf16[1024,64]{0,1:T(8,128)(2,1)S(1)} copy-done((bf16[1024,64]{0,1:T(8,128)(2,1)S(1)}, bf16[1024,64]{0,1:T(8,128)(2,1)}, u32[]{:S(2)}) %copy-start.2) | copy-done | bytes 131096
  6.3 2.4 %first_products.1 = (bf16[720,1024]{1,0:T(8,128)(2,1)S(1)}, f32[392,320]{1,0:T(8,128)S(1)}, f32[232,320]{1,0:T(8,128)S(1)}, f32[160,320]{1,0:T(8,128)S(1)}) custom-call(s32[2]{0:T(128)S(1)} %pad_add_fusion.ids_ref, bf16[1024,640]{1,0:T(8,128)(2,1)S(1)} %copy-done, bf16[192,1024]{1,0:T(8,128)(2,1)S(1)} %bitcast.7, bf16[64,1024]{1,0:T(8,128)(2,1)S(1)} %bitcast.8), custom_call_target="tpu_custom_call" | custom-call | flops 100000000 | tf_op jit(solution)/shard_map/first_products/pallas_call | solution.py:40
  8.7 0.0 collective-permute-start
  8.7 3.6 %collective-permute-done.2.refs_0_ = bf16[192,1024]{1,0:T(8,128)(2,1)S(1)} collective-permute-done((bf16[192,1024]{1,0:T(8,128)(2,1)}, bf16[192,1024]{1,0:T(8,128)(2,1)S(1)}, u32[]{:S(2)}, u32[]{:S(2)}) %collective-permute-start.2) | collective-permute-done | bytes 393248 | tf_op jit(solution)/shard_map/ppermute | solution.py:431
  12.3 1.5 %collective-permute-done.3.refs_1_ = bf16[192,1024]{1,0:T(8,128)(2,1)S(1)} collective-permute-done((bf16[192,1024]{1,0:T(8,128)(2,1)}, bf16[192,1024]{1,0:T(8,128)(2,1)S(1)}, u32[]{:S(2)}, u32[]{:S(2)}) %collective-permute-start.3) | collective-permute-done | bytes 393248 | tf_op jit(solution)/shard_map/ppermute | solution.py:434
  13.8 1.6 %collective-permute-start.6 = (bf16[192,1024]{1,0:T(8,128)(2,1)S(1)}, bf16[192,1024]{1,0:T(8,128)(2,1)S(1)}, u32[]{:S(2)}, u32[]{:S(2)}) collective-permute-start(bf16[192,1024]{1,0:T(8,128)(2,1)S(1)} %get-tuple-element.37.rest_0_), channel_id=1, source_target_pairs={{0,2},{2,4},{4,6},{6,7},{7,5},{5,3},{3,1},{1,0},{8,10},{10,12},{12... | collective-permute-start | bytes 1179656 | tf_op jit(solution)/shard_map/ppermute | solution.py:431
  15.4 0.4 collective-permute-start.7
  15.8 0.0 collective-permute-done.came_ref.rest_2_
  15.8 0.1 add_cores.5.rest_0_
  15.9 1.6 %collective-permute-start.1 = (f32[584,128]{1,0:T(8,128)S(1)}, f32[584,128]{1,0:T(8,128)S(1)}, u32[]{:S(2)}, u32[]{:S(2)}) collective-permute-start(f32[584,128]{1,0:T(8,128)S(1)} %add_cores.5.rest_0_), channel_id=1, source_target_pairs={{0,16},{8,24},{16,0},{24,8},{1,17},{9,25},{17,1},{25,9},{2,18},{10... | collective-permute-start | bytes 897032 | tf_op jit(solution)/shard_map/ppermute | solution.py:425
  17.5 1.3 %next_products.4 = (f32[392,384]{1,0:T(8,128)S(1)}, f32[232,384]{1,0:T(8,128)S(1)}, f32[160,384]{1,0:T(8,128)S(1)}) custom-call(bf16[720,1024]{1,0:T(8,128)(2,1)S(1)} %get-tuple-element.36.left_ref, bf16[192,1024]{1,0:T(8,128)(2,1)S(1)} %get-tuple-element.37.rest_0_, bf16[192,1024]{1,0:T(8,128)(2,1)S(1)} %get-tuple-element.38.rest_1_, ...), custom_call_target="tpu_custom_call" | custom-call | flops 100000000 | tf_op jit(solution)/shard_map/next_products/pallas_call | solution.py:40
  18.8 0.0 collective-permute-start.4
  18.8 4.7 %collective-permute-done.6.refs_0_ = bf16[192,1024]{1,0:T(8,128)(2,1)S(1)} collective-permute-done((bf16[192,1024]{1,0:T(8,128)(2,1)S(1)}, bf16[192,1024]{1,0:T(8,128)(2,1)S(1)}, u32[]{:S(2)}, u32[]{:S(2)}) %collective-permute-start.6) | collective-permute-done | bytes 393248 | tf_op jit(solution)/shard_map/ppermute | solution.py:431
  23.5 1.3 %collective-permute-done.7.refs_1_ = bf16[192,1024]{1,0:T(8,128)(2,1)S(1)} collective-permute-done((bf16[192,1024]{1,0:T(8,128)(2,1)S(1)}, bf16[192,1024]{1,0:T(8,128)(2,1)S(1)}, u32[]{:S(2)}, u32[]{:S(2)}) %collective-permute-start.7) | collective-permute-done | bytes 393248 | tf_op jit(solution)/shard_map/ppermute | solution.py:434
  24.8 0.0 collective-permute-done.1.rest_1_.refs_2_.rest_2_
  24.8 1.6 %collective-permute-start.10 = (bf16[192,1024]{1,0:T(8,128)(2,1)S(1)}, bf16[192,1024]{1,0:T(8,128)(2,1)S(1)}, u32[]{:S(2)}, u32[]{:S(2)}) collective-permute-start(bf16[192,1024]{1,0:T(8,128)(2,1)S(1)} %get-tuple-element.42.rest_0_), channel_id=1, source_target_pairs={{0,2},{2,4},{4,6},{6,7},{7,5},{5,3},{3,1},{1,0},{8,10},{10,12},{12... | collective-permute-start | bytes 1179656 | tf_op jit(solution)/shard_map/ppermute | solution.py:431
  26.4 0.4 collective-permute-start.11
  26.8 0.0 collective-permute-done.4.came_ref
  26.9 1.6 %collective-permute-start.5 = (f32[232,384]{1,0:T(8,128)S(1)}, f32[232,384]{1,0:T(8,128)S(1)}, u32[]{:S(2)}, u32[]{:S(2)}) collective-permute-start(f32[232,384]{1,0:T(8,128)S(1)} %add_cores.6.rest_0_), channel_id=1, source_target_pairs={{0,16},{8,24},{16,0},{24,8},{1,17},{9,25},{17,1},{25,9},{2,18},{10... | collective-permute-start | bytes 1069064 | tf_op jit(solution)/shard_map/ppermute | solution.py:425
  28.4 1.3 %next_products.5 = (f32[392,384]{1,0:T(8,128)S(1)}, f32[232,384]{1,0:T(8,128)S(1)}, f32[160,384]{1,0:T(8,128)S(1)}) custom-call(bf16[720,1024]{1,0:T(8,128)(2,1)S(1)} %get-tuple-element.36.left_ref, bf16[192,1024]{1,0:T(8,128)(2,1)S(1)} %get-tuple-element.42.rest_0_, bf16[192,1024]{1,0:T(8,128)(2,1)S(1)} %get-tuple-element.43.rest_1_, ...), custom_call_target="tpu_custom_call" | custom-call | flops 100000000 | tf_op jit(solution)/shard_map/next_products/pallas_call | solution.py:40
  29.7 0.0 collective-permute-start.8
  29.7 3.7 %solve.1 = (f32[232,72]{1,0:T(8,128)S(1)}, f32[160,128]{1,0:T(8,128)S(1)}) custom-call(f32[160,320]{1,0:T(8,128)S(1)} %get-tuple-element.31.mine_ref, f32[392,320]{1,0:T(8,128)S(1)} %collective-permute-done.came_ref.rest_2_, f32[584,128]{1,0:T(8,128)S(1)} %add_cores.5.rest_0_, f32[584,128]{1,0:T(8,128)S(1)} %collective-permute-done.1.rest_1_.refs_2_.rest_2_), custom_call_target="tpu_custom_call" | custom-call | flops 100000000 | tf_op jit(solution)/shard_map/solve/pallas_call | solution.py:40
  33.4 0.0 collective-permute-done.10.refs_0_
  33.4 1.2 %collective-permute-done.11.refs_1_ = bf16[192,1024]{1,0:T(8,128)(2,1)S(1)} collective-permute-done((bf16[192,1024]{1,0:T(8,128)(2,1)S(1)}, bf16[192,1024]{1,0:T(8,128)(2,1)S(1)}, u32[]{:S(2)}, u32[]{:S(2)}) %collective-permute-start.11) | collective-permute-done | bytes 393248 | tf_op jit(solution)/shard_map/ppermute | solution.py:434
  34.5 0.0 collective-permute-done.5.rest_1_.refs_2_
  34.6 1.6 %collective-permute-start.14 = (bf16[96,1024]{1,0:T(8,128)(2,1)S(1)}, bf16[96,1024]{1,0:T(8,128)(2,1)S(1)}, u32[]{:S(2)}, u32[]{:S(2)}) collective-permute-start(bf16[96,1024]{1,0:T(8,128)(2,1)S(1)} %slice.6), channel_id=1, source_target_pairs={{0,2},{2,4},{4,6},{6,7},{7,5},{5,3},{3,1},{1,0},{8,10},{10,12},{12... | collective-permute-start | bytes 589832 | tf_op jit(solution)/shard_map/ppermute | solution.py:431
  36.2 0.6 collective-permute-start.15
  36.7 0.0 collective-permute-done.8.came_ref
  36.8 1.6 %collective-permute-start.9 = (f32[232,384]{1,0:T(8,128)S(1)}, f32[232,384]{1,0:T(8,128)S(1)}, u32[]{:S(2)}, u32[]{:S(2)}) collective-permute-start(f32[232,384]{1,0:T(8,128)S(1)} %add_cores.7.rest_0_.rest_2_), channel_id=1, source_target_pairs={{0,16},{8,24},{16,0},{24,8},{1,17},{9,25},{17,1},{25,9},{2,18},{10... | collective-permute-start | bytes 1069064 | tf_op jit(solution)/shard_map/ppermute | solution.py:425
  38.3 1.3 %next_products.6 = (f32[392,384]{1,0:T(8,128)S(1)}, f32[232,384]{1,0:T(8,128)S(1)}, f32[160,384]{1,0:T(8,128)S(1)}) custom-call(bf16[720,1024]{1,0:T(8,128)(2,1)S(1)} %get-tuple-element.36.left_ref, bf16[192,1024]{1,0:T(8,128)(2,1)S(1)} %get-tuple-element.47.rest_0_, bf16[192,1024]{1,0:T(8,128)(2,1)S(1)} %get-tuple-element.48.rest_1_, ...), custom_call_target="tpu_custom_call" | custom-call | flops 100000000 | tf_op jit(solution)/shard_map/next_products/pallas_call | solution.py:40
  39.6 0.0 collective-permute-start.12
  39.6 1.2 %collective-permute-done.14.refs_0_ = bf16[96,1024]{1,0:T(8,128)(2,1)S(1)} collective-permute-done((bf16[96,1024]{1,0:T(8,128)(2,1)S(1)}, bf16[96,1024]{1,0:T(8,128)(2,1)S(1)}, u32[]{:S(2)}, u32[]{:S(2)}) %collective-permute-start.14) | collective-permute-done | bytes 196640 | tf_op jit(solution)/shard_map/ppermute | solution.py:431
  40.8 1.4 %collective-permute-done.15.refs_1_ = bf16[96,1024]{1,0:T(8,128)(2,1)S(1)} collective-permute-done((bf16[96,1024]{1,0:T(8,128)(2,1)S(1)}, bf16[96,1024]{1,0:T(8,128)(2,1)S(1)}, u32[]{:S(2)}, u32[]{:S(2)}) %collective-permute-start.15) | collective-permute-done | bytes 196640 | tf_op jit(solution)/shard_map/ppermute | solution.py:434
  42.2 0.0 collective-permute-done.12.came_ref
  42.2 0.0 copy-start.3
  42.2 0.0 copy-start.4
  42.2 0.0 copy-start.5
  42.3 0.8 %next_products.7 = (f32[392,192]{1,0:T(8,128)S(1)}, f32[232,192]{1,0:T(8,128)S(1)}, f32[160,192]{1,0:T(8,128)S(1)}) custom-call(bf16[720,1024]{1,0:T(8,128)(2,1)S(1)} %get-tuple-element.36.left_ref, bf16[96,1024]{1,0:T(8,128)(2,1)S(1)} %get-tuple-element.52.rest_0_, bf16[96,1024]{1,0:T(8,128)(2,1)S(1)} %get-tuple-element.53.rest_1_, ...), custom_call_target="tpu_custom_call" | custom-call | flops 100000000 | tf_op jit(solution)/shard_map/next_products/pallas_call | solution.py:40
  43.0 0.1 collective-permute-start.16
  43.1 1.3 %collective-permute-start.13 = (f32[232,384]{1,0:T(8,128)S(1)}, f32[232,384]{1,0:T(8,128)S(1)}, u32[]{:S(2)}, u32[]{:S(2)}) collective-permute-start(f32[232,384]{1,0:T(8,128)S(1)} %add_cores.8.rest_0_.rest_2_), channel_id=1, source_target_pairs={{0,16},{8,24},{16,0},{24,8},{1,17},{9,25},{17,1},{25,9},{2,18},{10... | collective-permute-start | bytes 1069064 | tf_op jit(solution)/shard_map/ppermute | solution.py:425
  44.4 1.5 %collective-permute-done.9.rest_1_.rest_0_ = f32[232,384]{1,0:T(8,128)S(1)} collective-permute-done((f32[232,384]{1,0:T(8,128)S(1)}, f32[232,384]{1,0:T(8,128)S(1)}, u32[]{:S(2)}, u32[]{:S(2)}) %collective-permute-start.9) | collective-permute-done | bytes 356384 | tf_op jit(solution)/shard_map/ppermute | solution.py:425
  45.9 0.0 collective-permute-done.16.came_ref
  45.9 0.1 add_cores.9.rest_0_
  46.0 0.6 %collective-permute-start.17 = (f32[352,128]{1,0:T(8,128)S(1)}, f32[352,128]{1,0:T(8,128)S(1)}, u32[]{:S(2)}, u32[]{:S(2)}) collective-permute-start(f32[352,128]{1,0:T(8,128)S(1)} %add_cores.9.rest_0_), channel_id=1, source_target_pairs={{0,16},{8,24},{16,0},{24,8},{1,17},{9,25},{17,1},{25,9},{2,18},{10... | collective-permute-start | bytes 540680 | tf_op jit(solution)/shard_map/ppermute | solution.py:425
  46.6 0.0 copy-done.3
  46.6 0.0 copy-done.4
  46.6 0.0 copy-done.5
  46.6 1.4 %widen.1.scale_ref = f32[160,1536]{1,0:T(8,128)S(1)} custom-call(f32[5,16]{1,0:T(8,128)S(1)} %copy-done.4, f32[160,128]{1,0:T(8,128)S(1)} %get-tuple-element.35.norm_ref, s32[24,160]{1,0:T(8,128)S(1)} %copy-done.3, s32[1,160]{1,0:T(1,128)S(1)} %bitcast.9), custom_call_target="tpu_custom_call" | custom-call | flops 1 | tf_op jit(solution)/shard_map/widen/pallas_call | solution.py:40
  48.0 0.5 chunk_stat.4.rest_0_
  48.5 0.6 chunk_stat.5.rest_1_
  49.0 0.6 chunk_stat.6.rest_2_
  49.6 4.7 %collective-permute-done.13.rest_1_ = f32[232,384]{1,0:T(8,128)S(1)} collective-permute-done((f32[232,384]{1,0:T(8,128)S(1)}, f32[232,384]{1,0:T(8,128)S(1)}, u32[]{:S(2)}, u32[]{:S(2)}) %collective-permute-start.13) | collective-permute-done | bytes 356384 | tf_op jit(solution)/shard_map/ppermute | solution.py:425
  54.3 0.6 chunk_stat.7.rest_3_
  54.9 1.0 %place.1.placed_ref = f32[160,1536]{1,0:T(8,128)S(1)} custom-call(s32[2]{0:T(128)S(1)} %pad_add_fusion.ids_ref, f32[160,1536]{1,0:T(8,128)S(1)} %widen.1.scale_ref, f32[160,192]{1,0:T(8,128)S(1)} %chunk_stat.4.rest_0_, f32[160,384]{1,0:T(8,128)S(1)} %chunk_stat.5.rest_1_, f32[160,384]{1,0:T(8,128)S(1)} %chunk_stat.6.rest_2_, f32[160,384]{1,0:T(8,128)S(1)} %chunk_stat.7.rest_3_), custom_call_target="tpu_custom_call" | custom-call | flops 1 | tf_op jit(solution)/shard_map/place/pallas_call | solution.py:40
  55.9 1.8 %collective-permute-done.17.rest_1_ = f32[352,128]{1,0:T(8,128)S(1)} collective-permute-done((f32[352,128]{1,0:T(8,128)S(1)}, f32[352,128]{1,0:T(8,128)S(1)}, u32[]{:S(2)}, u32[]{:S(2)}) %collective-permute-start.17) | collective-permute-done | bytes 180256 | tf_op jit(solution)/shard_map/ppermute | solution.py:425
  57.7 2.1 %finish.1 = f32[160,1536]{1,0:T(8,128)} custom-call(s32[2]{0:T(128)S(1)} %pad_add_fusion.ids_ref, f32[232,72]{1,0:T(8,128)S(1)} %get-tuple-element.34.solved_ref.refs_3_, f32[160,1536]{1,0:T(8,128)S(1)} %widen.1.scale_ref, f32[160,1536]{1,0:T(8,128)S(1)} %place.1.placed_ref, f32[160,192]{1,0:T(8,128)S(1)} %get-tuple-element.54.mine_ref, ...), custom_call_target="tpu_custom_call" | custom-call | flops 1 | tf_op jit(solution)/shard_map/finish/pallas_call | solution.py:40
  (9 shorter events, 0.2 us)
Async XLA Ops:
  0.0 12.3 %collective-permute-start.2 = (bf16[192,1024]{1,0:T(8,128)(2,1)}, bf16[192,1024]{1,0:T(8,128)(2,1)S(1)}, u32[]{:S(2)}, u32[]{:S(2)}) collective-permute-start(bf16[192,1024]{1,0:T(8,128)(2,1)} %bitcast.5), channel_id=1, source_target_pairs={{0,2},{2,4},{4,6},{6,7},{7,5},{5,3},{3,1},{1,0},{8,10},{10,12},{12... | collective-permute-start | bytes 1179656 | tf_op jit(solution)/shard_map/ppermute | solution.py:431
  3.0 10.8 %collective-permute-start.3 = (bf16[192,1024]{1,0:T(8,128)(2,1)}, bf16[192,1024]{1,0:T(8,128)(2,1)S(1)}, u32[]{:S(2)}, u32[]{:S(2)}) collective-permute-start(bf16[192,1024]{1,0:T(8,128)(2,1)} %bitcast.6), channel_id=1, source_target_pairs={{2,0},{4,2},{6,4},{7,6},{5,7},{3,5},{1,3},{0,1},{10,8},{12,10},{14... | collective-permute-start | bytes 1179656 | tf_op jit(solution)/shard_map/ppermute | solution.py:434
  3.1 1.3 %copy-start = (bf16[1024,640]{1,0:T(8,128)(2,1)S(1)}, bf16[1024,640]{1,0:T(8,128)(2,1)}, u32[]{:S(2)}) copy-start(bf16[1024,640]{1,0:T(8,128)(2,1)} %e_ref.1) | copy-start | bytes 3932164
  4.4 1.0 %copy-start.1 = (bf16[1024,192]{0,1:T(8,128)(2,1)S(1)}, bf16[1024,192]{0,1:T(8,128)(2,1)}, u32[]{:S(2)}) copy-start(bf16[1024,192]{0,1:T(8,128)(2,1)} %param.7) | copy-start | bytes 1179652
  5.4 0.9 %copy-start.2 = (bf16[1024,64]{0,1:T(8,128)(2,1)S(1)}, bf16[1024,64]{0,1:T(8,128)(2,1)}, u32[]{:S(2)}) copy-start(bf16[1024,64]{0,1:T(8,128)(2,1)} %param.8) | copy-start | bytes 393220
  8.7 7.2 %collective-permute-start = (f32[392,320]{1,0:T(8,128)S(1)}, f32[392,320]{1,0:T(8,128)S(1)}, u32[]{:S(2)}, u32[]{:S(2)}) collective-permute-start(f32[392,320]{1,0:T(8,128)S(1)} %get-tuple-element.32), channel_id=1, source_target_pairs={{0,8},{8,0},{16,24},{24,16},{1,9},{9,1},{17,25},{25,17},{2,10},{10... | collective-permute-start | bytes 1505288 | tf_op jit(solution)/shard_map/ppermute | solution.py:425
  13.8 9.7 %collective-permute-start.6 = (bf16[192,1024]{1,0:T(8,128)(2,1)S(1)}, bf16[192,1024]{1,0:T(8,128)(2,1)S(1)}, u32[]{:S(2)}, u32[]{:S(2)}) collective-permute-start(bf16[192,1024]{1,0:T(8,128)(2,1)S(1)} %get-tuple-element.37.rest_0_), channel_id=1, source_target_pairs={{0,2},{2,4},{4,6},{6,7},{7,5},{5,3},{3,1},{1,0},{8,10},{10,12},{12... | collective-permute-start | bytes 1179656 | tf_op jit(solution)/shard_map/ppermute | solution.py:431
  15.4 9.4 %collective-permute-start.7 = (bf16[192,1024]{1,0:T(8,128)(2,1)S(1)}, bf16[192,1024]{1,0:T(8,128)(2,1)S(1)}, u32[]{:S(2)}, u32[]{:S(2)}) collective-permute-start(bf16[192,1024]{1,0:T(8,128)(2,1)S(1)} %get-tuple-element.38.rest_1_), channel_id=1, source_target_pairs={{2,0},{4,2},{6,4},{7,6},{5,7},{3,5},{1,3},{0,1},{10,8},{12,10},{14... | collective-permute-start | bytes 1179656 | tf_op jit(solution)/shard_map/ppermute | solution.py:434
  15.9 8.8 %collective-permute-start.1 = (f32[584,128]{1,0:T(8,128)S(1)}, f32[584,128]{1,0:T(8,128)S(1)}, u32[]{:S(2)}, u32[]{:S(2)}) collective-permute-start(f32[584,128]{1,0:T(8,128)S(1)} %add_cores.5.rest_0_), channel_id=1, source_target_pairs={{0,16},{8,24},{16,0},{24,8},{1,17},{9,25},{17,1},{25,9},{2,18},{10... | collective-permute-start | bytes 897032 | tf_op jit(solution)/shard_map/ppermute | solution.py:425
  18.8 8.0 %collective-permute-start.4 = (f32[392,384]{1,0:T(8,128)S(1)}, f32[392,384]{1,0:T(8,128)S(1)}, u32[]{:S(2)}, u32[]{:S(2)}) collective-permute-start(f32[392,384]{1,0:T(8,128)S(1)} %get-tuple-element.40), channel_id=1, source_target_pairs={{0,8},{8,0},{16,24},{24,16},{1,9},{9,1},{17,25},{25,17},{2,10},{10... | collective-permute-start | bytes 1806344 | tf_op jit(solution)/shard_map/ppermute | solution.py:425
  24.8 8.6 %collective-permute-start.10 = (bf16[192,1024]{1,0:T(8,128)(2,1)S(1)}, bf16[192,1024]{1,0:T(8,128)(2,1)S(1)}, u32[]{:S(2)}, u32[]{:S(2)}) collective-permute-start(bf16[192,1024]{1,0:T(8,128)(2,1)S(1)} %get-tuple-element.42.rest_0_), channel_id=1, source_target_pairs={{0,2},{2,4},{4,6},{6,7},{7,5},{5,3},{3,1},{1,0},{8,10},{10,12},{12... | collective-permute-start | bytes 1179656 | tf_op jit(solution)/shard_map/ppermute | solution.py:431
  26.4 8.2 %collective-permute-start.11 = (bf16[192,1024]{1,0:T(8,128)(2,1)S(1)}, bf16[192,1024]{1,0:T(8,128)(2,1)S(1)}, u32[]{:S(2)}, u32[]{:S(2)}) collective-permute-start(bf16[192,1024]{1,0:T(8,128)(2,1)S(1)} %get-tuple-element.43.rest_1_), channel_id=1, source_target_pairs={{2,0},{4,2},{6,4},{7,6},{5,7},{3,5},{1,3},{0,1},{10,8},{12,10},{14... | collective-permute-start | bytes 1179656 | tf_op jit(solution)/shard_map/ppermute | solution.py:434
  26.9 7.7 %collective-permute-start.5 = (f32[232,384]{1,0:T(8,128)S(1)}, f32[232,384]{1,0:T(8,128)S(1)}, u32[]{:S(2)}, u32[]{:S(2)}) collective-permute-start(f32[232,384]{1,0:T(8,128)S(1)} %add_cores.6.rest_0_), channel_id=1, source_target_pairs={{0,16},{8,24},{16,0},{24,8},{1,17},{9,25},{17,1},{25,9},{2,18},{10... | collective-permute-start | bytes 1069064 | tf_op jit(solution)/shard_map/ppermute | solution.py:425
  29.7 7.0 %collective-permute-start.8 = (f32[392,384]{1,0:T(8,128)S(1)}, f32[392,384]{1,0:T(8,128)S(1)}, u32[]{:S(2)}, u32[]{:S(2)}) collective-permute-start(f32[392,384]{1,0:T(8,128)S(1)} %get-tuple-element.45), channel_id=1, source_target_pairs={{0,8},{8,0},{16,24},{24,16},{1,9},{9,1},{17,25},{25,17},{2,10},{10... | collective-permute-start | bytes 1806344 | tf_op jit(solution)/shard_map/ppermute | solution.py:425
  34.6 6.2 %collective-permute-start.14 = (bf16[96,1024]{1,0:T(8,128)(2,1)S(1)}, bf16[96,1024]{1,0:T(8,128)(2,1)S(1)}, u32[]{:S(2)}, u32[]{:S(2)}) collective-permute-start(bf16[96,1024]{1,0:T(8,128)(2,1)S(1)} %slice.6), channel_id=1, source_target_pairs={{0,2},{2,4},{4,6},{6,7},{7,5},{5,3},{3,1},{1,0},{8,10},{10,12},{12... | collective-permute-start | bytes 589832 | tf_op jit(solution)/shard_map/ppermute | solution.py:431
  36.2 6.0 %collective-permute-start.15 = (bf16[96,1024]{1,0:T(8,128)(2,1)S(1)}, bf16[96,1024]{1,0:T(8,128)(2,1)S(1)}, u32[]{:S(2)}, u32[]{:S(2)}) collective-permute-start(bf16[96,1024]{1,0:T(8,128)(2,1)S(1)} %slice.7), channel_id=1, source_target_pairs={{2,0},{4,2},{6,4},{7,6},{5,7},{3,5},{1,3},{0,1},{10,8},{12,10},{14... | collective-permute-start | bytes 589832 | tf_op jit(solution)/shard_map/ppermute | solution.py:434
  36.8 9.1 %collective-permute-start.9 = (f32[232,384]{1,0:T(8,128)S(1)}, f32[232,384]{1,0:T(8,128)S(1)}, u32[]{:S(2)}, u32[]{:S(2)}) collective-permute-start(f32[232,384]{1,0:T(8,128)S(1)} %add_cores.7.rest_0_.rest_2_), channel_id=1, source_target_pairs={{0,16},{8,24},{16,0},{24,8},{1,17},{9,25},{17,1},{25,9},{2,18},{10... | collective-permute-start | bytes 1069064 | tf_op jit(solution)/shard_map/ppermute | solution.py:425
  39.6 2.6 %collective-permute-start.12 = (f32[392,384]{1,0:T(8,128)S(1)}, f32[392,384]{1,0:T(8,128)S(1)}, u32[]{:S(2)}, u32[]{:S(2)}) collective-permute-start(f32[392,384]{1,0:T(8,128)S(1)} %get-tuple-element.50), channel_id=1, source_target_pairs={{0,8},{8,0},{16,24},{24,16},{1,9},{9,1},{17,25},{25,17},{2,10},{10... | collective-permute-start | bytes 1806344 | tf_op jit(solution)/shard_map/ppermute | solution.py:425
  42.2 4.4 %copy-start.3 = (s32[24,160]{1,0:T(8,128)S(1)}, s32[24,160]{1,0:T(8,128)}, u32[]{:S(2)}) copy-start(s32[24,160]{1,0:T(8,128)} %bins_ref.1) | copy-start | bytes 46084
  42.2 4.3 %copy-start.4 = (f32[5,16]{1,0:T(8,128)S(1)}, f32[5,16]{1,0:T(8,128)}, u32[]{:S(2)}) copy-start(f32[5,16]{1,0:T(8,128)} %weight_ref.1) | copy-start | bytes 964
  42.2 4.3 %copy-start.5 = (s32[160]{0:T(256)S(1)}, s32[160]{0:T(256)}, u32[]{:S(2)}) copy-start(s32[160]{0:T(256)} %param.10) | copy-start | bytes 1924
  43.0 2.9 %collective-permute-start.16 = (f32[392,192]{1,0:T(8,128)S(1)}, f32[392,192]{1,0:T(8,128)S(1)}, u32[]{:S(2)}, u32[]{:S(2)}) collective-permute-start(f32[392,192]{1,0:T(8,128)S(1)} %get-tuple-element.55), channel_id=1, source_target_pairs={{0,8},{8,0},{16,24},{24,16},{1,9},{9,1},{17,25},{25,17},{2,10},{10... | collective-permute-start | bytes 903176 | tf_op jit(solution)/shard_map/ppermute | solution.py:425
  43.1 11.2 %collective-permute-start.13 = (f32[232,384]{1,0:T(8,128)S(1)}, f32[232,384]{1,0:T(8,128)S(1)}, u32[]{:S(2)}, u32[]{:S(2)}) collective-permute-start(f32[232,384]{1,0:T(8,128)S(1)} %add_cores.8.rest_0_.rest_2_), channel_id=1, source_target_pairs={{0,16},{8,24},{16,0},{24,8},{1,17},{9,25},{17,1},{25,9},{2,18},{10... | collective-permute-start | bytes 1069064 | tf_op jit(solution)/shard_map/ppermute | solution.py:425
  46.0 11.7 %collective-permute-start.17 = (f32[352,128]{1,0:T(8,128)S(1)}, f32[352,128]{1,0:T(8,128)S(1)}, u32[]{:S(2)}, u32[]{:S(2)}) collective-permute-start(f32[352,128]{1,0:T(8,128)S(1)} %add_cores.9.rest_0_), channel_id=1, source_target_pairs={{0,16},{8,24},{16,0},{24,8},{1,17},{9,25},{17,1},{25,9},{2,18},{10... | collective-permute-start | bytes 540680 | tf_op jit(solution)/shard_map/ppermute | solution.py:425

commit v2 on v1

--- a/solution.py
+++ b/solution.py
@@ -442,7 +442,7 @@
         return [("came", 0) if k == 1 else ("got", 0) if k == 2 else ("sent", k - 1)]
 
     def turns(k):
-        return ([("got", k - 2)] if 1 < k < middle else []) + ([("solved", 0)] if k == middle - 1 else [])
+        return [("got", k - 2)] if 1 < k < middle else []
 
     def ends(k):
         return [("got", k - 2)] if k == middle else []
@@ -472,10 +472,8 @@
         if k == 0:
             solved, norm = solve(mine, came, swapped, covs, dof)
             scale = widen(fold_weights, norm, distance_bins, gene_folds[None], ring * variants)
-            done["solved", 0] = solved
         if k < middle:
             stats.append(chunk_stat(solved, mine, came, swapped, covs, LANES if k == 0 else 0))
-            done["stat", k] = stats[k]
             block = ahead
     placed = place(ids, scale, stats, ring, tuple(order))
     return finish(ids, solved, scale, placed, (mine, came, *swapped), covs, ring, tuple(order))

time: 60 us -> 59.8 us (level)
  waiting for transfers between devices: 22.9 us -> 21.4 us
  starting transfers between devices: 15.8 us -> 17.1 us
    ppermute x10, waiting for transfers between devices: 8.05 us -> 3.1 us  [exchange(): return lax.ppermute(x, 'samp', [(s, s ^ d) for s in range(parts)])]
    ppermute x4, waiting for transfers between devices: 9.52 us -> 12.5 us  [right(): return lax.ppermute(x, 'var', forward)]
    ppermute x10, starting transfers between devices: 6.61 us -> 7.85 us  [exchange(): return lax.ppermute(x, 'samp', [(s, s ^ d) for s in range(parts)])]
  transfers between devices with their start and end apart: 18 -> 18, of which waited for: 10 -> 11; matrix products, arithmetic and copies ran while one was open for 0% -> 0% of each run, Pallas kernels for 26% -> 26%
where the time goes in v2:
time: 59.8 us; the launch traced here: 59.6 us
  waiting for transfers between devices  21.4 us (36%)
  Pallas kernels  17.6 us (29%)
  starting transfers between devices  17.1 us (29%)
  local copies, waits for them, and re-layouts  3.26 us (5%)
    pallas_call x18, Pallas kernels, call(): pl.pallas_call(kernel, out_shape=out_shape, in_specs=[smem] * scalars + [...  17.6 us
    ppermute x4, waiting for transfers between devices, right(): return lax.ppermute(x, 'var', forward)  12.5 us
    ppermute x10, starting transfers between devices, exchange(): return lax.ppermute(x, 'samp', [(s, s ^ d) for s in range(parts)])  7.85 us
    ppermute x4, starting transfers between devices, right(): return lax.ppermute(x, 'var', forward)  7.85 us
    ppermute x4, waiting for transfers between devices, left(): return lax.ppermute(x, 'var', backward)  5.81 us
    unnamed x12, local copies, waits for them, and re-layouts  3.23 us
    ppermute x10, waiting for transfers between devices, exchange(): return lax.ppermute(x, 'samp', [(s, s ^ d) for s in range(parts)])  3.1 us
    ppermute x4, starting transfers between devices, left(): return lax.ppermute(x, 'var', backward)  1.36 us
  transfers between devices with their start and end apart: 18, of which 11 were waited for; matrix products, arithmetic and copies ran while one was open for 0% of the time, Pallas kernels for 26%

profile of v2, /device:TPU:0, one launch (start us, length us, event | category | flops | bytes accessed | tf_op | source)
XLA Modules:
  0.0 59.6 jit_solution(15811263000618454218)
XLA Ops:
  0.0 3.0 %collective-permute-start.2 = (bf16[192,1024]{1,0:T(8,128)(2,1)}, bf16[192,1024]{1,0:T(8,128)(2,1)S(1)}, u32[]{:S(2)}, u32[]{:S(2)}) collective-permute-start(bf16[192,1024]{1,0:T(8,128)(2,1)} %bitcast.5), channel_id=1, source_target_pairs={{0,2},{2,4},{4,6},{6,7},{7,5},{5,3},{3,1},{1,0},{8,10},{10,12},{12... | collective-permute-start | bytes 1179656 | tf_op jit(solution)/shard_map/ppermute | solution.py:431
  3.0 0.0 collective-permute-start.3
  3.0 0.1 pad_add_fusion.ids_ref
  3.1 0.0 copy-start
  3.1 1.3 %copy-done = bf16[1024,640]{1,0:T(8,128)(2,1)S(1)} copy-done((bf16[1024,640]{1,0:T(8,128)(2,1)S(1)}, bf16[1024,640]{1,0:T(8,128)(2,1)}, u32[]{:S(2)}) %copy-start) | copy-done | bytes 1310744
  4.4 0.0 copy-start.1
  4.4 1.0 %copy-done.1 = bf16[1024,192]{0,1:T(8,128)(2,1)S(1)} copy-done((bf16[1024,192]{0,1:T(8,128)(2,1)S(1)}, bf16[1024,192]{0,1:T(8,128)(2,1)}, u32[]{:S(2)}) %copy-start.1) | copy-done | bytes 393240
  5.4 0.9 %copy-done.2 = bf16[1024,64]{0,1:T(8,128)(2,1)S(1)} copy-done((bf16[1024,64]{0,1:T(8,128)(2,1)S(1)}, bf16[1024,64]{0,1:T(8,128)(2,1)}, u32[]{:S(2)}) %copy-start.2) | copy-done | bytes 131096
  6.3 2.4 %first_products.1 = (bf16[720,1024]{1,0:T(8,128)(2,1)S(1)}, f32[392,320]{1,0:T(8,128)S(1)}, f32[232,320]{1,0:T(8,128)S(1)}, f32[160,320]{1,0:T(8,128)S(1)}) custom-call(s32[2]{0:T(128)S(1)} %pad_add_fusion.ids_ref, bf16[1024,640]{1,0:T(8,128)(2,1)S(1)} %copy-done, bf16[192,1024]{1,0:T(8,128)(2,1)S(1)} %bitcast.7, bf16[64,1024]{1,0:T(8,128)(2,1)S(1)} %bitcast.8), custom_call_target="tpu_custom_call" | custom-call | flops 100000000 | tf_op jit(solution)/shard_map/first_products/pallas_call | solution.py:40
  8.7 0.0 collective-permute-start
  8.7 3.6 %collective-permute-done.2.refs_0_ = bf16[192,1024]{1,0:T(8,128)(2,1)S(1)} collective-permute-done((bf16[192,1024]{1,0:T(8,128)(2,1)}, bf16[192,1024]{1,0:T(8,128)(2,1)S(1)}, u32[]{:S(2)}, u32[]{:S(2)}) %collective-permute-start.2) | collective-permute-done | bytes 393248 | tf_op jit(solution)/shard_map/ppermute | solution.py:431
  12.3 1.5 %collective-permute-done.3.refs_1_ = bf16[192,1024]{1,0:T(8,128)(2,1)S(1)} collective-permute-done((bf16[192,1024]{1,0:T(8,128)(2,1)}, bf16[192,1024]{1,0:T(8,128)(2,1)S(1)}, u32[]{:S(2)}, u32[]{:S(2)}) %collective-permute-start.3) | collective-permute-done | bytes 393248 | tf_op jit(solution)/shard_map/ppermute | solution.py:434
  13.8 1.6 %collective-permute-start.6 = (bf16[192,1024]{1,0:T(8,128)(2,1)S(1)}, bf16[192,1024]{1,0:T(8,128)(2,1)S(1)}, u32[]{:S(2)}, u32[]{:S(2)}) collective-permute-start(bf16[192,1024]{1,0:T(8,128)(2,1)S(1)} %get-tuple-element.37.rest_0_), channel_id=1, source_target_pairs={{0,2},{2,4},{4,6},{6,7},{7,5},{5,3},{3,1},{1,0},{8,10},{10,12},{12... | collective-permute-start | bytes 1179656 | tf_op jit(solution)/shard_map/ppermute | solution.py:431
  15.4 0.4 collective-permute-start.7
  15.8 0.0 collective-permute-done.came_ref.rest_2_
  15.8 0.1 add_cores.5.rest_0_
  15.9 1.6 %collective-permute-start.1 = (f32[584,128]{1,0:T(8,128)S(1)}, f32[584,128]{1,0:T(8,128)S(1)}, u32[]{:S(2)}, u32[]{:S(2)}) collective-permute-start(f32[584,128]{1,0:T(8,128)S(1)} %add_cores.5.rest_0_), channel_id=1, source_target_pairs={{0,16},{8,24},{16,0},{24,8},{1,17},{9,25},{17,1},{25,9},{2,18},{10... | collective-permute-start | bytes 897032 | tf_op jit(solution)/shard_map/ppermute | solution.py:425
  17.5 1.3 %next_products.4 = (f32[392,384]{1,0:T(8,128)S(1)}, f32[232,384]{1,0:T(8,128)S(1)}, f32[160,384]{1,0:T(8,128)S(1)}) custom-call(bf16[720,1024]{1,0:T(8,128)(2,1)S(1)} %get-tuple-element.36.left_ref, bf16[192,1024]{1,0:T(8,128)(2,1)S(1)} %get-tuple-element.37.rest_0_, bf16[192,1024]{1,0:T(8,128)(2,1)S(1)} %get-tuple-element.38.rest_1_, ...), custom_call_target="tpu_custom_call" | custom-call | flops 100000000 | tf_op jit(solution)/shard_map/next_products/pallas_call | solution.py:40
  18.8 0.0 collective-permute-start.4
  18.8 4.7 %collective-permute-done.6.refs_0_ = bf16[192,1024]{1,0:T(8,128)(2,1)S(1)} collective-permute-done((bf16[192,1024]{1,0:T(8,128)(2,1)S(1)}, bf16[192,1024]{1,0:T(8,128)(2,1)S(1)}, u32[]{:S(2)}, u32[]{:S(2)}) %collective-permute-start.6) | collective-permute-done | bytes 393248 | tf_op jit(solution)/shard_map/ppermute | solution.py:431
  23.5 1.3 %collective-permute-done.7.refs_1_ = bf16[192,1024]{1,0:T(8,128)(2,1)S(1)} collective-permute-done((bf16[192,1024]{1,0:T(8,128)(2,1)S(1)}, bf16[192,1024]{1,0:T(8,128)(2,1)S(1)}, u32[]{:S(2)}, u32[]{:S(2)}) %collective-permute-start.7) | collective-permute-done | bytes 393248 | tf_op jit(solution)/shard_map/ppermute | solution.py:434
  24.8 0.0 collective-permute-done.1.rest_1_.refs_2_.rest_2_
  24.8 1.6 %collective-permute-start.10 = (bf16[192,1024]{1,0:T(8,128)(2,1)S(1)}, bf16[192,1024]{1,0:T(8,128)(2,1)S(1)}, u32[]{:S(2)}, u32[]{:S(2)}) collective-permute-start(bf16[192,1024]{1,0:T(8,128)(2,1)S(1)} %get-tuple-element.42.rest_0_), channel_id=1, source_target_pairs={{0,2},{2,4},{4,6},{6,7},{7,5},{5,3},{3,1},{1,0},{8,10},{10,12},{12... | collective-permute-start | bytes 1179656 | tf_op jit(solution)/shard_map/ppermute | solution.py:431
  26.4 0.4 collective-permute-start.11
  26.8 0.0 collective-permute-done.4.came_ref
  26.8 0.1 add_cores.6.rest_0_
  26.9 1.6 %collective-permute-start.5 = (f32[232,384]{1,0:T(8,128)S(1)}, f32[232,384]{1,0:T(8,128)S(1)}, u32[]{:S(2)}, u32[]{:S(2)}) collective-permute-start(f32[232,384]{1,0:T(8,128)S(1)} %add_cores.6.rest_0_), channel_id=1, source_target_pairs={{0,16},{8,24},{16,0},{24,8},{1,17},{9,25},{17,1},{25,9},{2,18},{10... | collective-permute-start | bytes 1069064 | tf_op jit(solution)/shard_map/ppermute | solution.py:425
  28.4 1.3 %next_products.5 = (f32[392,384]{1,0:T(8,128)S(1)}, f32[232,384]{1,0:T(8,128)S(1)}, f32[160,384]{1,0:T(8,128)S(1)}) custom-call(bf16[720,1024]{1,0:T(8,128)(2,1)S(1)} %get-tuple-element.36.left_ref, bf16[192,1024]{1,0:T(8,128)(2,1)S(1)} %get-tuple-element.42.rest_0_, bf16[192,1024]{1,0:T(8,128)(2,1)S(1)} %get-tuple-element.43.rest_1_, ...), custom_call_target="tpu_custom_call" | custom-call | flops 100000000 | tf_op jit(solution)/shard_map/next_products/pallas_call | solution.py:40
  29.7 0.0 collective-permute-start.8
  29.7 3.5 %collective-permute-done.10.refs_0_ = bf16[192,1024]{1,0:T(8,128)(2,1)S(1)} collective-permute-done((bf16[192,1024]{1,0:T(8,128)(2,1)S(1)}, bf16[192,1024]{1,0:T(8,128)(2,1)S(1)}, u32[]{:S(2)}, u32[]{:S(2)}) %collective-permute-start.10) | collective-permute-done | bytes 393248 | tf_op jit(solution)/shard_map/ppermute | solution.py:431
  33.2 1.3 %collective-permute-done.11.refs_1_ = bf16[192,1024]{1,0:T(8,128)(2,1)S(1)} collective-permute-done((bf16[192,1024]{1,0:T(8,128)(2,1)S(1)}, bf16[192,1024]{1,0:T(8,128)(2,1)S(1)}, u32[]{:S(2)}, u32[]{:S(2)}) %collective-permute-start.11) | collective-permute-done | bytes 393248 | tf_op jit(solution)/shard_map/ppermute | solution.py:434
  34.5 0.0 collective-permute-done.5.rest_1_.refs_2_
  34.6 1.7 %collective-permute-start.14 = (bf16[96,1024]{1,0:T(8,128)(2,1)S(1)}, bf16[96,1024]{1,0:T(8,128)(2,1)S(1)}, u32[]{:S(2)}, u32[]{:S(2)}) collective-permute-start(bf16[96,1024]{1,0:T(8,128)(2,1)S(1)} %slice.6), channel_id=1, source_target_pairs={{0,2},{2,4},{4,6},{6,7},{7,5},{5,3},{3,1},{1,0},{8,10},{10,12},{12... | collective-permute-start | bytes 589832 | tf_op jit(solution)/shard_map/ppermute | solution.py:431
  36.3 0.5 collective-permute-start.15
  36.7 0.0 collective-permute-done.8.came_ref
  36.8 1.6 %collective-permute-start.9 = (f32[232,384]{1,0:T(8,128)S(1)}, f32[232,384]{1,0:T(8,128)S(1)}, u32[]{:S(2)}, u32[]{:S(2)}) collective-permute-start(f32[232,384]{1,0:T(8,128)S(1)} %add_cores.7.rest_0_.rest_2_), channel_id=1, source_target_pairs={{0,16},{8,24},{16,0},{24,8},{1,17},{9,25},{17,1},{25,9},{2,18},{10... | collective-permute-start | bytes 1069064 | tf_op jit(solution)/shard_map/ppermute | solution.py:425
  38.3 1.3 %next_products.6 = (f32[392,384]{1,0:T(8,128)S(1)}, f32[232,384]{1,0:T(8,128)S(1)}, f32[160,384]{1,0:T(8,128)S(1)}) custom-call(bf16[720,1024]{1,0:T(8,128)(2,1)S(1)} %get-tuple-element.36.left_ref, bf16[192,1024]{1,0:T(8,128)(2,1)S(1)} %get-tuple-element.47.rest_0_, bf16[192,1024]{1,0:T(8,128)(2,1)S(1)} %get-tuple-element.48.rest_1_, ...), custom_call_target="tpu_custom_call" | custom-call | flops 100000000 | tf_op jit(solution)/shard_map/next_products/pallas_call | solution.py:40
  39.6 0.0 collective-permute-start.12
  39.6 0.7 %collective-permute-done.14.refs_0_ = bf16[96,1024]{1,0:T(8,128)(2,1)S(1)} collective-permute-done((bf16[96,1024]{1,0:T(8,128)(2,1)S(1)}, bf16[96,1024]{1,0:T(8,128)(2,1)S(1)}, u32[]{:S(2)}, u32[]{:S(2)}) %collective-permute-start.14) | collective-permute-done | bytes 196640 | tf_op jit(solution)/shard_map/ppermute | solution.py:431
  40.3 1.7 %collective-permute-done.15.refs_1_ = bf16[96,1024]{1,0:T(8,128)(2,1)S(1)} collective-permute-done((bf16[96,1024]{1,0:T(8,128)(2,1)S(1)}, bf16[96,1024]{1,0:T(8,128)(2,1)S(1)}, u32[]{:S(2)}, u32[]{:S(2)}) %collective-permute-start.15) | collective-permute-done | bytes 196640 | tf_op jit(solution)/shard_map/ppermute | solution.py:434
  42.0 0.0 collective-permute-done.12.came_ref
  42.0 0.8 %next_products.7 = (f32[392,192]{1,0:T(8,128)S(1)}, f32[232,192]{1,0:T(8,128)S(1)}, f32[160,192]{1,0:T(8,128)S(1)}) custom-call(bf16[720,1024]{1,0:T(8,128)(2,1)S(1)} %get-tuple-element.36.left_ref, bf16[96,1024]{1,0:T(8,128)(2,1)S(1)} %get-tuple-element.52.rest_0_, bf16[96,1024]{1,0:T(8,128)(2,1)S(1)} %get-tuple-element.53.rest_1_, ...), custom_call_target="tpu_custom_call" | custom-call | flops 100000000 | tf_op jit(solution)/shard_map/next_products/pallas_call | solution.py:40
  42.8 0.0 copy-start.3
  42.8 0.0 copy-start.4
  42.8 0.0 copy-start.5
  42.8 0.1 collective-permute-start.16
  42.9 1.6 %collective-permute-start.13 = (f32[232,384]{1,0:T(8,128)S(1)}, f32[232,384]{1,0:T(8,128)S(1)}, u32[]{:S(2)}, u32[]{:S(2)}) collective-permute-start(f32[232,384]{1,0:T(8,128)S(1)} %add_cores.8.rest_0_.rest_2_), channel_id=1, source_target_pairs={{0,16},{8,24},{16,0},{24,8},{1,17},{9,25},{17,1},{25,9},{2,18},{10... | collective-permute-start | bytes 1069064 | tf_op jit(solution)/shard_map/ppermute | solution.py:425
  44.5 0.0 collective-permute-done.9.rest_1_.rest_0_
  44.5 0.2 collective-permute-done.16.came_ref
  44.6 0.1 add_cores.9.rest_0_
  44.7 1.6 %collective-permute-start.17 = (f32[352,128]{1,0:T(8,128)S(1)}, f32[352,128]{1,0:T(8,128)S(1)}, u32[]{:S(2)}, u32[]{:S(2)}) collective-permute-start(f32[352,128]{1,0:T(8,128)S(1)} %add_cores.9.rest_0_), channel_id=1, source_target_pairs={{0,16},{8,24},{16,0},{24,8},{1,17},{9,25},{17,1},{25,9},{2,18},{10... | collective-permute-start | bytes 540680 | tf_op jit(solution)/shard_map/ppermute | solution.py:425
  46.3 3.6 %solve.1 = (f32[232,72]{1,0:T(8,128)S(1)}, f32[160,128]{1,0:T(8,128)S(1)}) custom-call(f32[160,320]{1,0:T(8,128)S(1)} %get-tuple-element.31.mine_ref, f32[392,320]{1,0:T(8,128)S(1)} %collective-permute-done.came_ref.rest_2_, f32[584,128]{1,0:T(8,128)S(1)} %add_cores.5.rest_0_, f32[584,128]{1,0:T(8,128)S(1)} %collective-permute-done.1.rest_1_.refs_2_.rest_2_), custom_call_target="tpu_custom_call" | custom-call | flops 100000000 | tf_op jit(solution)/shard_map/solve/pallas_call | solution.py:40
  49.9 0.0 copy-done.3
  49.9 0.0 copy-done.4
  50.0 0.0 copy-done.5
  50.0 1.4 %widen.1.scale_ref = f32[160,1536]{1,0:T(8,128)S(1)} custom-call(f32[5,16]{1,0:T(8,128)S(1)} %copy-done.4, f32[160,128]{1,0:T(8,128)S(1)} %get-tuple-element.35.norm_ref, s32[24,160]{1,0:T(8,128)S(1)} %copy-done.3, s32[1,160]{1,0:T(1,128)S(1)} %bitcast.9), custom_call_target="tpu_custom_call" | custom-call | flops 1 | tf_op jit(solution)/shard_map/widen/pallas_call | solution.py:40
  51.4 0.5 chunk_stat.4.rest_0_
  51.8 0.6 chunk_stat.5.rest_1_
  52.4 0.6 chunk_stat.6.rest_2_
  53.0 1.1 %collective-permute-done.13.rest_1_ = f32[232,384]{1,0:T(8,128)S(1)} collective-permute-done((f32[232,384]{1,0:T(8,128)S(1)}, f32[232,384]{1,0:T(8,128)S(1)}, u32[]{:S(2)}, u32[]{:S(2)}) %collective-permute-start.13) | collective-permute-done | bytes 356384 | tf_op jit(solution)/shard_map/ppermute | solution.py:425
  54.1 0.6 chunk_stat.7.rest_3_
  54.7 1.0 %place.1.placed_ref = f32[160,1536]{1,0:T(8,128)S(1)} custom-call(s32[2]{0:T(128)S(1)} %pad_add_fusion.ids_ref, f32[160,1536]{1,0:T(8,128)S(1)} %widen.1.scale_ref, f32[160,192]{1,0:T(8,128)S(1)} %chunk_stat.4.rest_0_, f32[160,384]{1,0:T(8,128)S(1)} %chunk_stat.5.rest_1_, f32[160,384]{1,0:T(8,128)S(1)} %chunk_stat.6.rest_2_, f32[160,384]{1,0:T(8,128)S(1)} %chunk_stat.7.rest_3_), custom_call_target="tpu_custom_call" | custom-call | flops 1 | tf_op jit(solution)/shard_map/place/pallas_call | solution.py:40
  55.7 1.8 %collective-permute-done.17.rest_1_ = f32[352,128]{1,0:T(8,128)S(1)} collective-permute-done((f32[352,128]{1,0:T(8,128)S(1)}, f32[352,128]{1,0:T(8,128)S(1)}, u32[]{:S(2)}, u32[]{:S(2)}) %collective-permute-start.17) | collective-permute-done | bytes 180256 | tf_op jit(solution)/shard_map/ppermute | solution.py:425
  57.5 2.1 %finish.1 = f32[160,1536]{1,0:T(8,128)} custom-call(s32[2]{0:T(128)S(1)} %pad_add_fusion.ids_ref, f32[232,72]{1,0:T(8,128)S(1)} %get-tuple-element.34.solved_ref, f32[160,1536]{1,0:T(8,128)S(1)} %widen.1.scale_ref, f32[160,1536]{1,0:T(8,128)S(1)} %place.1.placed_ref, f32[160,192]{1,0:T(8,128)S(1)} %get-tuple-element.54.mine_ref, ...), custom_call_target="tpu_custom_call" | custom-call | flops 1 | tf_op jit(solution)/shard_map/finish/pallas_call | solution.py:40
  (9 shorter events, 0.1 us)
Async XLA Ops:
  0.0 12.3 %collective-permute-start.2 = (bf16[192,1024]{1,0:T(8,128)(2,1)}, bf16[192,1024]{1,0:T(8,128)(2,1)S(1)}, u32[]{:S(2)}, u32[]{:S(2)}) collective-permute-start(bf16[192,1024]{1,0:T(8,128)(2,1)} %bitcast.5), channel_id=1, source_target_pairs={{0,2},{2,4},{4,6},{6,7},{7,5},{5,3},{3,1},{1,0},{8,10},{10,12},{12... | collective-permute-start | bytes 1179656 | tf_op jit(solution)/shard_map/ppermute | solution.py:431
  3.0 10.8 %collective-permute-start.3 = (bf16[192,1024]{1,0:T(8,128)(2,1)}, bf16[192,1024]{1,0:T(8,128)(2,1)S(1)}, u32[]{:S(2)}, u32[]{:S(2)}) collective-permute-start(bf16[192,1024]{1,0:T(8,128)(2,1)} %bitcast.6), channel_id=1, source_target_pairs={{2,0},{4,2},{6,4},{7,6},{5,7},{3,5},{1,3},{0,1},{10,8},{12,10},{14... | collective-permute-start | bytes 1179656 | tf_op jit(solution)/shard_map/ppermute | solution.py:434
  3.1 1.3 %copy-start = (bf16[1024,640]{1,0:T(8,128)(2,1)S(1)}, bf16[1024,640]{1,0:T(8,128)(2,1)}, u32[]{:S(2)}) copy-start(bf16[1024,640]{1,0:T(8,128)(2,1)} %e_ref.1) | copy-start | bytes 3932164
  4.4 1.0 %copy-start.1 = (bf16[1024,192]{0,1:T(8,128)(2,1)S(1)}, bf16[1024,192]{0,1:T(8,128)(2,1)}, u32[]{:S(2)}) copy-start(bf16[1024,192]{0,1:T(8,128)(2,1)} %param.7) | copy-start | bytes 1179652
  5.4 0.9 %copy-start.2 = (bf16[1024,64]{0,1:T(8,128)(2,1)S(1)}, bf16[1024,64]{0,1:T(8,128)(2,1)}, u32[]{:S(2)}) copy-start(bf16[1024,64]{0,1:T(8,128)(2,1)} %param.8) | copy-start | bytes 393220
  8.7 7.2 %collective-permute-start = (f32[392,320]{1,0:T(8,128)S(1)}, f32[392,320]{1,0:T(8,128)S(1)}, u32[]{:S(2)}, u32[]{:S(2)}) collective-permute-start(f32[392,320]{1,0:T(8,128)S(1)} %get-tuple-element.32), channel_id=1, source_target_pairs={{0,8},{8,0},{16,24},{24,16},{1,9},{9,1},{17,25},{25,17},{2,10},{10... | collective-permute-start | bytes 1505288 | tf_op jit(solution)/shard_map/ppermute | solution.py:425
  13.8 9.7 %collective-permute-start.6 = (bf16[192,1024]{1,0:T(8,128)(2,1)S(1)}, bf16[192,1024]{1,0:T(8,128)(2,1)S(1)}, u32[]{:S(2)}, u32[]{:S(2)}) collective-permute-start(bf16[192,1024]{1,0:T(8,128)(2,1)S(1)} %get-tuple-element.37.rest_0_), channel_id=1, source_target_pairs={{0,2},{2,4},{4,6},{6,7},{7,5},{5,3},{3,1},{1,0},{8,10},{10,12},{12... | collective-permute-start | bytes 1179656 | tf_op jit(solution)/shard_map/ppermute | solution.py:431
  15.4 9.4 %collective-permute-start.7 = (bf16[192,1024]{1,0:T(8,128)(2,1)S(1)}, bf16[192,1024]{1,0:T(8,128)(2,1)S(1)}, u32[]{:S(2)}, u32[]{:S(2)}) collective-permute-start(bf16[192,1024]{1,0:T(8,128)(2,1)S(1)} %get-tuple-element.38.rest_1_), channel_id=1, source_target_pairs={{2,0},{4,2},{6,4},{7,6},{5,7},{3,5},{1,3},{0,1},{10,8},{12,10},{14... | collective-permute-start | bytes 1179656 | tf_op jit(solution)/shard_map/ppermute | solution.py:434
  15.9 8.8 %collective-permute-start.1 = (f32[584,128]{1,0:T(8,128)S(1)}, f32[584,128]{1,0:T(8,128)S(1)}, u32[]{:S(2)}, u32[]{:S(2)}) collective-permute-start(f32[584,128]{1,0:T(8,128)S(1)} %add_cores.5.rest_0_), channel_id=1, source_target_pairs={{0,16},{8,24},{16,0},{24,8},{1,17},{9,25},{17,1},{25,9},{2,18},{10... | collective-permute-start | bytes 897032 | tf_op jit(solution)/shard_map/ppermute | solution.py:425
  18.8 8.0 %collective-permute-start.4 = (f32[392,384]{1,0:T(8,128)S(1)}, f32[392,384]{1,0:T(8,128)S(1)}, u32[]{:S(2)}, u32[]{:S(2)}) collective-permute-start(f32[392,384]{1,0:T(8,128)S(1)} %get-tuple-element.40), channel_id=1, source_target_pairs={{0,8},{8,0},{16,24},{24,16},{1,9},{9,1},{17,25},{25,17},{2,10},{10... | collective-permute-start | bytes 1806344 | tf_op jit(solution)/shard_map/ppermute | solution.py:425
  24.8 8.5 %collective-permute-start.10 = (bf16[192,1024]{1,0:T(8,128)(2,1)S(1)}, bf16[192,1024]{1,0:T(8,128)(2,1)S(1)}, u32[]{:S(2)}, u32[]{:S(2)}) collective-permute-start(bf16[192,1024]{1,0:T(8,128)(2,1)S(1)} %get-tuple-element.42.rest_0_), channel_id=1, source_target_pairs={{0,2},{2,4},{4,6},{6,7},{7,5},{5,3},{3,1},{1,0},{8,10},{10,12},{12... | collective-permute-start | bytes 1179656 | tf_op jit(solution)/shard_map/ppermute | solution.py:431
  26.4 8.2 %collective-permute-start.11 = (bf16[192,1024]{1,0:T(8,128)(2,1)S(1)}, bf16[192,1024]{1,0:T(8,128)(2,1)S(1)}, u32[]{:S(2)}, u32[]{:S(2)}) collective-permute-start(bf16[192,1024]{1,0:T(8,128)(2,1)S(1)} %get-tuple-element.43.rest_1_), channel_id=1, source_target_pairs={{2,0},{4,2},{6,4},{7,6},{5,7},{3,5},{1,3},{0,1},{10,8},{12,10},{14... | collective-permute-start | bytes 1179656 | tf_op jit(solution)/shard_map/ppermute | solution.py:434
  26.9 7.7 %collective-permute-start.5 = (f32[232,384]{1,0:T(8,128)S(1)}, f32[232,384]{1,0:T(8,128)S(1)}, u32[]{:S(2)}, u32[]{:S(2)}) collective-permute-start(f32[232,384]{1,0:T(8,128)S(1)} %add_cores.6.rest_0_), channel_id=1, source_target_pairs={{0,16},{8,24},{16,0},{24,8},{1,17},{9,25},{17,1},{25,9},{2,18},{10... | collective-permute-start | bytes 1069064 | tf_op jit(solution)/shard_map/ppermute | solution.py:425
  29.7 7.0 %collective-permute-start.8 = (f32[392,384]{1,0:T(8,128)S(1)}, f32[392,384]{1,0:T(8,128)S(1)}, u32[]{:S(2)}, u32[]{:S(2)}) collective-permute-start(f32[392,384]{1,0:T(8,128)S(1)} %get-tuple-element.45), channel_id=1, source_target_pairs={{0,8},{8,0},{16,24},{24,16},{1,9},{9,1},{17,25},{25,17},{2,10},{10... | collective-permute-start | bytes 1806344 | tf_op jit(solution)/shard_map/ppermute | solution.py:425
  34.6 5.7 %collective-permute-start.14 = (bf16[96,1024]{1,0:T(8,128)(2,1)S(1)}, bf16[96,1024]{1,0:T(8,128)(2,1)S(1)}, u32[]{:S(2)}, u32[]{:S(2)}) collective-permute-start(bf16[96,1024]{1,0:T(8,128)(2,1)S(1)} %slice.6), channel_id=1, source_target_pairs={{0,2},{2,4},{4,6},{6,7},{7,5},{5,3},{3,1},{1,0},{8,10},{10,12},{12... | collective-permute-start | bytes 589832 | tf_op jit(solution)/shard_map/ppermute | solution.py:431
  36.3 5.7 %collective-permute-start.15 = (bf16[96,1024]{1,0:T(8,128)(2,1)S(1)}, bf16[96,1024]{1,0:T(8,128)(2,1)S(1)}, u32[]{:S(2)}, u32[]{:S(2)}) collective-permute-start(bf16[96,1024]{1,0:T(8,128)(2,1)S(1)} %slice.7), channel_id=1, source_target_pairs={{2,0},{4,2},{6,4},{7,6},{5,7},{3,5},{1,3},{0,1},{10,8},{12,10},{14... | collective-permute-start | bytes 589832 | tf_op jit(solution)/shard_map/ppermute | solution.py:434
  36.8 7.7 %collective-permute-start.9 = (f32[232,384]{1,0:T(8,128)S(1)}, f32[232,384]{1,0:T(8,128)S(1)}, u32[]{:S(2)}, u32[]{:S(2)}) collective-permute-start(f32[232,384]{1,0:T(8,128)S(1)} %add_cores.7.rest_0_.rest_2_), channel_id=1, source_target_pairs={{0,16},{8,24},{16,0},{24,8},{1,17},{9,25},{17,1},{25,9},{2,18},{10... | collective-permute-start | bytes 1069064 | tf_op jit(solution)/shard_map/ppermute | solution.py:425
  39.6 2.4 %collective-permute-start.12 = (f32[392,384]{1,0:T(8,128)S(1)}, f32[392,384]{1,0:T(8,128)S(1)}, u32[]{:S(2)}, u32[]{:S(2)}) collective-permute-start(f32[392,384]{1,0:T(8,128)S(1)} %get-tuple-element.50), channel_id=1, source_target_pairs={{0,8},{8,0},{16,24},{24,16},{1,9},{9,1},{17,25},{25,17},{2,10},{10... | collective-permute-start | bytes 1806344 | tf_op jit(solution)/shard_map/ppermute | solution.py:425
  42.8 7.1 %copy-start.3 = (s32[24,160]{1,0:T(8,128)S(1)}, s32[24,160]{1,0:T(8,128)}, u32[]{:S(2)}) copy-start(s32[24,160]{1,0:T(8,128)} %bins_ref.1) | copy-start | bytes 46084
  42.8 7.1 %copy-start.4 = (f32[5,16]{1,0:T(8,128)S(1)}, f32[5,16]{1,0:T(8,128)}, u32[]{:S(2)}) copy-start(f32[5,16]{1,0:T(8,128)} %weight_ref.1) | copy-start | bytes 964
  42.8 7.1 %copy-start.5 = (s32[160]{0:T(256)S(1)}, s32[160]{0:T(256)}, u32[]{:S(2)}) copy-start(s32[160]{0:T(256)} %param.10) | copy-start | bytes 1924
  42.8 1.8 %collective-permute-start.16 = (f32[392,192]{1,0:T(8,128)S(1)}, f32[392,192]{1,0:T(8,128)S(1)}, u32[]{:S(2)}, u32[]{:S(2)}) collective-permute-start(f32[392,192]{1,0:T(8,128)S(1)} %get-tuple-element.55), channel_id=1, source_target_pairs={{0,8},{8,0},{16,24},{24,16},{1,9},{9,1},{17,25},{25,17},{2,10},{10... | collective-permute-start | bytes 903176 | tf_op jit(solution)/shard_map/ppermute | solution.py:425
  42.9 11.2 %collective-permute-start.13 = (f32[232,384]{1,0:T(8,128)S(1)}, f32[232,384]{1,0:T(8,128)S(1)}, u32[]{:S(2)}, u32[]{:S(2)}) collective-permute-start(f32[232,384]{1,0:T(8,128)S(1)} %add_cores.8.rest_0_.rest_2_), channel_id=1, source_target_pairs={{0,16},{8,24},{16,0},{24,8},{1,17},{9,25},{17,1},{25,9},{2,18},{10... | collective-permute-start | bytes 1069064 | tf_op jit(solution)/shard_map/ppermute | solution.py:425
  44.7 12.8 %collective-permute-start.17 = (f32[352,128]{1,0:T(8,128)S(1)}, f32[352,128]{1,0:T(8,128)S(1)}, u32[]{:S(2)}, u32[]{:S(2)}) collective-permute-start(f32[352,128]{1,0:T(8,128)S(1)} %add_cores.9.rest_0_), channel_id=1, source_target_pairs={{0,16},{8,24},{16,0},{24,8},{1,17},{9,25},{17,1},{25,9},{2,18},{10... | collective-permute-start | bytes 540680 | tf_op jit(solution)/shard_map/ppermute | solution.py:425

commit v3 on v2

--- a/solution.py
+++ b/solution.py
@@ -382,12 +382,13 @@
 
 
 def finish_kernel(covs, ring, order, ids_ref, solved_ref, scale_ref, placed_ref, mine_ref, came_ref, *rest):
-    out_ref = rest[-1]
+    out_ref, last, sems = rest[-3:]
+    whole = pltpu.make_async_copy(placed_ref, out_ref, sems.at[0])
+    whole.start()
     variants = mine_ref.shape[1]
     group = LANES // math.gcd(variants, LANES)
     width = group * variants
-    stat = fitted_stat(covs, 0, solved_ref, mine_ref, came_ref, rest[:-1])
-    out_ref[...] = placed_ref[...]
+    stat = fitted_stat(covs, 0, solved_ref, mine_ref, came_ref, rest[:-3])
     index = jnp.int32(0)
     for block in range(ring):
         index = jnp.where(slot_of(block, ids_ref[1], ring, order) == ring // 2, block, index)
@@ -396,17 +397,28 @@
     lane = lax.broadcasted_iota(jnp.int32, stat.shape, 1)
     first = lax.rem(index, group) * variants
     inside = jnp.logical_and(lane >= first, lane < first + variants)
-    out_ref[:, span] = jnp.where(inside, stat * scale_ref[:, span], placed_ref[:, span])
+    last[...] = jnp.where(inside, stat * scale_ref[:, span], placed_ref[:, span])
+    whole.wait()
+    part = pltpu.make_async_copy(last, out_ref.at[:, span], sems.at[1])
+    part.start()
+    part.wait()
 
 
 def finish(ids, solved, scale, placed, last, covs, ring, order):
-    return call(
+    genes, total = scale.shape
+    variants = total // ring
+    width = LANES // math.gcd(variants, LANES) * variants
+    vmem = pl.BlockSpec(memory_space=pltpu.VMEM)
+    return pl.pallas_call(
         functools.partial(finish_kernel, covs, ring, order),
-        jax.ShapeDtypeStruct(scale.shape, jnp.float32),
-        "finish",
-        COST["finish"],
-        (ids, solved, scale, placed, *last),
-    )
+        out_shape=jax.ShapeDtypeStruct(scale.shape, jnp.float32),
+        in_specs=[pl.BlockSpec(memory_space=pltpu.SMEM)] + [vmem] * (3 + len(last)),
+        out_specs=pl.BlockSpec(memory_space=pl.ANY),
+        scratch_shapes=[pltpu.VMEM((genes, width), jnp.float32), pltpu.SemaphoreType.DMA((2,))],
+        compiler_params=pltpu.CompilerParams(vmem_limit_bytes=VMEM_LIMIT),
+        cost_estimate=pl.CostEstimate(flops=COST["finish"], bytes_accessed=0, transcendentals=0),
+        name="finish",
+    )(ids, solved, scale, placed, *last)
 
 
 def shards(order, expression, genotypes, covariates, distance_bins, gene_folds, fold_weights):

time: 59.8 us -> 59.9 us (level)
    pallas_call x0 -> x1, Pallas kernels: none -> 2.19 us  [finish(): pl.pallas_call(functools.partial(finish_kernel, covs, ring, order), out_s...]
    pallas_call x18 -> x17, Pallas kernels: 17.6 us -> 15.5 us  [call(): pl.pallas_call(kernel, out_shape=out_shape, in_specs=[smem] * scalars + [...]
where the time goes in v3:
time: 59.9 us; the launch traced here: 59.7 us
  waiting for transfers between devices  21.4 us (36%)
  Pallas kernels  17.7 us (30%)
  starting transfers between devices  17.1 us (29%)
  local copies, waits for them, and re-layouts  3.26 us (5%)
    pallas_call x17, Pallas kernels, call(): pl.pallas_call(kernel, out_shape=out_shape, in_specs=[smem] * scalars + [...  15.5 us
    ppermute x4, waiting for transfers between devices, right(): return lax.ppermute(x, 'var', forward)  12.5 us
    ppermute x10, starting transfers between devices, exchange(): return lax.ppermute(x, 'samp', [(s, s ^ d) for s in range(parts)])  7.85 us
    ppermute x4, starting transfers between devices, right(): return lax.ppermute(x, 'var', forward)  7.85 us
    ppermute x4, waiting for transfers between devices, left(): return lax.ppermute(x, 'var', backward)  5.81 us
    unnamed x12, local copies, waits for them, and re-layouts  3.23 us
    ppermute x10, waiting for transfers between devices, exchange(): return lax.ppermute(x, 'samp', [(s, s ^ d) for s in range(parts)])  3.1 us
    pallas_call x1, Pallas kernels, finish(): pl.pallas_call(functools.partial(finish_kernel, covs, ring, order), out_s...  2.19 us
  transfers between devices with their start and end apart: 18, of which 11 were waited for; matrix products, arithmetic and copies ran while one was open for 0% of the time, Pallas kernels for 26%

profile of v3, /device:TPU:0, one launch (start us, length us, event | category | flops | bytes accessed | tf_op | source)
XLA Modules:
  0.0 59.7 jit_solution(9944796570534112017)
XLA Ops:
  0.0 3.0 %collective-permute-start.2 = (bf16[192,1024]{1,0:T(8,128)(2,1)}, bf16[192,1024]{1,0:T(8,128)(2,1)S(1)}, u32[]{:S(2)}, u32[]{:S(2)}) collective-permute-start(bf16[192,1024]{1,0:T(8,128)(2,1)} %bitcast.5), channel_id=1, source_target_pairs={{0,2},{2,4},{4,6},{6,7},{7,5},{5,3},{3,1},{1,0},{8,10},{10,12},{12... | collective-permute-start | bytes 1179656 | tf_op jit(solution)/shard_map/ppermute | solution.py:443
  3.0 0.0 collective-permute-start.3
  3.0 0.1 pad_add_fusion.ids_ref
  3.1 0.0 copy-start
  3.1 1.3 %copy-done = bf16[1024,640]{1,0:T(8,128)(2,1)S(1)} copy-done((bf16[1024,640]{1,0:T(8,128)(2,1)S(1)}, bf16[1024,640]{1,0:T(8,128)(2,1)}, u32[]{:S(2)}) %copy-start) | copy-done | bytes 1310744
  4.4 0.0 copy-start.1
  4.4 1.0 %copy-done.1 = bf16[1024,192]{0,1:T(8,128)(2,1)S(1)} copy-done((bf16[1024,192]{0,1:T(8,128)(2,1)S(1)}, bf16[1024,192]{0,1:T(8,128)(2,1)}, u32[]{:S(2)}) %copy-start.1) | copy-done | bytes 393240
  5.4 0.9 %copy-done.2 = bf16[1024,64]{0,1:T(8,128)(2,1)S(1)} copy-done((bf16[1024,64]{0,1:T(8,128)(2,1)S(1)}, bf16[1024,64]{0,1:T(8,128)(2,1)}, u32[]{:S(2)}) %copy-start.2) | copy-done | bytes 131096
  6.3 2.4 %first_products.1 = (bf16[720,1024]{1,0:T(8,128)(2,1)S(1)}, f32[392,320]{1,0:T(8,128)S(1)}, f32[232,320]{1,0:T(8,128)S(1)}, f32[160,320]{1,0:T(8,128)S(1)}) custom-call(s32[2]{0:T(128)S(1)} %pad_add_fusion.ids_ref, bf16[1024,640]{1,0:T(8,128)(2,1)S(1)} %copy-done, bf16[192,1024]{1,0:T(8,128)(2,1)S(1)} %bitcast.7, bf16[64,1024]{1,0:T(8,128)(2,1)S(1)} %bitcast.8), custom_call_target="tpu_custom_call" | custom-call | flops 100000000 | tf_op jit(solution)/shard_map/first_products/pallas_call | solution.py:40
  8.7 0.0 collective-permute-start
  8.7 3.6 %collective-permute-done.2.refs_0_ = bf16[192,1024]{1,0:T(8,128)(2,1)S(1)} collective-permute-done((bf16[192,1024]{1,0:T(8,128)(2,1)}, bf16[192,1024]{1,0:T(8,128)(2,1)S(1)}, u32[]{:S(2)}, u32[]{:S(2)}) %collective-permute-start.2) | collective-permute-done | bytes 393248 | tf_op jit(solution)/shard_map/ppermute | solution.py:443
  12.3 1.5 %collective-permute-done.3.refs_1_ = bf16[192,1024]{1,0:T(8,128)(2,1)S(1)} collective-permute-done((bf16[192,1024]{1,0:T(8,128)(2,1)}, bf16[192,1024]{1,0:T(8,128)(2,1)S(1)}, u32[]{:S(2)}, u32[]{:S(2)}) %collective-permute-start.3) | collective-permute-done | bytes 393248 | tf_op jit(solution)/shard_map/ppermute | solution.py:446
  13.8 1.6 %collective-permute-start.6 = (bf16[192,1024]{1,0:T(8,128)(2,1)S(1)}, bf16[192,1024]{1,0:T(8,128)(2,1)S(1)}, u32[]{:S(2)}, u32[]{:S(2)}) collective-permute-start(bf16[192,1024]{1,0:T(8,128)(2,1)S(1)} %get-tuple-element.37.rest_0_), channel_id=1, source_target_pairs={{0,2},{2,4},{4,6},{6,7},{7,5},{5,3},{3,1},{1,0},{8,10},{10,12},{12... | collective-permute-start | bytes 1179656 | tf_op jit(solution)/shard_map/ppermute | solution.py:443
  15.4 0.4 collective-permute-start.7
  15.8 0.0 collective-permute-done.came_ref.rest_2_
  15.8 0.1 add_cores.5.rest_0_
  15.9 1.6 %collective-permute-start.1 = (f32[584,128]{1,0:T(8,128)S(1)}, f32[584,128]{1,0:T(8,128)S(1)}, u32[]{:S(2)}, u32[]{:S(2)}) collective-permute-start(f32[584,128]{1,0:T(8,128)S(1)} %add_cores.5.rest_0_), channel_id=1, source_target_pairs={{0,16},{8,24},{16,0},{24,8},{1,17},{9,25},{17,1},{25,9},{2,18},{10... | collective-permute-start | bytes 897032 | tf_op jit(solution)/shard_map/ppermute | solution.py:437
  17.5 1.3 %next_products.4 = (f32[392,384]{1,0:T(8,128)S(1)}, f32[232,384]{1,0:T(8,128)S(1)}, f32[160,384]{1,0:T(8,128)S(1)}) custom-call(bf16[720,1024]{1,0:T(8,128)(2,1)S(1)} %get-tuple-element.36.left_ref, bf16[192,1024]{1,0:T(8,128)(2,1)S(1)} %get-tuple-element.37.rest_0_, bf16[192,1024]{1,0:T(8,128)(2,1)S(1)} %get-tuple-element.38.rest_1_, ...), custom_call_target="tpu_custom_call" | custom-call | flops 100000000 | tf_op jit(solution)/shard_map/next_products/pallas_call | solution.py:40
  18.8 0.0 collective-permute-start.4
  18.8 4.7 %collective-permute-done.6.refs_0_ = bf16[192,1024]{1,0:T(8,128)(2,1)S(1)} collective-permute-done((bf16[192,1024]{1,0:T(8,128)(2,1)S(1)}, bf16[192,1024]{1,0:T(8,128)(2,1)S(1)}, u32[]{:S(2)}, u32[]{:S(2)}) %collective-permute-start.6) | collective-permute-done | bytes 393248 | tf_op jit(solution)/shard_map/ppermute | solution.py:443
  23.5 1.3 %collective-permute-done.7.refs_1_ = bf16[192,1024]{1,0:T(8,128)(2,1)S(1)} collective-permute-done((bf16[192,1024]{1,0:T(8,128)(2,1)S(1)}, bf16[192,1024]{1,0:T(8,128)(2,1)S(1)}, u32[]{:S(2)}, u32[]{:S(2)}) %collective-permute-start.7) | collective-permute-done | bytes 393248 | tf_op jit(solution)/shard_map/ppermute | solution.py:446
  24.8 0.0 collective-permute-done.1.rest_1_.refs_2_.rest_2_
  24.8 1.6 %collective-permute-start.10 = (bf16[192,1024]{1,0:T(8,128)(2,1)S(1)}, bf16[192,1024]{1,0:T(8,128)(2,1)S(1)}, u32[]{:S(2)}, u32[]{:S(2)}) collective-permute-start(bf16[192,1024]{1,0:T(8,128)(2,1)S(1)} %get-tuple-element.42.rest_0_), channel_id=1, source_target_pairs={{0,2},{2,4},{4,6},{6,7},{7,5},{5,3},{3,1},{1,0},{8,10},{10,12},{12... | collective-permute-start | bytes 1179656 | tf_op jit(solution)/shard_map/ppermute | solution.py:443
  26.4 0.4 collective-permute-start.11
  26.8 0.0 collective-permute-done.4.came_ref
  26.8 0.1 add_cores.6.rest_0_
  26.9 1.6 %collective-permute-start.5 = (f32[232,384]{1,0:T(8,128)S(1)}, f32[232,384]{1,0:T(8,128)S(1)}, u32[]{:S(2)}, u32[]{:S(2)}) collective-permute-start(f32[232,384]{1,0:T(8,128)S(1)} %add_cores.6.rest_0_), channel_id=1, source_target_pairs={{0,16},{8,24},{16,0},{24,8},{1,17},{9,25},{17,1},{25,9},{2,18},{10... | collective-permute-start | bytes 1069064 | tf_op jit(solution)/shard_map/ppermute | solution.py:437
  28.4 1.3 %next_products.5 = (f32[392,384]{1,0:T(8,128)S(1)}, f32[232,384]{1,0:T(8,128)S(1)}, f32[160,384]{1,0:T(8,128)S(1)}) custom-call(bf16[720,1024]{1,0:T(8,128)(2,1)S(1)} %get-tuple-element.36.left_ref, bf16[192,1024]{1,0:T(8,128)(2,1)S(1)} %get-tuple-element.42.rest_0_, bf16[192,1024]{1,0:T(8,128)(2,1)S(1)} %get-tuple-element.43.rest_1_, ...), custom_call_target="tpu_custom_call" | custom-call | flops 100000000 | tf_op jit(solution)/shard_map/next_products/pallas_call | solution.py:40
  29.7 0.0 collective-permute-start.8
  29.7 3.5 %collective-permute-done.10.refs_0_ = bf16[192,1024]{1,0:T(8,128)(2,1)S(1)} collective-permute-done((bf16[192,1024]{1,0:T(8,128)(2,1)S(1)}, bf16[192,1024]{1,0:T(8,128)(2,1)S(1)}, u32[]{:S(2)}, u32[]{:S(2)}) %collective-permute-start.10) | collective-permute-done | bytes 393248 | tf_op jit(solution)/shard_map/ppermute | solution.py:443
  33.2 1.3 %collective-permute-done.11.refs_1_ = bf16[192,1024]{1,0:T(8,128)(2,1)S(1)} collective-permute-done((bf16[192,1024]{1,0:T(8,128)(2,1)S(1)}, bf16[192,1024]{1,0:T(8,128)(2,1)S(1)}, u32[]{:S(2)}, u32[]{:S(2)}) %collective-permute-start.11) | collective-permute-done | bytes 393248 | tf_op jit(solution)/shard_map/ppermute | solution.py:446
  34.5 0.0 collective-permute-done.5.rest_1_.refs_2_
  34.6 1.7 %collective-permute-start.14 = (bf16[96,1024]{1,0:T(8,128)(2,1)S(1)}, bf16[96,1024]{1,0:T(8,128)(2,1)S(1)}, u32[]{:S(2)}, u32[]{:S(2)}) collective-permute-start(bf16[96,1024]{1,0:T(8,128)(2,1)S(1)} %slice.6), channel_id=1, source_target_pairs={{0,2},{2,4},{4,6},{6,7},{7,5},{5,3},{3,1},{1,0},{8,10},{10,12},{12... | collective-permute-start | bytes 589832 | tf_op jit(solution)/shard_map/ppermute | solution.py:443
  36.3 0.5 collective-permute-start.15
  36.7 0.0 collective-permute-done.8.came_ref
  36.8 1.6 %collective-permute-start.9 = (f32[232,384]{1,0:T(8,128)S(1)}, f32[232,384]{1,0:T(8,128)S(1)}, u32[]{:S(2)}, u32[]{:S(2)}) collective-permute-start(f32[232,384]{1,0:T(8,128)S(1)} %add_cores.7.rest_0_.rest_2_), channel_id=1, source_target_pairs={{0,16},{8,24},{16,0},{24,8},{1,17},{9,25},{17,1},{25,9},{2,18},{10... | collective-permute-start | bytes 1069064 | tf_op jit(solution)/shard_map/ppermute | solution.py:437
  38.3 1.3 %next_products.6 = (f32[392,384]{1,0:T(8,128)S(1)}, f32[232,384]{1,0:T(8,128)S(1)}, f32[160,384]{1,0:T(8,128)S(1)}) custom-call(bf16[720,1024]{1,0:T(8,128)(2,1)S(1)} %get-tuple-element.36.left_ref, bf16[192,1024]{1,0:T(8,128)(2,1)S(1)} %get-tuple-element.47.rest_0_, bf16[192,1024]{1,0:T(8,128)(2,1)S(1)} %get-tuple-element.48.rest_1_, ...), custom_call_target="tpu_custom_call" | custom-call | flops 100000000 | tf_op jit(solution)/shard_map/next_products/pallas_call | solution.py:40
  39.6 0.0 collective-permute-start.12
  39.6 0.7 %collective-permute-done.14.refs_0_ = bf16[96,1024]{1,0:T(8,128)(2,1)S(1)} collective-permute-done((bf16[96,1024]{1,0:T(8,128)(2,1)S(1)}, bf16[96,1024]{1,0:T(8,128)(2,1)S(1)}, u32[]{:S(2)}, u32[]{:S(2)}) %collective-permute-start.14) | collective-permute-done | bytes 196640 | tf_op jit(solution)/shard_map/ppermute | solution.py:443
  40.3 1.7 %collective-permute-done.15.refs_1_ = bf16[96,1024]{1,0:T(8,128)(2,1)S(1)} collective-permute-done((bf16[96,1024]{1,0:T(8,128)(2,1)S(1)}, bf16[96,1024]{1,0:T(8,128)(2,1)S(1)}, u32[]{:S(2)}, u32[]{:S(2)}) %collective-permute-start.15) | collective-permute-done | bytes 196640 | tf_op jit(solution)/shard_map/ppermute | solution.py:446
  42.0 0.0 collective-permute-done.12.came_ref
  42.0 0.8 %next_products.7 = (f32[392,192]{1,0:T(8,128)S(1)}, f32[232,192]{1,0:T(8,128)S(1)}, f32[160,192]{1,0:T(8,128)S(1)}) custom-call(bf16[720,1024]{1,0:T(8,128)(2,1)S(1)} %get-tuple-element.36.left_ref, bf16[96,1024]{1,0:T(8,128)(2,1)S(1)} %get-tuple-element.52.rest_0_, bf16[96,1024]{1,0:T(8,128)(2,1)S(1)} %get-tuple-element.53.rest_1_, ...), custom_call_target="tpu_custom_call" | custom-call | flops 100000000 | tf_op jit(solution)/shard_map/next_products/pallas_call | solution.py:40
  42.8 0.0 copy-start.3
  42.8 0.0 copy-start.4
  42.8 0.0 copy-start.5
  42.8 0.1 collective-permute-start.16
  42.9 1.6 %collective-permute-start.13 = (f32[232,384]{1,0:T(8,128)S(1)}, f32[232,384]{1,0:T(8,128)S(1)}, u32[]{:S(2)}, u32[]{:S(2)}) collective-permute-start(f32[232,384]{1,0:T(8,128)S(1)} %add_cores.8.rest_0_.rest_2_), channel_id=1, source_target_pairs={{0,16},{8,24},{16,0},{24,8},{1,17},{9,25},{17,1},{25,9},{2,18},{10... | collective-permute-start | bytes 1069064 | tf_op jit(solution)/shard_map/ppermute | solution.py:437
  44.5 0.0 collective-permute-done.9.rest_1_.rest_0_
  44.5 0.2 collective-permute-done.16.came_ref
  44.6 0.1 add_cores.9.rest_0_
  44.7 1.6 %collective-permute-start.17 = (f32[352,128]{1,0:T(8,128)S(1)}, f32[352,128]{1,0:T(8,128)S(1)}, u32[]{:S(2)}, u32[]{:S(2)}) collective-permute-start(f32[352,128]{1,0:T(8,128)S(1)} %add_cores.9.rest_0_), channel_id=1, source_target_pairs={{0,16},{8,24},{16,0},{24,8},{1,17},{9,25},{17,1},{25,9},{2,18},{10... | collective-permute-start | bytes 540680 | tf_op jit(solution)/shard_map/ppermute | solution.py:437
  46.3 3.6 %solve.1 = (f32[232,72]{1,0:T(8,128)S(1)}, f32[160,128]{1,0:T(8,128)S(1)}) custom-call(f32[160,320]{1,0:T(8,128)S(1)} %get-tuple-element.31.mine_ref, f32[392,320]{1,0:T(8,128)S(1)} %collective-permute-done.came_ref.rest_2_, f32[584,128]{1,0:T(8,128)S(1)} %add_cores.5.rest_0_, f32[584,128]{1,0:T(8,128)S(1)} %collective-permute-done.1.rest_1_.refs_2_.rest_2_), custom_call_target="tpu_custom_call" | custom-call | flops 100000000 | tf_op jit(solution)/shard_map/solve/pallas_call | solution.py:40
  49.9 0.0 copy-done.3
  49.9 0.0 copy-done.4
  50.0 0.0 copy-done.5
  50.0 1.4 %widen.1.scale_ref = f32[160,1536]{1,0:T(8,128)S(1)} custom-call(f32[5,16]{1,0:T(8,128)S(1)} %copy-done.4, f32[160,128]{1,0:T(8,128)S(1)} %get-tuple-element.35.norm_ref, s32[24,160]{1,0:T(8,128)S(1)} %copy-done.3, s32[1,160]{1,0:T(1,128)S(1)} %bitcast.9), custom_call_target="tpu_custom_call" | custom-call | flops 1 | tf_op jit(solution)/shard_map/widen/pallas_call | solution.py:40
  51.4 0.5 chunk_stat.4.rest_0_
  51.8 0.6 chunk_stat.5.rest_1_
  52.4 0.6 chunk_stat.6.rest_2_
  53.0 1.1 %collective-permute-done.13.rest_1_ = f32[232,384]{1,0:T(8,128)S(1)} collective-permute-done((f32[232,384]{1,0:T(8,128)S(1)}, f32[232,384]{1,0:T(8,128)S(1)}, u32[]{:S(2)}, u32[]{:S(2)}) %collective-permute-start.13) | collective-permute-done | bytes 356384 | tf_op jit(solution)/shard_map/ppermute | solution.py:437
  54.1 0.6 chunk_stat.7.rest_3_
  54.7 1.0 %place.1.placed_ref = f32[160,1536]{1,0:T(8,128)S(1)} custom-call(s32[2]{0:T(128)S(1)} %pad_add_fusion.ids_ref, f32[160,1536]{1,0:T(8,128)S(1)} %widen.1.scale_ref, f32[160,192]{1,0:T(8,128)S(1)} %chunk_stat.4.rest_0_, f32[160,384]{1,0:T(8,128)S(1)} %chunk_stat.5.rest_1_, f32[160,384]{1,0:T(8,128)S(1)} %chunk_stat.6.rest_2_, f32[160,384]{1,0:T(8,128)S(1)} %chunk_stat.7.rest_3_), custom_call_target="tpu_custom_call" | custom-call | flops 1 | tf_op jit(solution)/shard_map/place/pallas_call | solution.py:40
  55.7 1.8 %collective-permute-done.17.rest_1_ = f32[352,128]{1,0:T(8,128)S(1)} collective-permute-done((f32[352,128]{1,0:T(8,128)S(1)}, f32[352,128]{1,0:T(8,128)S(1)}, u32[]{:S(2)}, u32[]{:S(2)}) %collective-permute-start.17) | collective-permute-done | bytes 180256 | tf_op jit(solution)/shard_map/ppermute | solution.py:437
  57.5 2.2 %finish.1 = f32[160,1536]{1,0:T(8,128)} custom-call(s32[2]{0:T(128)S(1)} %pad_add_fusion.ids_ref, f32[232,72]{1,0:T(8,128)S(1)} %get-tuple-element.34.solved_ref, f32[160,1536]{1,0:T(8,128)S(1)} %widen.1.scale_ref, f32[160,1536]{1,0:T(8,128)S(1)} %place.1.placed_ref, f32[160,192]{1,0:T(8,128)S(1)} %get-tuple-element.54.mine_ref, ...), custom_call_target="tpu_custom_call" | custom-call | flops 1 | tf_op jit(solution)/shard_map/finish/pallas_call | solution.py:412
  (9 shorter events, 0.1 us)
Async XLA Ops:
  0.0 12.3 %collective-permute-start.2 = (bf16[192,1024]{1,0:T(8,128)(2,1)}, bf16[192,1024]{1,0:T(8,128)(2,1)S(1)}, u32[]{:S(2)}, u32[]{:S(2)}) collective-permute-start(bf16[192,1024]{1,0:T(8,128)(2,1)} %bitcast.5), channel_id=1, source_target_pairs={{0,2},{2,4},{4,6},{6,7},{7,5},{5,3},{3,1},{1,0},{8,10},{10,12},{12... | collective-permute-start | bytes 1179656 | tf_op jit(solution)/shard_map/ppermute | solution.py:443
  3.0 10.8 %collective-permute-start.3 = (bf16[192,1024]{1,0:T(8,128)(2,1)}, bf16[192,1024]{1,0:T(8,128)(2,1)S(1)}, u32[]{:S(2)}, u32[]{:S(2)}) collective-permute-start(bf16[192,1024]{1,0:T(8,128)(2,1)} %bitcast.6), channel_id=1, source_target_pairs={{2,0},{4,2},{6,4},{7,6},{5,7},{3,5},{1,3},{0,1},{10,8},{12,10},{14... | collective-permute-start | bytes 1179656 | tf_op jit(solution)/shard_map/ppermute | solution.py:446
  3.1 1.3 %copy-start = (bf16[1024,640]{1,0:T(8,128)(2,1)S(1)}, bf16[1024,640]{1,0:T(8,128)(2,1)}, u32[]{:S(2)}) copy-start(bf16[1024,640]{1,0:T(8,128)(2,1)} %e_ref.1) | copy-start | bytes 3932164
  4.4 1.0 %copy-start.1 = (bf16[1024,192]{0,1:T(8,128)(2,1)S(1)}, bf16[1024,192]{0,1:T(8,128)(2,1)}, u32[]{:S(2)}) copy-start(bf16[1024,192]{0,1:T(8,128)(2,1)} %param.7) | copy-start | bytes 1179652
  5.4 0.9 %copy-start.2 = (bf16[1024,64]{0,1:T(8,128)(2,1)S(1)}, bf16[1024,64]{0,1:T(8,128)(2,1)}, u32[]{:S(2)}) copy-start(bf16[1024,64]{0,1:T(8,128)(2,1)} %param.8) | copy-start | bytes 393220
  8.7 7.2 %collective-permute-start = (f32[392,320]{1,0:T(8,128)S(1)}, f32[392,320]{1,0:T(8,128)S(1)}, u32[]{:S(2)}, u32[]{:S(2)}) collective-permute-start(f32[392,320]{1,0:T(8,128)S(1)} %get-tuple-element.32), channel_id=1, source_target_pairs={{0,8},{8,0},{16,24},{24,16},{1,9},{9,1},{17,25},{25,17},{2,10},{10... | collective-permute-start | bytes 1505288 | tf_op jit(solution)/shard_map/ppermute | solution.py:437
  13.8 9.7 %collective-permute-start.6 = (bf16[192,1024]{1,0:T(8,128)(2,1)S(1)}, bf16[192,1024]{1,0:T(8,128)(2,1)S(1)}, u32[]{:S(2)}, u32[]{:S(2)}) collective-permute-start(bf16[192,1024]{1,0:T(8,128)(2,1)S(1)} %get-tuple-element.37.rest_0_), channel_id=1, source_target_pairs={{0,2},{2,4},{4,6},{6,7},{7,5},{5,3},{3,1},{1,0},{8,10},{10,12},{12... | collective-permute-start | bytes 1179656 | tf_op jit(solution)/shard_map/ppermute | solution.py:443
  15.4 9.4 %collective-permute-start.7 = (bf16[192,1024]{1,0:T(8,128)(2,1)S(1)}, bf16[192,1024]{1,0:T(8,128)(2,1)S(1)}, u32[]{:S(2)}, u32[]{:S(2)}) collective-permute-start(bf16[192,1024]{1,0:T(8,128)(2,1)S(1)} %get-tuple-element.38.rest_1_), channel_id=1, source_target_pairs={{2,0},{4,2},{6,4},{7,6},{5,7},{3,5},{1,3},{0,1},{10,8},{12,10},{14... | collective-permute-start | bytes 1179656 | tf_op jit(solution)/shard_map/ppermute | solution.py:446
  15.9 8.8 %collective-permute-start.1 = (f32[584,128]{1,0:T(8,128)S(1)}, f32[584,128]{1,0:T(8,128)S(1)}, u32[]{:S(2)}, u32[]{:S(2)}) collective-permute-start(f32[584,128]{1,0:T(8,128)S(1)} %add_cores.5.rest_0_), channel_id=1, source_target_pairs={{0,16},{8,24},{16,0},{24,8},{1,17},{9,25},{17,1},{25,9},{2,18},{10... | collective-permute-start | bytes 897032 | tf_op jit(solution)/shard_map/ppermute | solution.py:437
  18.8 8.0 %collective-permute-start.4 = (f32[392,384]{1,0:T(8,128)S(1)}, f32[392,384]{1,0:T(8,128)S(1)}, u32[]{:S(2)}, u32[]{:S(2)}) collective-permute-start(f32[392,384]{1,0:T(8,128)S(1)} %get-tuple-element.40), channel_id=1, source_target_pairs={{0,8},{8,0},{16,24},{24,16},{1,9},{9,1},{17,25},{25,17},{2,10},{10... | collective-permute-start | bytes 1806344 | tf_op jit(solution)/shard_map/ppermute | solution.py:437
  24.8 8.5 %collective-permute-start.10 = (bf16[192,1024]{1,0:T(8,128)(2,1)S(1)}, bf16[192,1024]{1,0:T(8,128)(2,1)S(1)}, u32[]{:S(2)}, u32[]{:S(2)}) collective-permute-start(bf16[192,1024]{1,0:T(8,128)(2,1)S(1)} %get-tuple-element.42.rest_0_), channel_id=1, source_target_pairs={{0,2},{2,4},{4,6},{6,7},{7,5},{5,3},{3,1},{1,0},{8,10},{10,12},{12... | collective-permute-start | bytes 1179656 | tf_op jit(solution)/shard_map/ppermute | solution.py:443
  26.4 8.2 %collective-permute-start.11 = (bf16[192,1024]{1,0:T(8,128)(2,1)S(1)}, bf16[192,1024]{1,0:T(8,128)(2,1)S(1)}, u32[]{:S(2)}, u32[]{:S(2)}) collective-permute-start(bf16[192,1024]{1,0:T(8,128)(2,1)S(1)} %get-tuple-element.43.rest_1_), channel_id=1, source_target_pairs={{2,0},{4,2},{6,4},{7,6},{5,7},{3,5},{1,3},{0,1},{10,8},{12,10},{14... | collective-permute-start | bytes 1179656 | tf_op jit(solution)/shard_map/ppermute | solution.py:446
  26.9 7.7 %collective-permute-start.5 = (f32[232,384]{1,0:T(8,128)S(1)}, f32[232,384]{1,0:T(8,128)S(1)}, u32[]{:S(2)}, u32[]{:S(2)}) collective-permute-start(f32[232,384]{1,0:T(8,128)S(1)} %add_cores.6.rest_0_), channel_id=1, source_target_pairs={{0,16},{8,24},{16,0},{24,8},{1,17},{9,25},{17,1},{25,9},{2,18},{10... | collective-permute-start | bytes 1069064 | tf_op jit(solution)/shard_map/ppermute | solution.py:437
  29.7 7.0 %collective-permute-start.8 = (f32[392,384]{1,0:T(8,128)S(1)}, f32[392,384]{1,0:T(8,128)S(1)}, u32[]{:S(2)}, u32[]{:S(2)}) collective-permute-start(f32[392,384]{1,0:T(8,128)S(1)} %get-tuple-element.45), channel_id=1, source_target_pairs={{0,8},{8,0},{16,24},{24,16},{1,9},{9,1},{17,25},{25,17},{2,10},{10... | collective-permute-start | bytes 1806344 | tf_op jit(solution)/shard_map/ppermute | solution.py:437
  34.6 5.7 %collective-permute-start.14 = (bf16[96,1024]{1,0:T(8,128)(2,1)S(1)}, bf16[96,1024]{1,0:T(8,128)(2,1)S(1)}, u32[]{:S(2)}, u32[]{:S(2)}) collective-permute-start(bf16[96,1024]{1,0:T(8,128)(2,1)S(1)} %slice.6), channel_id=1, source_target_pairs={{0,2},{2,4},{4,6},{6,7},{7,5},{5,3},{3,1},{1,0},{8,10},{10,12},{12... | collective-permute-start | bytes 589832 | tf_op jit(solution)/shard_map/ppermute | solution.py:443
  36.3 5.7 %collective-permute-start.15 = (bf16[96,1024]{1,0:T(8,128)(2,1)S(1)}, bf16[96,1024]{1,0:T(8,128)(2,1)S(1)}, u32[]{:S(2)}, u32[]{:S(2)}) collective-permute-start(bf16[96,1024]{1,0:T(8,128)(2,1)S(1)} %slice.7), channel_id=1, source_target_pairs={{2,0},{4,2},{6,4},{7,6},{5,7},{3,5},{1,3},{0,1},{10,8},{12,10},{14... | collective-permute-start | bytes 589832 | tf_op jit(solution)/shard_map/ppermute | solution.py:446
  36.8 7.7 %collective-permute-start.9 = (f32[232,384]{1,0:T(8,128)S(1)}, f32[232,384]{1,0:T(8,128)S(1)}, u32[]{:S(2)}, u32[]{:S(2)}) collective-permute-start(f32[232,384]{1,0:T(8,128)S(1)} %add_cores.7.rest_0_.rest_2_), channel_id=1, source_target_pairs={{0,16},{8,24},{16,0},{24,8},{1,17},{9,25},{17,1},{25,9},{2,18},{10... | collective-permute-start | bytes 1069064 | tf_op jit(solution)/shard_map/ppermute | solution.py:437
  39.6 2.4 %collective-permute-start.12 = (f32[392,384]{1,0:T(8,128)S(1)}, f32[392,384]{1,0:T(8,128)S(1)}, u32[]{:S(2)}, u32[]{:S(2)}) collective-permute-start(f32[392,384]{1,0:T(8,128)S(1)} %get-tuple-element.50), channel_id=1, source_target_pairs={{0,8},{8,0},{16,24},{24,16},{1,9},{9,1},{17,25},{25,17},{2,10},{10... | collective-permute-start | bytes 1806344 | tf_op jit(solution)/shard_map/ppermute | solution.py:437
  42.8 7.1 %copy-start.3 = (s32[24,160]{1,0:T(8,128)S(1)}, s32[24,160]{1,0:T(8,128)}, u32[]{:S(2)}) copy-start(s32[24,160]{1,0:T(8,128)} %bins_ref.1) | copy-start | bytes 46084
  42.8 7.1 %copy-start.4 = (f32[5,16]{1,0:T(8,128)S(1)}, f32[5,16]{1,0:T(8,128)}, u32[]{:S(2)}) copy-start(f32[5,16]{1,0:T(8,128)} %weight_ref.1) | copy-start | bytes 964
  42.8 7.1 %copy-start.5 = (s32[160]{0:T(256)S(1)}, s32[160]{0:T(256)}, u32[]{:S(2)}) copy-start(s32[160]{0:T(256)} %param.10) | copy-start | bytes 1924
  42.8 1.8 %collective-permute-start.16 = (f32[392,192]{1,0:T(8,128)S(1)}, f32[392,192]{1,0:T(8,128)S(1)}, u32[]{:S(2)}, u32[]{:S(2)}) collective-permute-start(f32[392,192]{1,0:T(8,128)S(1)} %get-tuple-element.55), channel_id=1, source_target_pairs={{0,8},{8,0},{16,24},{24,16},{1,9},{9,1},{17,25},{25,17},{2,10},{10... | collective-permute-start | bytes 903176 | tf_op jit(solution)/shard_map/ppermute | solution.py:437
  42.9 11.2 %collective-permute-start.13 = (f32[232,384]{1,0:T(8,128)S(1)}, f32[232,384]{1,0:T(8,128)S(1)}, u32[]{:S(2)}, u32[]{:S(2)}) collective-permute-start(f32[232,384]{1,0:T(8,128)S(1)} %add_cores.8.rest_0_.rest_2_), channel_id=1, source_target_pairs={{0,16},{8,24},{16,0},{24,8},{1,17},{9,25},{17,1},{25,9},{2,18},{10... | collective-permute-start | bytes 1069064 | tf_op jit(solution)/shard_map/ppermute | solution.py:437
  44.7 12.8 %collective-permute-start.17 = (f32[352,128]{1,0:T(8,128)S(1)}, f32[352,128]{1,0:T(8,128)S(1)}, u32[]{:S(2)}, u32[]{:S(2)}) collective-permute-start(f32[352,128]{1,0:T(8,128)S(1)} %add_cores.9.rest_0_), channel_id=1, source_target_pairs={{0,16},{8,24},{16,0},{24,8},{1,17},{9,25},{17,1},{25,9},{2,18},{10... | collective-permute-start | bytes 540680 | tf_op jit(solution)/shard_map/ppermute | solution.py:437

commit v4 on v2

--- a/solution.py
+++ b/solution.py
@@ -344,12 +344,16 @@
     )
 
 
-def slot_of(index, here, ring, order):
-    position = {block: i for i, block in enumerate(order)}
-    mine = jnp.int32(0)
-    for block in range(ring):
-        mine = jnp.where(here == block, position[block], mine)
-    return lax.rem(position[index] - mine + ring, ring)
+def lookup(key, table):
+    value = jnp.int32(table[0])
+    for i in range(1, len(table)):
+        value = jnp.where(key == i, jnp.int32(table[i]), value)
+    return value
+
+
+def wrap(step, ring):
+    step = jnp.where(step < 0, step + ring, step)
+    return jnp.where(step >= ring, step - ring, step)
 
 
 def place_kernel(ring, order, ids_ref, scale_ref, *rest):
@@ -363,8 +367,10 @@
             held[ring - k] = stat[:, :variants]
             held[k] = stat[:, variants:]
     group = LANES // math.gcd(variants, LANES)
+    position = [order.index(block) for block in range(ring)]
+    mine = lookup(ids_ref[1], position)
     for j in range(0, ring, group):
-        pieces = [held[slot_of(j + b, ids_ref[1], ring, order)] for b in range(group)]
+        pieces = [held[wrap(position[j + b] - mine, ring)] for b in range(group)]
         span = slice(j * variants, (j + group) * variants)
         out_ref[:, span] = jnp.concatenate(pieces, axis=1) * scale_ref[:, span]
 
@@ -388,13 +394,12 @@
     width = group * variants
     stat = fitted_stat(covs, 0, solved_ref, mine_ref, came_ref, rest[:-1])
     out_ref[...] = placed_ref[...]
-    index = jnp.int32(0)
-    for block in range(ring):
-        index = jnp.where(slot_of(block, ids_ref[1], ring, order) == ring // 2, block, index)
-    span = pl.ds(pl.multiple_of(index // group * width, LANES), width)
+    across = [order[(order.index(block) + ring // 2) % ring] for block in range(ring)]
+    start = lookup(ids_ref[1], [block // group * width for block in across])
+    first = lookup(ids_ref[1], [block % group * variants for block in across])
+    span = pl.ds(pl.multiple_of(start, LANES), width)
     stat = jnp.concatenate([stat] * group, axis=1)
     lane = lax.broadcasted_iota(jnp.int32, stat.shape, 1)
-    first = lax.rem(index, group) * variants
     inside = jnp.logical_and(lane >= first, lane < first + variants)
     out_ref[:, span] = jnp.where(inside, stat * scale_ref[:, span], placed_ref[:, span])
 

time: 59.8 us -> 59.8 us (level)
  no operation moved by 1% of the time
where the time goes in v4:
time: 59.8 us; the launch traced here: 59.6 us
  waiting for transfers between devices  21.4 us (36%)
  Pallas kernels  17.6 us (29%)
  starting transfers between devices  17.1 us (29%)
  local copies, waits for them, and re-layouts  3.26 us (5%)
    pallas_call x18, Pallas kernels, call(): pl.pallas_call(kernel, out_shape=out_shape, in_specs=[smem] * scalars + [...  17.6 us
    ppermute x4, waiting for transfers between devices, right(): return lax.ppermute(x, 'var', forward)  12.5 us
    ppermute x10, starting transfers between devices, exchange(): return lax.ppermute(x, 'samp', [(s, s ^ d) for s in range(parts)])  7.85 us
    ppermute x4, starting transfers between devices, right(): return lax.ppermute(x, 'var', forward)  7.85 us
    ppermute x4, waiting for transfers between devices, left(): return lax.ppermute(x, 'var', backward)  5.81 us
    unnamed x12, local copies, waits for them, and re-layouts  3.23 us
    ppermute x10, waiting for transfers between devices, exchange(): return lax.ppermute(x, 'samp', [(s, s ^ d) for s in range(parts)])  3.1 us
    ppermute x4, starting transfers between devices, left(): return lax.ppermute(x, 'var', backward)  1.36 us
  transfers between devices with their start and end apart: 18, of which 11 were waited for; matrix products, arithmetic and copies ran while one was open for 0% of the time, Pallas kernels for 26%

profile of v4, /device:TPU:0, one launch (start us, length us, event | category | flops | bytes accessed | tf_op | source)
XLA Modules:
  0.0 59.6 jit_solution(10266958036126711136)
XLA Ops:
  0.0 3.0 %collective-permute-start.2 = (bf16[192,1024]{1,0:T(8,128)(2,1)}, bf16[192,1024]{1,0:T(8,128)(2,1)S(1)}, u32[]{:S(2)}, u32[]{:S(2)}) collective-permute-start(bf16[192,1024]{1,0:T(8,128)(2,1)} %bitcast.5), channel_id=1, source_target_pairs={{0,2},{2,4},{4,6},{6,7},{7,5},{5,3},{3,1},{1,0},{8,10},{10,12},{12... | collective-permute-start | bytes 1179656 | tf_op jit(solution)/shard_map/ppermute | solution.py:436
  3.0 0.0 collective-permute-start.3
  3.0 0.1 pad_add_fusion.ids_ref
  3.1 0.0 copy-start
  3.1 1.3 %copy-done = bf16[1024,640]{1,0:T(8,128)(2,1)S(1)} copy-done((bf16[1024,640]{1,0:T(8,128)(2,1)S(1)}, bf16[1024,640]{1,0:T(8,128)(2,1)}, u32[]{:S(2)}) %copy-start) | copy-done | bytes 1310744
  4.4 0.0 copy-start.1
  4.4 1.0 %copy-done.1 = bf16[1024,192]{0,1:T(8,128)(2,1)S(1)} copy-done((bf16[1024,192]{0,1:T(8,128)(2,1)S(1)}, bf16[1024,192]{0,1:T(8,128)(2,1)}, u32[]{:S(2)}) %copy-start.1) | copy-done | bytes 393240
  5.4 0.9 %copy-done.2 = bf16[1024,64]{0,1:T(8,128)(2,1)S(1)} copy-done((bf16[1024,64]{0,1:T(8,128)(2,1)S(1)}, bf16[1024,64]{0,1:T(8,128)(2,1)}, u32[]{:S(2)}) %copy-start.2) | copy-done | bytes 131096
  6.3 2.4 %first_products.1 = (bf16[720,1024]{1,0:T(8,128)(2,1)S(1)}, f32[392,320]{1,0:T(8,128)S(1)}, f32[232,320]{1,0:T(8,128)S(1)}, f32[160,320]{1,0:T(8,128)S(1)}) custom-call(s32[2]{0:T(128)S(1)} %pad_add_fusion.ids_ref, bf16[1024,640]{1,0:T(8,128)(2,1)S(1)} %copy-done, bf16[192,1024]{1,0:T(8,128)(2,1)S(1)} %bitcast.7, bf16[64,1024]{1,0:T(8,128)(2,1)S(1)} %bitcast.8), custom_call_target="tpu_custom_call" | custom-call | flops 100000000 | tf_op jit(solution)/shard_map/first_products/pallas_call | solution.py:40
  8.7 0.0 collective-permute-start
  8.7 3.6 %collective-permute-done.2.refs_0_ = bf16[192,1024]{1,0:T(8,128)(2,1)S(1)} collective-permute-done((bf16[192,1024]{1,0:T(8,128)(2,1)}, bf16[192,1024]{1,0:T(8,128)(2,1)S(1)}, u32[]{:S(2)}, u32[]{:S(2)}) %collective-permute-start.2) | collective-permute-done | bytes 393248 | tf_op jit(solution)/shard_map/ppermute | solution.py:436
  12.3 1.5 %collective-permute-done.3.refs_1_ = bf16[192,1024]{1,0:T(8,128)(2,1)S(1)} collective-permute-done((bf16[192,1024]{1,0:T(8,128)(2,1)}, bf16[192,1024]{1,0:T(8,128)(2,1)S(1)}, u32[]{:S(2)}, u32[]{:S(2)}) %collective-permute-start.3) | collective-permute-done | bytes 393248 | tf_op jit(solution)/shard_map/ppermute | solution.py:439
  13.8 1.6 %collective-permute-start.6 = (bf16[192,1024]{1,0:T(8,128)(2,1)S(1)}, bf16[192,1024]{1,0:T(8,128)(2,1)S(1)}, u32[]{:S(2)}, u32[]{:S(2)}) collective-permute-start(bf16[192,1024]{1,0:T(8,128)(2,1)S(1)} %get-tuple-element.37.rest_0_), channel_id=1, source_target_pairs={{0,2},{2,4},{4,6},{6,7},{7,5},{5,3},{3,1},{1,0},{8,10},{10,12},{12... | collective-permute-start | bytes 1179656 | tf_op jit(solution)/shard_map/ppermute | solution.py:436
  15.4 0.4 collective-permute-start.7
  15.8 0.0 collective-permute-done.came_ref.rest_2_
  15.8 0.1 add_cores.5.rest_0_
  15.9 1.6 %collective-permute-start.1 = (f32[584,128]{1,0:T(8,128)S(1)}, f32[584,128]{1,0:T(8,128)S(1)}, u32[]{:S(2)}, u32[]{:S(2)}) collective-permute-start(f32[584,128]{1,0:T(8,128)S(1)} %add_cores.5.rest_0_), channel_id=1, source_target_pairs={{0,16},{8,24},{16,0},{24,8},{1,17},{9,25},{17,1},{25,9},{2,18},{10... | collective-permute-start | bytes 897032 | tf_op jit(solution)/shard_map/ppermute | solution.py:430
  17.5 1.3 %next_products.4 = (f32[392,384]{1,0:T(8,128)S(1)}, f32[232,384]{1,0:T(8,128)S(1)}, f32[160,384]{1,0:T(8,128)S(1)}) custom-call(bf16[720,1024]{1,0:T(8,128)(2,1)S(1)} %get-tuple-element.36.left_ref, bf16[192,1024]{1,0:T(8,128)(2,1)S(1)} %get-tuple-element.37.rest_0_, bf16[192,1024]{1,0:T(8,128)(2,1)S(1)} %get-tuple-element.38.rest_1_, ...), custom_call_target="tpu_custom_call" | custom-call | flops 100000000 | tf_op jit(solution)/shard_map/next_products/pallas_call | solution.py:40
  18.8 0.0 collective-permute-start.4
  18.8 4.7 %collective-permute-done.6.refs_0_ = bf16[192,1024]{1,0:T(8,128)(2,1)S(1)} collective-permute-done((bf16[192,1024]{1,0:T(8,128)(2,1)S(1)}, bf16[192,1024]{1,0:T(8,128)(2,1)S(1)}, u32[]{:S(2)}, u32[]{:S(2)}) %collective-permute-start.6) | collective-permute-done | bytes 393248 | tf_op jit(solution)/shard_map/ppermute | solution.py:436
  23.5 1.3 %collective-permute-done.7.refs_1_ = bf16[192,1024]{1,0:T(8,128)(2,1)S(1)} collective-permute-done((bf16[192,1024]{1,0:T(8,128)(2,1)S(1)}, bf16[192,1024]{1,0:T(8,128)(2,1)S(1)}, u32[]{:S(2)}, u32[]{:S(2)}) %collective-permute-start.7) | collective-permute-done | bytes 393248 | tf_op jit(solution)/shard_map/ppermute | solution.py:439
  24.8 0.0 collective-permute-done.1.rest_1_.refs_2_.rest_2_
  24.8 1.6 %collective-permute-start.10 = (bf16[192,1024]{1,0:T(8,128)(2,1)S(1)}, bf16[192,1024]{1,0:T(8,128)(2,1)S(1)}, u32[]{:S(2)}, u32[]{:S(2)}) collective-permute-start(bf16[192,1024]{1,0:T(8,128)(2,1)S(1)} %get-tuple-element.42.rest_0_), channel_id=1, source_target_pairs={{0,2},{2,4},{4,6},{6,7},{7,5},{5,3},{3,1},{1,0},{8,10},{10,12},{12... | collective-permute-start | bytes 1179656 | tf_op jit(solution)/shard_map/ppermute | solution.py:436
  26.4 0.4 collective-permute-start.11
  26.8 0.0 collective-permute-done.4.came_ref
  26.8 0.1 add_cores.6.rest_0_
  26.9 1.6 %collective-permute-start.5 = (f32[232,384]{1,0:T(8,128)S(1)}, f32[232,384]{1,0:T(8,128)S(1)}, u32[]{:S(2)}, u32[]{:S(2)}) collective-permute-start(f32[232,384]{1,0:T(8,128)S(1)} %add_cores.6.rest_0_), channel_id=1, source_target_pairs={{0,16},{8,24},{16,0},{24,8},{1,17},{9,25},{17,1},{25,9},{2,18},{10... | collective-permute-start | bytes 1069064 | tf_op jit(solution)/shard_map/ppermute | solution.py:430
  28.4 1.3 %next_products.5 = (f32[392,384]{1,0:T(8,128)S(1)}, f32[232,384]{1,0:T(8,128)S(1)}, f32[160,384]{1,0:T(8,128)S(1)}) custom-call(bf16[720,1024]{1,0:T(8,128)(2,1)S(1)} %get-tuple-element.36.left_ref, bf16[192,1024]{1,0:T(8,128)(2,1)S(1)} %get-tuple-element.42.rest_0_, bf16[192,1024]{1,0:T(8,128)(2,1)S(1)} %get-tuple-element.43.rest_1_, ...), custom_call_target="tpu_custom_call" | custom-call | flops 100000000 | tf_op jit(solution)/shard_map/next_products/pallas_call | solution.py:40
  29.7 0.0 collective-permute-start.8
  29.7 3.5 %collective-permute-done.10.refs_0_ = bf16[192,1024]{1,0:T(8,128)(2,1)S(1)} collective-permute-done((bf16[192,1024]{1,0:T(8,128)(2,1)S(1)}, bf16[192,1024]{1,0:T(8,128)(2,1)S(1)}, u32[]{:S(2)}, u32[]{:S(2)}) %collective-permute-start.10) | collective-permute-done | bytes 393248 | tf_op jit(solution)/shard_map/ppermute | solution.py:436
  33.2 1.3 %collective-permute-done.11.refs_1_ = bf16[192,1024]{1,0:T(8,128)(2,1)S(1)} collective-permute-done((bf16[192,1024]{1,0:T(8,128)(2,1)S(1)}, bf16[192,1024]{1,0:T(8,128)(2,1)S(1)}, u32[]{:S(2)}, u32[]{:S(2)}) %collective-permute-start.11) | collective-permute-done | bytes 393248 | tf_op jit(solution)/shard_map/ppermute | solution.py:439
  34.5 0.0 collective-permute-done.5.rest_1_.refs_2_
  34.6 1.7 %collective-permute-start.14 = (bf16[96,1024]{1,0:T(8,128)(2,1)S(1)}, bf16[96,1024]{1,0:T(8,128)(2,1)S(1)}, u32[]{:S(2)}, u32[]{:S(2)}) collective-permute-start(bf16[96,1024]{1,0:T(8,128)(2,1)S(1)} %slice.6), channel_id=1, source_target_pairs={{0,2},{2,4},{4,6},{6,7},{7,5},{5,3},{3,1},{1,0},{8,10},{10,12},{12... | collective-permute-start | bytes 589832 | tf_op jit(solution)/shard_map/ppermute | solution.py:436
  36.3 0.5 collective-permute-start.15
  36.7 0.0 collective-permute-done.8.came_ref
  36.8 1.6 %collective-permute-start.9 = (f32[232,384]{1,0:T(8,128)S(1)}, f32[232,384]{1,0:T(8,128)S(1)}, u32[]{:S(2)}, u32[]{:S(2)}) collective-permute-start(f32[232,384]{1,0:T(8,128)S(1)} %add_cores.7.rest_0_.rest_2_), channel_id=1, source_target_pairs={{0,16},{8,24},{16,0},{24,8},{1,17},{9,25},{17,1},{25,9},{2,18},{10... | collective-permute-start | bytes 1069064 | tf_op jit(solution)/shard_map/ppermute | solution.py:430
  38.3 1.3 %next_products.6 = (f32[392,384]{1,0:T(8,128)S(1)}, f32[232,384]{1,0:T(8,128)S(1)}, f32[160,384]{1,0:T(8,128)S(1)}) custom-call(bf16[720,1024]{1,0:T(8,128)(2,1)S(1)} %get-tuple-element.36.left_ref, bf16[192,1024]{1,0:T(8,128)(2,1)S(1)} %get-tuple-element.47.rest_0_, bf16[192,1024]{1,0:T(8,128)(2,1)S(1)} %get-tuple-element.48.rest_1_, ...), custom_call_target="tpu_custom_call" | custom-call | flops 100000000 | tf_op jit(solution)/shard_map/next_products/pallas_call | solution.py:40
  39.6 0.0 collective-permute-start.12
  39.6 0.7 %collective-permute-done.14.refs_0_ = bf16[96,1024]{1,0:T(8,128)(2,1)S(1)} collective-permute-done((bf16[96,1024]{1,0:T(8,128)(2,1)S(1)}, bf16[96,1024]{1,0:T(8,128)(2,1)S(1)}, u32[]{:S(2)}, u32[]{:S(2)}) %collective-permute-start.14) | collective-permute-done | bytes 196640 | tf_op jit(solution)/shard_map/ppermute | solution.py:436
  40.3 1.7 %collective-permute-done.15.refs_1_ = bf16[96,1024]{1,0:T(8,128)(2,1)S(1)} collective-permute-done((bf16[96,1024]{1,0:T(8,128)(2,1)S(1)}, bf16[96,1024]{1,0:T(8,128)(2,1)S(1)}, u32[]{:S(2)}, u32[]{:S(2)}) %collective-permute-start.15) | collective-permute-done | bytes 196640 | tf_op jit(solution)/shard_map/ppermute | solution.py:439
  42.0 0.0 collective-permute-done.12.came_ref
  42.0 0.8 %next_products.7 = (f32[392,192]{1,0:T(8,128)S(1)}, f32[232,192]{1,0:T(8,128)S(1)}, f32[160,192]{1,0:T(8,128)S(1)}) custom-call(bf16[720,1024]{1,0:T(8,128)(2,1)S(1)} %get-tuple-element.36.left_ref, bf16[96,1024]{1,0:T(8,128)(2,1)S(1)} %get-tuple-element.52.rest_0_, bf16[96,1024]{1,0:T(8,128)(2,1)S(1)} %get-tuple-element.53.rest_1_, ...), custom_call_target="tpu_custom_call" | custom-call | flops 100000000 | tf_op jit(solution)/shard_map/next_products/pallas_call | solution.py:40
  42.8 0.0 copy-start.3
  42.8 0.0 copy-start.4
  42.8 0.0 copy-start.5
  42.8 0.1 collective-permute-start.16
  42.9 1.6 %collective-permute-start.13 = (f32[232,384]{1,0:T(8,128)S(1)}, f32[232,384]{1,0:T(8,128)S(1)}, u32[]{:S(2)}, u32[]{:S(2)}) collective-permute-start(f32[232,384]{1,0:T(8,128)S(1)} %add_cores.8.rest_0_.rest_2_), channel_id=1, source_target_pairs={{0,16},{8,24},{16,0},{24,8},{1,17},{9,25},{17,1},{25,9},{2,18},{10... | collective-permute-start | bytes 1069064 | tf_op jit(solution)/shard_map/ppermute | solution.py:430
  44.5 0.0 collective-permute-done.9.rest_1_.rest_0_
  44.5 0.2 collective-permute-done.16.came_ref
  44.6 0.1 add_cores.9.rest_0_
  44.7 1.6 %collective-permute-start.17 = (f32[352,128]{1,0:T(8,128)S(1)}, f32[352,128]{1,0:T(8,128)S(1)}, u32[]{:S(2)}, u32[]{:S(2)}) collective-permute-start(f32[352,128]{1,0:T(8,128)S(1)} %add_cores.9.rest_0_), channel_id=1, source_target_pairs={{0,16},{8,24},{16,0},{24,8},{1,17},{9,25},{17,1},{25,9},{2,18},{10... | collective-permute-start | bytes 540680 | tf_op jit(solution)/shard_map/ppermute | solution.py:430
  46.3 3.6 %solve.1 = (f32[232,72]{1,0:T(8,128)S(1)}, f32[160,128]{1,0:T(8,128)S(1)}) custom-call(f32[160,320]{1,0:T(8,128)S(1)} %get-tuple-element.31.mine_ref, f32[392,320]{1,0:T(8,128)S(1)} %collective-permute-done.came_ref.rest_2_, f32[584,128]{1,0:T(8,128)S(1)} %add_cores.5.rest_0_, f32[584,128]{1,0:T(8,128)S(1)} %collective-permute-done.1.rest_1_.refs_2_.rest_2_), custom_call_target="tpu_custom_call" | custom-call | flops 100000000 | tf_op jit(solution)/shard_map/solve/pallas_call | solution.py:40
  49.9 0.0 copy-done.3
  49.9 0.0 copy-done.4
  50.0 0.0 copy-done.5
  50.0 1.4 %widen.1.scale_ref = f32[160,1536]{1,0:T(8,128)S(1)} custom-call(f32[5,16]{1,0:T(8,128)S(1)} %copy-done.4, f32[160,128]{1,0:T(8,128)S(1)} %get-tuple-element.35.norm_ref, s32[24,160]{1,0:T(8,128)S(1)} %copy-done.3, s32[1,160]{1,0:T(1,128)S(1)} %bitcast.9), custom_call_target="tpu_custom_call" | custom-call | flops 1 | tf_op jit(solution)/shard_map/widen/pallas_call | solution.py:40
  51.4 0.5 chunk_stat.4.rest_0_
  51.8 0.6 chunk_stat.5.rest_1_
  52.4 0.6 chunk_stat.6.rest_2_
  53.0 1.1 %collective-permute-done.13.rest_1_ = f32[232,384]{1,0:T(8,128)S(1)} collective-permute-done((f32[232,384]{1,0:T(8,128)S(1)}, f32[232,384]{1,0:T(8,128)S(1)}, u32[]{:S(2)}, u32[]{:S(2)}) %collective-permute-start.13) | collective-permute-done | bytes 356384 | tf_op jit(solution)/shard_map/ppermute | solution.py:430
  54.1 0.6 chunk_stat.7.rest_3_
  54.7 1.0 %place.1.placed_ref = f32[160,1536]{1,0:T(8,128)S(1)} custom-call(s32[2]{0:T(128)S(1)} %pad_add_fusion.ids_ref, f32[160,1536]{1,0:T(8,128)S(1)} %widen.1.scale_ref, f32[160,192]{1,0:T(8,128)S(1)} %chunk_stat.4.rest_0_, f32[160,384]{1,0:T(8,128)S(1)} %chunk_stat.5.rest_1_, f32[160,384]{1,0:T(8,128)S(1)} %chunk_stat.6.rest_2_, f32[160,384]{1,0:T(8,128)S(1)} %chunk_stat.7.rest_3_), custom_call_target="tpu_custom_call" | custom-call | flops 1 | tf_op jit(solution)/shard_map/place/pallas_call | solution.py:40
  55.7 1.8 %collective-permute-done.17.rest_1_ = f32[352,128]{1,0:T(8,128)S(1)} collective-permute-done((f32[352,128]{1,0:T(8,128)S(1)}, f32[352,128]{1,0:T(8,128)S(1)}, u32[]{:S(2)}, u32[]{:S(2)}) %collective-permute-start.17) | collective-permute-done | bytes 180256 | tf_op jit(solution)/shard_map/ppermute | solution.py:430
  57.5 2.0 %finish.1 = f32[160,1536]{1,0:T(8,128)} custom-call(s32[2]{0:T(128)S(1)} %pad_add_fusion.ids_ref, f32[232,72]{1,0:T(8,128)S(1)} %get-tuple-element.34.solved_ref, f32[160,1536]{1,0:T(8,128)S(1)} %widen.1.scale_ref, f32[160,1536]{1,0:T(8,128)S(1)} %place.1.placed_ref, f32[160,192]{1,0:T(8,128)S(1)} %get-tuple-element.54.mine_ref, ...), custom_call_target="tpu_custom_call" | custom-call | flops 1 | tf_op jit(solution)/shard_map/finish/pallas_call | solution.py:40
  (9 shorter events, 0.1 us)
Async XLA Ops:
  0.0 12.3 %collective-permute-start.2 = (bf16[192,1024]{1,0:T(8,128)(2,1)}, bf16[192,1024]{1,0:T(8,128)(2,1)S(1)}, u32[]{:S(2)}, u32[]{:S(2)}) collective-permute-start(bf16[192,1024]{1,0:T(8,128)(2,1)} %bitcast.5), channel_id=1, source_target_pairs={{0,2},{2,4},{4,6},{6,7},{7,5},{5,3},{3,1},{1,0},{8,10},{10,12},{12... | collective-permute-start | bytes 1179656 | tf_op jit(solution)/shard_map/ppermute | solution.py:436
  3.0 10.8 %collective-permute-start.3 = (bf16[192,1024]{1,0:T(8,128)(2,1)}, bf16[192,1024]{1,0:T(8,128)(2,1)S(1)}, u32[]{:S(2)}, u32[]{:S(2)}) collective-permute-start(bf16[192,1024]{1,0:T(8,128)(2,1)} %bitcast.6), channel_id=1, source_target_pairs={{2,0},{4,2},{6,4},{7,6},{5,7},{3,5},{1,3},{0,1},{10,8},{12,10},{14... | collective-permute-start | bytes 1179656 | tf_op jit(solution)/shard_map/ppermute | solution.py:439
  3.1 1.3 %copy-start = (bf16[1024,640]{1,0:T(8,128)(2,1)S(1)}, bf16[1024,640]{1,0:T(8,128)(2,1)}, u32[]{:S(2)}) copy-start(bf16[1024,640]{1,0:T(8,128)(2,1)} %e_ref.1) | copy-start | bytes 3932164
  4.4 1.0 %copy-start.1 = (bf16[1024,192]{0,1:T(8,128)(2,1)S(1)}, bf16[1024,192]{0,1:T(8,128)(2,1)}, u32[]{:S(2)}) copy-start(bf16[1024,192]{0,1:T(8,128)(2,1)} %param.7) | copy-start | bytes 1179652
  5.4 0.9 %copy-start.2 = (bf16[1024,64]{0,1:T(8,128)(2,1)S(1)}, bf16[1024,64]{0,1:T(8,128)(2,1)}, u32[]{:S(2)}) copy-start(bf16[1024,64]{0,1:T(8,128)(2,1)} %param.8) | copy-start | bytes 393220
  8.7 7.2 %collective-permute-start = (f32[392,320]{1,0:T(8,128)S(1)}, f32[392,320]{1,0:T(8,128)S(1)}, u32[]{:S(2)}, u32[]{:S(2)}) collective-permute-start(f32[392,320]{1,0:T(8,128)S(1)} %get-tuple-element.32), channel_id=1, source_target_pairs={{0,8},{8,0},{16,24},{24,16},{1,9},{9,1},{17,25},{25,17},{2,10},{10... | collective-permute-start | bytes 1505288 | tf_op jit(solution)/shard_map/ppermute | solution.py:430
  13.8 9.7 %collective-permute-start.6 = (bf16[192,1024]{1,0:T(8,128)(2,1)S(1)}, bf16[192,1024]{1,0:T(8,128)(2,1)S(1)}, u32[]{:S(2)}, u32[]{:S(2)}) collective-permute-start(bf16[192,1024]{1,0:T(8,128)(2,1)S(1)} %get-tuple-element.37.rest_0_), channel_id=1, source_target_pairs={{0,2},{2,4},{4,6},{6,7},{7,5},{5,3},{3,1},{1,0},{8,10},{10,12},{12... | collective-permute-start | bytes 1179656 | tf_op jit(solution)/shard_map/ppermute | solution.py:436
  15.4 9.4 %collective-permute-start.7 = (bf16[192,1024]{1,0:T(8,128)(2,1)S(1)}, bf16[192,1024]{1,0:T(8,128)(2,1)S(1)}, u32[]{:S(2)}, u32[]{:S(2)}) collective-permute-start(bf16[192,1024]{1,0:T(8,128)(2,1)S(1)} %get-tuple-element.38.rest_1_), channel_id=1, source_target_pairs={{2,0},{4,2},{6,4},{7,6},{5,7},{3,5},{1,3},{0,1},{10,8},{12,10},{14... | collective-permute-start | bytes 1179656 | tf_op jit(solution)/shard_map/ppermute | solution.py:439
  15.9 8.8 %collective-permute-start.1 = (f32[584,128]{1,0:T(8,128)S(1)}, f32[584,128]{1,0:T(8,128)S(1)}, u32[]{:S(2)}, u32[]{:S(2)}) collective-permute-start(f32[584,128]{1,0:T(8,128)S(1)} %add_cores.5.rest_0_), channel_id=1, source_target_pairs={{0,16},{8,24},{16,0},{24,8},{1,17},{9,25},{17,1},{25,9},{2,18},{10... | collective-permute-start | bytes 897032 | tf_op jit(solution)/shard_map/ppermute | solution.py:430
  18.8 8.0 %collective-permute-start.4 = (f32[392,384]{1,0:T(8,128)S(1)}, f32[392,384]{1,0:T(8,128)S(1)}, u32[]{:S(2)}, u32[]{:S(2)}) collective-permute-start(f32[392,384]{1,0:T(8,128)S(1)} %get-tuple-element.40), channel_id=1, source_target_pairs={{0,8},{8,0},{16,24},{24,16},{1,9},{9,1},{17,25},{25,17},{2,10},{10... | collective-permute-start | bytes 1806344 | tf_op jit(solution)/shard_map/ppermute | solution.py:430
  24.8 8.5 %collective-permute-start.10 = (bf16[192,1024]{1,0:T(8,128)(2,1)S(1)}, bf16[192,1024]{1,0:T(8,128)(2,1)S(1)}, u32[]{:S(2)}, u32[]{:S(2)}) collective-permute-start(bf16[192,1024]{1,0:T(8,128)(2,1)S(1)} %get-tuple-element.42.rest_0_), channel_id=1, source_target_pairs={{0,2},{2,4},{4,6},{6,7},{7,5},{5,3},{3,1},{1,0},{8,10},{10,12},{12... | collective-permute-start | bytes 1179656 | tf_op jit(solution)/shard_map/ppermute | solution.py:436
  26.4 8.2 %collective-permute-start.11 = (bf16[192,1024]{1,0:T(8,128)(2,1)S(1)}, bf16[192,1024]{1,0:T(8,128)(2,1)S(1)}, u32[]{:S(2)}, u32[]{:S(2)}) collective-permute-start(bf16[192,1024]{1,0:T(8,128)(2,1)S(1)} %get-tuple-element.43.rest_1_), channel_id=1, source_target_pairs={{2,0},{4,2},{6,4},{7,6},{5,7},{3,5},{1,3},{0,1},{10,8},{12,10},{14... | collective-permute-start | bytes 1179656 | tf_op jit(solution)/shard_map/ppermute | solution.py:439
  26.9 7.7 %collective-permute-start.5 = (f32[232,384]{1,0:T(8,128)S(1)}, f32[232,384]{1,0:T(8,128)S(1)}, u32[]{:S(2)}, u32[]{:S(2)}) collective-permute-start(f32[232,384]{1,0:T(8,128)S(1)} %add_cores.6.rest_0_), channel_id=1, source_target_pairs={{0,16},{8,24},{16,0},{24,8},{1,17},{9,25},{17,1},{25,9},{2,18},{10... | collective-permute-start | bytes 1069064 | tf_op jit(solution)/shard_map/ppermute | solution.py:430
  29.7 7.0 %collective-permute-start.8 = (f32[392,384]{1,0:T(8,128)S(1)}, f32[392,384]{1,0:T(8,128)S(1)}, u32[]{:S(2)}, u32[]{:S(2)}) collective-permute-start(f32[392,384]{1,0:T(8,128)S(1)} %get-tuple-element.45), channel_id=1, source_target_pairs={{0,8},{8,0},{16,24},{24,16},{1,9},{9,1},{17,25},{25,17},{2,10},{10... | collective-permute-start | bytes 1806344 | tf_op jit(solution)/shard_map/ppermute | solution.py:430
  34.6 5.7 %collective-permute-start.14 = (bf16[96,1024]{1,0:T(8,128)(2,1)S(1)}, bf16[96,1024]{1,0:T(8,128)(2,1)S(1)}, u32[]{:S(2)}, u32[]{:S(2)}) collective-permute-start(bf16[96,1024]{1,0:T(8,128)(2,1)S(1)} %slice.6), channel_id=1, source_target_pairs={{0,2},{2,4},{4,6},{6,7},{7,5},{5,3},{3,1},{1,0},{8,10},{10,12},{12... | collective-permute-start | bytes 589832 | tf_op jit(solution)/shard_map/ppermute | solution.py:436
  36.3 5.7 %collective-permute-start.15 = (bf16[96,1024]{1,0:T(8,128)(2,1)S(1)}, bf16[96,1024]{1,0:T(8,128)(2,1)S(1)}, u32[]{:S(2)}, u32[]{:S(2)}) collective-permute-start(bf16[96,1024]{1,0:T(8,128)(2,1)S(1)} %slice.7), channel_id=1, source_target_pairs={{2,0},{4,2},{6,4},{7,6},{5,7},{3,5},{1,3},{0,1},{10,8},{12,10},{14... | collective-permute-start | bytes 589832 | tf_op jit(solution)/shard_map/ppermute | solution.py:439
  36.8 7.7 %collective-permute-start.9 = (f32[232,384]{1,0:T(8,128)S(1)}, f32[232,384]{1,0:T(8,128)S(1)}, u32[]{:S(2)}, u32[]{:S(2)}) collective-permute-start(f32[232,384]{1,0:T(8,128)S(1)} %add_cores.7.rest_0_.rest_2_), channel_id=1, source_target_pairs={{0,16},{8,24},{16,0},{24,8},{1,17},{9,25},{17,1},{25,9},{2,18},{10... | collective-permute-start | bytes 1069064 | tf_op jit(solution)/shard_map/ppermute | solution.py:430
  39.6 2.4 %collective-permute-start.12 = (f32[392,384]{1,0:T(8,128)S(1)}, f32[392,384]{1,0:T(8,128)S(1)}, u32[]{:S(2)}, u32[]{:S(2)}) collective-permute-start(f32[392,384]{1,0:T(8,128)S(1)} %get-tuple-element.50), channel_id=1, source_target_pairs={{0,8},{8,0},{16,24},{24,16},{1,9},{9,1},{17,25},{25,17},{2,10},{10... | collective-permute-start | bytes 1806344 | tf_op jit(solution)/shard_map/ppermute | solution.py:430
  42.8 7.1 %copy-start.3 = (s32[24,160]{1,0:T(8,128)S(1)}, s32[24,160]{1,0:T(8,128)}, u32[]{:S(2)}) copy-start(s32[24,160]{1,0:T(8,128)} %bins_ref.1) | copy-start | bytes 46084
  42.8 7.1 %copy-start.4 = (f32[5,16]{1,0:T(8,128)S(1)}, f32[5,16]{1,0:T(8,128)}, u32[]{:S(2)}) copy-start(f32[5,16]{1,0:T(8,128)} %weight_ref.1) | copy-start | bytes 964
  42.8 7.1 %copy-start.5 = (s32[160]{0:T(256)S(1)}, s32[160]{0:T(256)}, u32[]{:S(2)}) copy-start(s32[160]{0:T(256)} %param.10) | copy-start | bytes 1924
  42.8 1.8 %collective-permute-start.16 = (f32[392,192]{1,0:T(8,128)S(1)}, f32[392,192]{1,0:T(8,128)S(1)}, u32[]{:S(2)}, u32[]{:S(2)}) collective-permute-start(f32[392,192]{1,0:T(8,128)S(1)} %get-tuple-element.55), channel_id=1, source_target_pairs={{0,8},{8,0},{16,24},{24,16},{1,9},{9,1},{17,25},{25,17},{2,10},{10... | collective-permute-start | bytes 903176 | tf_op jit(solution)/shard_map/ppermute | solution.py:430
  42.9 11.2 %collective-permute-start.13 = (f32[232,384]{1,0:T(8,128)S(1)}, f32[232,384]{1,0:T(8,128)S(1)}, u32[]{:S(2)}, u32[]{:S(2)}) collective-permute-start(f32[232,384]{1,0:T(8,128)S(1)} %add_cores.8.rest_0_.rest_2_), channel_id=1, source_target_pairs={{0,16},{8,24},{16,0},{24,8},{1,17},{9,25},{17,1},{25,9},{2,18},{10... | collective-permute-start | bytes 1069064 | tf_op jit(solution)/shard_map/ppermute | solution.py:430
  44.7 12.8 %collective-permute-start.17 = (f32[352,128]{1,0:T(8,128)S(1)}, f32[352,128]{1,0:T(8,128)S(1)}, u32[]{:S(2)}, u32[]{:S(2)}) collective-permute-start(f32[352,128]{1,0:T(8,128)S(1)} %add_cores.9.rest_0_), channel_id=1, source_target_pairs={{0,16},{8,24},{16,0},{24,8},{1,17},{9,25},{17,1},{25,9},{2,18},{10... | collective-permute-start | bytes 540680 | tf_op jit(solution)/shard_map/ppermute | solution.py:430

commit v5 on v4

--- a/solution.py
+++ b/solution.py
@@ -388,30 +388,43 @@
 
 
 def finish_kernel(covs, ring, order, ids_ref, solved_ref, scale_ref, placed_ref, mine_ref, came_ref, *rest):
-    out_ref = rest[-1]
+    out_ref, last, sems = rest[-3:]
     variants = mine_ref.shape[1]
     group = LANES // math.gcd(variants, LANES)
     width = group * variants
-    stat = fitted_stat(covs, 0, solved_ref, mine_ref, came_ref, rest[:-1])
-    out_ref[...] = placed_ref[...]
     across = [order[(order.index(block) + ring // 2) % ring] for block in range(ring)]
     start = lookup(ids_ref[1], [block // group * width for block in across])
     first = lookup(ids_ref[1], [block % group * variants for block in across])
     span = pl.ds(pl.multiple_of(start, LANES), width)
+    there = pltpu.make_async_copy(placed_ref.at[:, span], last, sems.at[0])
+    there.start()
+    stat = fitted_stat(covs, 0, solved_ref, mine_ref, came_ref, rest[:-3])
     stat = jnp.concatenate([stat] * group, axis=1)
     lane = lax.broadcasted_iota(jnp.int32, stat.shape, 1)
     inside = jnp.logical_and(lane >= first, lane < first + variants)
-    out_ref[:, span] = jnp.where(inside, stat * scale_ref[:, span], placed_ref[:, span])
+    there.wait()
+    last[...] = jnp.where(inside, stat * scale_ref[:, span], last[...])
+    back = pltpu.make_async_copy(last, out_ref.at[:, span], sems.at[1])
+    back.start()
+    back.wait()
 
 
 def finish(ids, solved, scale, placed, last, covs, ring, order):
-    return call(
+    genes, total = scale.shape
+    variants = total // ring
+    width = LANES // math.gcd(variants, LANES) * variants
+    vmem, anywhere = pl.BlockSpec(memory_space=pltpu.VMEM), pl.BlockSpec(memory_space=pl.ANY)
+    return pl.pallas_call(
         functools.partial(finish_kernel, covs, ring, order),
-        jax.ShapeDtypeStruct(scale.shape, jnp.float32),
-        "finish",
-        COST["finish"],
-        (ids, solved, scale, placed, *last),
-    )
+        out_shape=jax.ShapeDtypeStruct(scale.shape, jnp.float32),
+        in_specs=[pl.BlockSpec(memory_space=pltpu.SMEM), vmem, vmem, anywhere] + [vmem] * len(last),
+        out_specs=anywhere,
+        input_output_aliases={3: 0},
+        scratch_shapes=[pltpu.VMEM((genes, width), jnp.float32), pltpu.SemaphoreType.DMA((2,))],
+        compiler_params=pltpu.CompilerParams(vmem_limit_bytes=VMEM_LIMIT),
+        cost_estimate=pl.CostEstimate(flops=COST["finish"], bytes_accessed=0, transcendentals=0),
+        name="finish",
+    )(ids, solved, scale, placed, *last)
 
 
 def shards(order, expression, genotypes, covariates, distance_bins, gene_folds, fold_weights):

time: 59.8 us -> 60.5 us (1.012)
  Pallas kernels: 17.6 us -> 19.2 us
  waiting for transfers between devices: 21.4 us -> 20.5 us
    pallas_call x0 -> x1, Pallas kernels: none -> 2.72 us  [finish(): pl.pallas_call(functools.partial(finish_kernel, covs, ring, order), out_s...]
    pallas_call x18 -> x17, Pallas kernels: 17.6 us -> 16.5 us  [call(): pl.pallas_call(kernel, out_shape=out_shape, in_specs=[smem] * scalars + [...]
    ppermute x10, waiting for transfers between devices: 3.1 us -> 2.19 us  [exchange(): return lax.ppermute(x, 'samp', [(s, s ^ d) for s in range(parts)])]
  transfers between devices with their start and end apart: 18 -> 18, of which waited for: 11 -> 11; matrix products, arithmetic and copies ran while one was open for 0% -> 0% of each run, Pallas kernels for 26% -> 27%
where the time goes in v5:
time: 60.5 us; the launch traced here: 60.2 us
  waiting for transfers between devices  20.5 us (34%)
  Pallas kernels  19.2 us (32%)
  starting transfers between devices  17 us (28%)
  local copies, waits for them, and re-layouts  3.26 us (5%)
    pallas_call x17, Pallas kernels, call(): pl.pallas_call(kernel, out_shape=out_shape, in_specs=[smem] * scalars + [...  16.5 us
    ppermute x4, waiting for transfers between devices, right(): return lax.ppermute(x, 'var', forward)  12.5 us
    ppermute x4, starting transfers between devices, right(): return lax.ppermute(x, 'var', forward)  7.85 us
    ppermute x10, starting transfers between devices, exchange(): return lax.ppermute(x, 'samp', [(s, s ^ d) for s in range(parts)])  7.84 us
    ppermute x4, waiting for transfers between devices, left(): return lax.ppermute(x, 'var', backward)  5.81 us
    unnamed x12, local copies, waits for them, and re-layouts  3.23 us
    pallas_call x1, Pallas kernels, finish(): pl.pallas_call(functools.partial(finish_kernel, covs, ring, order), out_s...  2.72 us
    ppermute x10, waiting for transfers between devices, exchange(): return lax.ppermute(x, 'samp', [(s, s ^ d) for s in range(parts)])  2.19 us
  transfers between devices with their start and end apart: 18, of which 11 were waited for; matrix products, arithmetic and copies ran while one was open for 0% of the time, Pallas kernels for 27%

profile of v5, /device:TPU:0, one launch (start us, length us, event | category | flops | bytes accessed | tf_op | source)
XLA Modules:
  0.0 60.2 jit_solution(3673245982365491079)
XLA Ops:
  0.0 3.0 %collective-permute-start.2 = (bf16[192,1024]{1,0:T(8,128)(2,1)}, bf16[192,1024]{1,0:T(8,128)(2,1)S(1)}, u32[]{:S(2)}, u32[]{:S(2)}) collective-permute-start(bf16[192,1024]{1,0:T(8,128)(2,1)} %bitcast.5), channel_id=1, source_target_pairs={{0,2},{2,4},{4,6},{6,7},{7,5},{5,3},{3,1},{1,0},{8,10},{10,12},{12... | collective-permute-start | bytes 1179656 | tf_op jit(solution)/shard_map/ppermute | solution.py:449
  3.0 0.0 collective-permute-start.3
  3.0 0.1 pad_add_fusion.ids_ref
  3.1 0.0 copy-start
  3.1 1.3 %copy-done = bf16[1024,640]{1,0:T(8,128)(2,1)S(1)} copy-done((bf16[1024,640]{1,0:T(8,128)(2,1)S(1)}, bf16[1024,640]{1,0:T(8,128)(2,1)}, u32[]{:S(2)}) %copy-start) | copy-done | bytes 1310744
  4.4 0.0 copy-start.1
  4.4 1.0 %copy-done.1 = bf16[1024,192]{0,1:T(8,128)(2,1)S(1)} copy-done((bf16[1024,192]{0,1:T(8,128)(2,1)S(1)}, bf16[1024,192]{0,1:T(8,128)(2,1)}, u32[]{:S(2)}) %copy-start.1) | copy-done | bytes 393240
  5.4 0.9 %copy-done.2 = bf16[1024,64]{0,1:T(8,128)(2,1)S(1)} copy-done((bf16[1024,64]{0,1:T(8,128)(2,1)S(1)}, bf16[1024,64]{0,1:T(8,128)(2,1)}, u32[]{:S(2)}) %copy-start.2) | copy-done | bytes 131096
  6.3 2.4 %first_products.1 = (bf16[720,1024]{1,0:T(8,128)(2,1)S(1)}, f32[392,320]{1,0:T(8,128)S(1)}, f32[232,320]{1,0:T(8,128)S(1)}, f32[160,320]{1,0:T(8,128)S(1)}) custom-call(s32[2]{0:T(128)S(1)} %pad_add_fusion.ids_ref, bf16[1024,640]{1,0:T(8,128)(2,1)S(1)} %copy-done, bf16[192,1024]{1,0:T(8,128)(2,1)S(1)} %bitcast.7, bf16[64,1024]{1,0:T(8,128)(2,1)S(1)} %bitcast.8), custom_call_target="tpu_custom_call" | custom-call | flops 100000000 | tf_op jit(solution)/shard_map/first_products/pallas_call | solution.py:40
  8.7 0.0 collective-permute-start
  8.7 3.6 %collective-permute-done.2.refs_0_ = bf16[192,1024]{1,0:T(8,128)(2,1)S(1)} collective-permute-done((bf16[192,1024]{1,0:T(8,128)(2,1)}, bf16[192,1024]{1,0:T(8,128)(2,1)S(1)}, u32[]{:S(2)}, u32[]{:S(2)}) %collective-permute-start.2) | collective-permute-done | bytes 393248 | tf_op jit(solution)/shard_map/ppermute | solution.py:449
  12.3 1.5 %collective-permute-done.3.refs_1_ = bf16[192,1024]{1,0:T(8,128)(2,1)S(1)} collective-permute-done((bf16[192,1024]{1,0:T(8,128)(2,1)}, bf16[192,1024]{1,0:T(8,128)(2,1)S(1)}, u32[]{:S(2)}, u32[]{:S(2)}) %collective-permute-start.3) | collective-permute-done | bytes 393248 | tf_op jit(solution)/shard_map/ppermute | solution.py:452
  13.8 1.6 %collective-permute-start.6 = (bf16[192,1024]{1,0:T(8,128)(2,1)S(1)}, bf16[192,1024]{1,0:T(8,128)(2,1)S(1)}, u32[]{:S(2)}, u32[]{:S(2)}) collective-permute-start(bf16[192,1024]{1,0:T(8,128)(2,1)S(1)} %get-tuple-element.37.rest_0_), channel_id=1, source_target_pairs={{0,2},{2,4},{4,6},{6,7},{7,5},{5,3},{3,1},{1,0},{8,10},{10,12},{12... | collective-permute-start | bytes 1179656 | tf_op jit(solution)/shard_map/ppermute | solution.py:449
  15.4 0.4 collective-permute-start.7
  15.8 0.0 collective-permute-done.came_ref.rest_2_
  15.8 0.1 add_cores.5.rest_0_
  15.9 1.6 %collective-permute-start.1 = (f32[584,128]{1,0:T(8,128)S(1)}, f32[584,128]{1,0:T(8,128)S(1)}, u32[]{:S(2)}, u32[]{:S(2)}) collective-permute-start(f32[584,128]{1,0:T(8,128)S(1)} %add_cores.5.rest_0_), channel_id=1, source_target_pairs={{0,16},{8,24},{16,0},{24,8},{1,17},{9,25},{17,1},{25,9},{2,18},{10... | collective-permute-start | bytes 897032 | tf_op jit(solution)/shard_map/ppermute | solution.py:443
  17.5 1.3 %next_products.4 = (f32[392,384]{1,0:T(8,128)S(1)}, f32[232,384]{1,0:T(8,128)S(1)}, f32[160,384]{1,0:T(8,128)S(1)}) custom-call(bf16[720,1024]{1,0:T(8,128)(2,1)S(1)} %get-tuple-element.36.left_ref, bf16[192,1024]{1,0:T(8,128)(2,1)S(1)} %get-tuple-element.37.rest_0_, bf16[192,1024]{1,0:T(8,128)(2,1)S(1)} %get-tuple-element.38.rest_1_, ...), custom_call_target="tpu_custom_call" | custom-call | flops 100000000 | tf_op jit(solution)/shard_map/next_products/pallas_call | solution.py:40
  18.8 0.0 collective-permute-start.4
  18.8 4.7 %collective-permute-done.6.refs_0_ = bf16[192,1024]{1,0:T(8,128)(2,1)S(1)} collective-permute-done((bf16[192,1024]{1,0:T(8,128)(2,1)S(1)}, bf16[192,1024]{1,0:T(8,128)(2,1)S(1)}, u32[]{:S(2)}, u32[]{:S(2)}) %collective-permute-start.6) | collective-permute-done | bytes 393248 | tf_op jit(solution)/shard_map/ppermute | solution.py:449
  23.5 1.3 %collective-permute-done.7.refs_1_ = bf16[192,1024]{1,0:T(8,128)(2,1)S(1)} collective-permute-done((bf16[192,1024]{1,0:T(8,128)(2,1)S(1)}, bf16[192,1024]{1,0:T(8,128)(2,1)S(1)}, u32[]{:S(2)}, u32[]{:S(2)}) %collective-permute-start.7) | collective-permute-done | bytes 393248 | tf_op jit(solution)/shard_map/ppermute | solution.py:452
  24.8 0.0 collective-permute-done.1.rest_1_.refs_2_.rest_2_
  24.8 1.6 %collective-permute-start.10 = (bf16[192,1024]{1,0:T(8,128)(2,1)S(1)}, bf16[192,1024]{1,0:T(8,128)(2,1)S(1)}, u32[]{:S(2)}, u32[]{:S(2)}) collective-permute-start(bf16[192,1024]{1,0:T(8,128)(2,1)S(1)} %get-tuple-element.42.rest_0_), channel_id=1, source_target_pairs={{0,2},{2,4},{4,6},{6,7},{7,5},{5,3},{3,1},{1,0},{8,10},{10,12},{12... | collective-permute-start | bytes 1179656 | tf_op jit(solution)/shard_map/ppermute | solution.py:449
  26.4 0.4 collective-permute-start.11
  26.8 0.0 collective-permute-done.4.came_ref
  26.8 0.1 add_cores.6.rest_0_
  26.9 1.6 %collective-permute-start.5 = (f32[232,384]{1,0:T(8,128)S(1)}, f32[232,384]{1,0:T(8,128)S(1)}, u32[]{:S(2)}, u32[]{:S(2)}) collective-permute-start(f32[232,384]{1,0:T(8,128)S(1)} %add_cores.6.rest_0_), channel_id=1, source_target_pairs={{0,16},{8,24},{16,0},{24,8},{1,17},{9,25},{17,1},{25,9},{2,18},{10... | collective-permute-start | bytes 1069064 | tf_op jit(solution)/shard_map/ppermute | solution.py:443
  28.4 1.3 %next_products.5 = (f32[392,384]{1,0:T(8,128)S(1)}, f32[232,384]{1,0:T(8,128)S(1)}, f32[160,384]{1,0:T(8,128)S(1)}) custom-call(bf16[720,1024]{1,0:T(8,128)(2,1)S(1)} %get-tuple-element.36.left_ref, bf16[192,1024]{1,0:T(8,128)(2,1)S(1)} %get-tuple-element.42.rest_0_, bf16[192,1024]{1,0:T(8,128)(2,1)S(1)} %get-tuple-element.43.rest_1_, ...), custom_call_target="tpu_custom_call" | custom-call | flops 100000000 | tf_op jit(solution)/shard_map/next_products/pallas_call | solution.py:40
  29.7 0.0 collective-permute-start.8
  29.7 3.5 %collective-permute-done.10.refs_0_ = bf16[192,1024]{1,0:T(8,128)(2,1)S(1)} collective-permute-done((bf16[192,1024]{1,0:T(8,128)(2,1)S(1)}, bf16[192,1024]{1,0:T(8,128)(2,1)S(1)}, u32[]{:S(2)}, u32[]{:S(2)}) %collective-permute-start.10) | collective-permute-done | bytes 393248 | tf_op jit(solution)/shard_map/ppermute | solution.py:449
  33.2 1.3 %collective-permute-done.11.refs_1_ = bf16[192,1024]{1,0:T(8,128)(2,1)S(1)} collective-permute-done((bf16[192,1024]{1,0:T(8,128)(2,1)S(1)}, bf16[192,1024]{1,0:T(8,128)(2,1)S(1)}, u32[]{:S(2)}, u32[]{:S(2)}) %collective-permute-start.11) | collective-permute-done | bytes 393248 | tf_op jit(solution)/shard_map/ppermute | solution.py:452
  34.5 0.0 collective-permute-done.5.rest_1_.refs_2_
  34.6 1.7 %collective-permute-start.14 = (bf16[96,1024]{1,0:T(8,128)(2,1)S(1)}, bf16[96,1024]{1,0:T(8,128)(2,1)S(1)}, u32[]{:S(2)}, u32[]{:S(2)}) collective-permute-start(bf16[96,1024]{1,0:T(8,128)(2,1)S(1)} %slice.6), channel_id=1, source_target_pairs={{0,2},{2,4},{4,6},{6,7},{7,5},{5,3},{3,1},{1,0},{8,10},{10,12},{12... | collective-permute-start | bytes 589832 | tf_op jit(solution)/shard_map/ppermute | solution.py:449
  36.3 0.5 collective-permute-start.15
  36.7 0.0 collective-permute-done.8.came_ref
  36.8 1.6 %collective-permute-start.9 = (f32[232,384]{1,0:T(8,128)S(1)}, f32[232,384]{1,0:T(8,128)S(1)}, u32[]{:S(2)}, u32[]{:S(2)}) collective-permute-start(f32[232,384]{1,0:T(8,128)S(1)} %add_cores.7.rest_0_.rest_2_), channel_id=1, source_target_pairs={{0,16},{8,24},{16,0},{24,8},{1,17},{9,25},{17,1},{25,9},{2,18},{10... | collective-permute-start | bytes 1069064 | tf_op jit(solution)/shard_map/ppermute | solution.py:443
  38.3 1.3 %next_products.6 = (f32[392,384]{1,0:T(8,128)S(1)}, f32[232,384]{1,0:T(8,128)S(1)}, f32[160,384]{1,0:T(8,128)S(1)}) custom-call(bf16[720,1024]{1,0:T(8,128)(2,1)S(1)} %get-tuple-element.36.left_ref, bf16[192,1024]{1,0:T(8,128)(2,1)S(1)} %get-tuple-element.47.rest_0_, bf16[192,1024]{1,0:T(8,128)(2,1)S(1)} %get-tuple-element.48.rest_1_, ...), custom_call_target="tpu_custom_call" | custom-call | flops 100000000 | tf_op jit(solution)/shard_map/next_products/pallas_call | solution.py:40
  39.6 0.0 collective-permute-start.12
  39.6 0.7 %collective-permute-done.14.refs_0_ = bf16[96,1024]{1,0:T(8,128)(2,1)S(1)} collective-permute-done((bf16[96,1024]{1,0:T(8,128)(2,1)S(1)}, bf16[96,1024]{1,0:T(8,128)(2,1)S(1)}, u32[]{:S(2)}, u32[]{:S(2)}) %collective-permute-start.14) | collective-permute-done | bytes 196640 | tf_op jit(solution)/shard_map/ppermute | solution.py:449
  40.3 1.7 %collective-permute-done.15.refs_1_ = bf16[96,1024]{1,0:T(8,128)(2,1)S(1)} collective-permute-done((bf16[96,1024]{1,0:T(8,128)(2,1)S(1)}, bf16[96,1024]{1,0:T(8,128)(2,1)S(1)}, u32[]{:S(2)}, u32[]{:S(2)}) %collective-permute-start.15) | collective-permute-done | bytes 196640 | tf_op jit(solution)/shard_map/ppermute | solution.py:452
  42.0 0.0 collective-permute-done.12.came_ref
  42.0 0.8 %next_products.7 = (f32[392,192]{1,0:T(8,128)S(1)}, f32[232,192]{1,0:T(8,128)S(1)}, f32[160,192]{1,0:T(8,128)S(1)}) custom-call(bf16[720,1024]{1,0:T(8,128)(2,1)S(1)} %get-tuple-element.36.left_ref, bf16[96,1024]{1,0:T(8,128)(2,1)S(1)} %get-tuple-element.52.rest_0_, bf16[96,1024]{1,0:T(8,128)(2,1)S(1)} %get-tuple-element.53.rest_1_, ...), custom_call_target="tpu_custom_call" | custom-call | flops 100000000 | tf_op jit(solution)/shard_map/next_products/pallas_call | solution.py:40
  42.8 0.0 copy-start.3
  42.8 0.0 copy-start.4
  42.8 0.0 copy-start.5
  42.8 0.1 collective-permute-start.16
  42.9 1.5 %collective-permute-start.13 = (f32[232,384]{1,0:T(8,128)S(1)}, f32[232,384]{1,0:T(8,128)S(1)}, u32[]{:S(2)}, u32[]{:S(2)}) collective-permute-start(f32[232,384]{1,0:T(8,128)S(1)} %add_cores.8.rest_0_.rest_2_), channel_id=1, source_target_pairs={{0,16},{8,24},{16,0},{24,8},{1,17},{9,25},{17,1},{25,9},{2,18},{10... | collective-permute-start | bytes 1069064 | tf_op jit(solution)/shard_map/ppermute | solution.py:443
  44.5 0.0 collective-permute-done.9.rest_1_.rest_0_
  44.5 0.2 collective-permute-done.16.came_ref
  44.6 0.1 add_cores.9.rest_0_
  44.7 1.5 %collective-permute-start.17 = (f32[352,128]{1,0:T(8,128)S(1)}, f32[352,128]{1,0:T(8,128)S(1)}, u32[]{:S(2)}, u32[]{:S(2)}) collective-permute-start(f32[352,128]{1,0:T(8,128)S(1)} %add_cores.9.rest_0_), channel_id=1, source_target_pairs={{0,16},{8,24},{16,0},{24,8},{1,17},{9,25},{17,1},{25,9},{2,18},{10... | collective-permute-start | bytes 540680 | tf_op jit(solution)/shard_map/ppermute | solution.py:443
  46.3 3.6 %solve.1 = (f32[232,72]{1,0:T(8,128)S(1)}, f32[160,128]{1,0:T(8,128)S(1)}) custom-call(f32[160,320]{1,0:T(8,128)S(1)} %get-tuple-element.31.mine_ref, f32[392,320]{1,0:T(8,128)S(1)} %collective-permute-done.came_ref.rest_2_, f32[584,128]{1,0:T(8,128)S(1)} %add_cores.5.rest_0_, f32[584,128]{1,0:T(8,128)S(1)} %collective-permute-done.1.rest_1_.refs_2_.rest_2_), custom_call_target="tpu_custom_call" | custom-call | flops 100000000 | tf_op jit(solution)/shard_map/solve/pallas_call | solution.py:40
  49.9 0.0 copy-done.3
  49.9 0.0 copy-done.4
  50.0 0.0 copy-done.5
  50.0 1.4 %widen.1.scale_ref = f32[160,1536]{1,0:T(8,128)S(1)} custom-call(f32[5,16]{1,0:T(8,128)S(1)} %copy-done.4, f32[160,128]{1,0:T(8,128)S(1)} %get-tuple-element.35.norm_ref, s32[24,160]{1,0:T(8,128)S(1)} %copy-done.3, s32[1,160]{1,0:T(1,128)S(1)} %bitcast.9), custom_call_target="tpu_custom_call" | custom-call | flops 1 | tf_op jit(solution)/shard_map/widen/pallas_call | solution.py:40
  51.4 0.5 chunk_stat.4.rest_0_
  51.8 0.6 chunk_stat.5.rest_1_
  52.4 0.6 chunk_stat.6.rest_2_
  53.0 1.1 %collective-permute-done.13.rest_1_ = f32[232,384]{1,0:T(8,128)S(1)} collective-permute-done((f32[232,384]{1,0:T(8,128)S(1)}, f32[232,384]{1,0:T(8,128)S(1)}, u32[]{:S(2)}, u32[]{:S(2)}) %collective-permute-start.13) | collective-permute-done | bytes 356384 | tf_op jit(solution)/shard_map/ppermute | solution.py:443
  54.1 0.6 chunk_stat.7.rest_3_
  54.7 1.9 %place.1.placed_ref = f32[160,1536]{1,0:T(8,128)} custom-call(s32[2]{0:T(128)S(1)} %pad_add_fusion.ids_ref, f32[160,1536]{1,0:T(8,128)S(1)} %widen.1.scale_ref, f32[160,192]{1,0:T(8,128)S(1)} %chunk_stat.4.rest_0_, f32[160,384]{1,0:T(8,128)S(1)} %chunk_stat.5.rest_1_, f32[160,384]{1,0:T(8,128)S(1)} %chunk_stat.6.rest_2_, f32[160,384]{1,0:T(8,128)S(1)} %chunk_stat.7.rest_3_), custom_call_target="tpu_custom_call" | custom-call | flops 1 | tf_op jit(solution)/shard_map/place/pallas_call | solution.py:40
  56.6 0.9 %collective-permute-done.17.rest_1_ = f32[352,128]{1,0:T(8,128)S(1)} collective-permute-done((f32[352,128]{1,0:T(8,128)S(1)}, f32[352,128]{1,0:T(8,128)S(1)}, u32[]{:S(2)}, u32[]{:S(2)}) %collective-permute-start.17) | collective-permute-done | bytes 180256 | tf_op jit(solution)/shard_map/ppermute | solution.py:443
  57.5 2.7 %finish.1 = f32[160,1536]{1,0:T(8,128)} custom-call(s32[2]{0:T(128)S(1)} %pad_add_fusion.ids_ref, f32[232,72]{1,0:T(8,128)S(1)} %get-tuple-element.34.solved_ref, f32[160,1536]{1,0:T(8,128)S(1)} %widen.1.scale_ref, f32[160,1536]{1,0:T(8,128)} %place.1.placed_ref, f32[160,192]{1,0:T(8,128)S(1)} %get-tuple-element.54.mine_ref, ...), custom_call_target="tpu_custom_call", output_to_operand_aliasing={{}: (3, {})} | custom-call | flops 1 | tf_op jit(solution)/shard_map/finish/pallas_call | solution.py:417
  (9 shorter events, 0.1 us)
Async XLA Ops:
  0.0 12.3 %collective-permute-start.2 = (bf16[192,1024]{1,0:T(8,128)(2,1)}, bf16[192,1024]{1,0:T(8,128)(2,1)S(1)}, u32[]{:S(2)}, u32[]{:S(2)}) collective-permute-start(bf16[192,1024]{1,0:T(8,128)(2,1)} %bitcast.5), channel_id=1, source_target_pairs={{0,2},{2,4},{4,6},{6,7},{7,5},{5,3},{3,1},{1,0},{8,10},{10,12},{12... | collective-permute-start | bytes 1179656 | tf_op jit(solution)/shard_map/ppermute | solution.py:449
  3.0 10.8 %collective-permute-start.3 = (bf16[192,1024]{1,0:T(8,128)(2,1)}, bf16[192,1024]{1,0:T(8,128)(2,1)S(1)}, u32[]{:S(2)}, u32[]{:S(2)}) collective-permute-start(bf16[192,1024]{1,0:T(8,128)(2,1)} %bitcast.6), channel_id=1, source_target_pairs={{2,0},{4,2},{6,4},{7,6},{5,7},{3,5},{1,3},{0,1},{10,8},{12,10},{14... | collective-permute-start | bytes 1179656 | tf_op jit(solution)/shard_map/ppermute | solution.py:452
  3.1 1.3 %copy-start = (bf16[1024,640]{1,0:T(8,128)(2,1)S(1)}, bf16[1024,640]{1,0:T(8,128)(2,1)}, u32[]{:S(2)}) copy-start(bf16[1024,640]{1,0:T(8,128)(2,1)} %e_ref.1) | copy-start | bytes 3932164
  4.4 1.0 %copy-start.1 = (bf16[1024,192]{0,1:T(8,128)(2,1)S(1)}, bf16[1024,192]{0,1:T(8,128)(2,1)}, u32[]{:S(2)}) copy-start(bf16[1024,192]{0,1:T(8,128)(2,1)} %param.7) | copy-start | bytes 1179652
  5.4 0.9 %copy-start.2 = (bf16[1024,64]{0,1:T(8,128)(2,1)S(1)}, bf16[1024,64]{0,1:T(8,128)(2,1)}, u32[]{:S(2)}) copy-start(bf16[1024,64]{0,1:T(8,128)(2,1)} %param.8) | copy-start | bytes 393220
  8.7 7.2 %collective-permute-start = (f32[392,320]{1,0:T(8,128)S(1)}, f32[392,320]{1,0:T(8,128)S(1)}, u32[]{:S(2)}, u32[]{:S(2)}) collective-permute-start(f32[392,320]{1,0:T(8,128)S(1)} %get-tuple-element.32), channel_id=1, source_target_pairs={{0,8},{8,0},{16,24},{24,16},{1,9},{9,1},{17,25},{25,17},{2,10},{10... | collective-permute-start | bytes 1505288 | tf_op jit(solution)/shard_map/ppermute | solution.py:443
  13.8 9.7 %collective-permute-start.6 = (bf16[192,1024]{1,0:T(8,128)(2,1)S(1)}, bf16[192,1024]{1,0:T(8,128)(2,1)S(1)}, u32[]{:S(2)}, u32[]{:S(2)}) collective-permute-start(bf16[192,1024]{1,0:T(8,128)(2,1)S(1)} %get-tuple-element.37.rest_0_), channel_id=1, source_target_pairs={{0,2},{2,4},{4,6},{6,7},{7,5},{5,3},{3,1},{1,0},{8,10},{10,12},{12... | collective-permute-start | bytes 1179656 | tf_op jit(solution)/shard_map/ppermute | solution.py:449
  15.4 9.4 %collective-permute-start.7 = (bf16[192,1024]{1,0:T(8,128)(2,1)S(1)}, bf16[192,1024]{1,0:T(8,128)(2,1)S(1)}, u32[]{:S(2)}, u32[]{:S(2)}) collective-permute-start(bf16[192,1024]{1,0:T(8,128)(2,1)S(1)} %get-tuple-element.38.rest_1_), channel_id=1, source_target_pairs={{2,0},{4,2},{6,4},{7,6},{5,7},{3,5},{1,3},{0,1},{10,8},{12,10},{14... | collective-permute-start | bytes 1179656 | tf_op jit(solution)/shard_map/ppermute | solution.py:452
  15.9 8.8 %collective-permute-start.1 = (f32[584,128]{1,0:T(8,128)S(1)}, f32[584,128]{1,0:T(8,128)S(1)}, u32[]{:S(2)}, u32[]{:S(2)}) collective-permute-start(f32[584,128]{1,0:T(8,128)S(1)} %add_cores.5.rest_0_), channel_id=1, source_target_pairs={{0,16},{8,24},{16,0},{24,8},{1,17},{9,25},{17,1},{25,9},{2,18},{10... | collective-permute-start | bytes 897032 | tf_op jit(solution)/shard_map/ppermute | solution.py:443
  18.8 8.0 %collective-permute-start.4 = (f32[392,384]{1,0:T(8,128)S(1)}, f32[392,384]{1,0:T(8,128)S(1)}, u32[]{:S(2)}, u32[]{:S(2)}) collective-permute-start(f32[392,384]{1,0:T(8,128)S(1)} %get-tuple-element.40), channel_id=1, source_target_pairs={{0,8},{8,0},{16,24},{24,16},{1,9},{9,1},{17,25},{25,17},{2,10},{10... | collective-permute-start | bytes 1806344 | tf_op jit(solution)/shard_map/ppermute | solution.py:443
  24.8 8.5 %collective-permute-start.10 = (bf16[192,1024]{1,0:T(8,128)(2,1)S(1)}, bf16[192,1024]{1,0:T(8,128)(2,1)S(1)}, u32[]{:S(2)}, u32[]{:S(2)}) collective-permute-start(bf16[192,1024]{1,0:T(8,128)(2,1)S(1)} %get-tuple-element.42.rest_0_), channel_id=1, source_target_pairs={{0,2},{2,4},{4,6},{6,7},{7,5},{5,3},{3,1},{1,0},{8,10},{10,12},{12... | collective-permute-start | bytes 1179656 | tf_op jit(solution)/shard_map/ppermute | solution.py:449
  26.4 8.2 %collective-permute-start.11 = (bf16[192,1024]{1,0:T(8,128)(2,1)S(1)}, bf16[192,1024]{1,0:T(8,128)(2,1)S(1)}, u32[]{:S(2)}, u32[]{:S(2)}) collective-permute-start(bf16[192,1024]{1,0:T(8,128)(2,1)S(1)} %get-tuple-element.43.rest_1_), channel_id=1, source_target_pairs={{2,0},{4,2},{6,4},{7,6},{5,7},{3,5},{1,3},{0,1},{10,8},{12,10},{14... | collective-permute-start | bytes 1179656 | tf_op jit(solution)/shard_map/ppermute | solution.py:452
  26.9 7.7 %collective-permute-start.5 = (f32[232,384]{1,0:T(8,128)S(1)}, f32[232,384]{1,0:T(8,128)S(1)}, u32[]{:S(2)}, u32[]{:S(2)}) collective-permute-start(f32[232,384]{1,0:T(8,128)S(1)} %add_cores.6.rest_0_), channel_id=1, source_target_pairs={{0,16},{8,24},{16,0},{24,8},{1,17},{9,25},{17,1},{25,9},{2,18},{10... | collective-permute-start | bytes 1069064 | tf_op jit(solution)/shard_map/ppermute | solution.py:443
  29.7 7.0 %collective-permute-start.8 = (f32[392,384]{1,0:T(8,128)S(1)}, f32[392,384]{1,0:T(8,128)S(1)}, u32[]{:S(2)}, u32[]{:S(2)}) collective-permute-start(f32[392,384]{1,0:T(8,128)S(1)} %get-tuple-element.45), channel_id=1, source_target_pairs={{0,8},{8,0},{16,24},{24,16},{1,9},{9,1},{17,25},{25,17},{2,10},{10... | collective-permute-start | bytes 1806344 | tf_op jit(solution)/shard_map/ppermute | solution.py:443
  34.6 5.7 %collective-permute-start.14 = (bf16[96,1024]{1,0:T(8,128)(2,1)S(1)}, bf16[96,1024]{1,0:T(8,128)(2,1)S(1)}, u32[]{:S(2)}, u32[]{:S(2)}) collective-permute-start(bf16[96,1024]{1,0:T(8,128)(2,1)S(1)} %slice.6), channel_id=1, source_target_pairs={{0,2},{2,4},{4,6},{6,7},{7,5},{5,3},{3,1},{1,0},{8,10},{10,12},{12... | collective-permute-start | bytes 589832 | tf_op jit(solution)/shard_map/ppermute | solution.py:449
  36.3 5.7 %collective-permute-start.15 = (bf16[96,1024]{1,0:T(8,128)(2,1)S(1)}, bf16[96,1024]{1,0:T(8,128)(2,1)S(1)}, u32[]{:S(2)}, u32[]{:S(2)}) collective-permute-start(bf16[96,1024]{1,0:T(8,128)(2,1)S(1)} %slice.7), channel_id=1, source_target_pairs={{2,0},{4,2},{6,4},{7,6},{5,7},{3,5},{1,3},{0,1},{10,8},{12,10},{14... | collective-permute-start | bytes 589832 | tf_op jit(solution)/shard_map/ppermute | solution.py:452
  36.8 7.7 %collective-permute-start.9 = (f32[232,384]{1,0:T(8,128)S(1)}, f32[232,384]{1,0:T(8,128)S(1)}, u32[]{:S(2)}, u32[]{:S(2)}) collective-permute-start(f32[232,384]{1,0:T(8,128)S(1)} %add_cores.7.rest_0_.rest_2_), channel_id=1, source_target_pairs={{0,16},{8,24},{16,0},{24,8},{1,17},{9,25},{17,1},{25,9},{2,18},{10... | collective-permute-start | bytes 1069064 | tf_op jit(solution)/shard_map/ppermute | solution.py:443
  39.6 2.4 %collective-permute-start.12 = (f32[392,384]{1,0:T(8,128)S(1)}, f32[392,384]{1,0:T(8,128)S(1)}, u32[]{:S(2)}, u32[]{:S(2)}) collective-permute-start(f32[392,384]{1,0:T(8,128)S(1)} %get-tuple-element.50), channel_id=1, source_target_pairs={{0,8},{8,0},{16,24},{24,16},{1,9},{9,1},{17,25},{25,17},{2,10},{10... | collective-permute-start | bytes 1806344 | tf_op jit(solution)/shard_map/ppermute | solution.py:443
  42.8 7.1 %copy-start.3 = (s32[24,160]{1,0:T(8,128)S(1)}, s32[24,160]{1,0:T(8,128)}, u32[]{:S(2)}) copy-start(s32[24,160]{1,0:T(8,128)} %bins_ref.1) | copy-start | bytes 46084
  42.8 7.1 %copy-start.4 = (f32[5,16]{1,0:T(8,128)S(1)}, f32[5,16]{1,0:T(8,128)}, u32[]{:S(2)}) copy-start(f32[5,16]{1,0:T(8,128)} %weight_ref.1) | copy-start | bytes 964
  42.8 7.1 %copy-start.5 = (s32[160]{0:T(256)S(1)}, s32[160]{0:T(256)}, u32[]{:S(2)}) copy-start(s32[160]{0:T(256)} %param.10) | copy-start | bytes 1924
  42.8 1.8 %collective-permute-start.16 = (f32[392,192]{1,0:T(8,128)S(1)}, f32[392,192]{1,0:T(8,128)S(1)}, u32[]{:S(2)}, u32[]{:S(2)}) collective-permute-start(f32[392,192]{1,0:T(8,128)S(1)} %get-tuple-element.55), channel_id=1, source_target_pairs={{0,8},{8,0},{16,24},{24,16},{1,9},{9,1},{17,25},{25,17},{2,10},{10... | collective-permute-start | bytes 903176 | tf_op jit(solution)/shard_map/ppermute | solution.py:443
  42.9 11.2 %collective-permute-start.13 = (f32[232,384]{1,0:T(8,128)S(1)}, f32[232,384]{1,0:T(8,128)S(1)}, u32[]{:S(2)}, u32[]{:S(2)}) collective-permute-start(f32[232,384]{1,0:T(8,128)S(1)} %add_cores.8.rest_0_.rest_2_), channel_id=1, source_target_pairs={{0,16},{8,24},{16,0},{24,8},{1,17},{9,25},{17,1},{25,9},{2,18},{10... | collective-permute-start | bytes 1069064 | tf_op jit(solution)/shard_map/ppermute | solution.py:443
  44.7 12.8 %collective-permute-start.17 = (f32[352,128]{1,0:T(8,128)S(1)}, f32[352,128]{1,0:T(8,128)S(1)}, u32[]{:S(2)}, u32[]{:S(2)}) collective-permute-start(f32[352,128]{1,0:T(8,128)S(1)} %add_cores.9.rest_0_), channel_id=1, source_target_pairs={{0,16},{8,24},{16,0},{24,8},{1,17},{9,25},{17,1},{25,9},{2,18},{10... | collective-permute-start | bytes 540680 | tf_op jit(solution)/shard_map/ppermute | solution.py:443
